TPU v7x, 256 devices: a whole 4x4x8 slice. The times are simulated.
256 devices in a mesh: acq: 4 (over x), tile: 64 (over z, y, core).
Axes of the slice: x: 4, y: 4, z: 8, core: 2. Of those that a mesh axis runs over, the one named last changes fastest.
Arguments:
- slc: bfloat16 [16, 2, 8192, 1280], P('acq', None, 'tile')
- match: int32 [2, 16], replicated, may hold values from 0 to 3, as said below
- dest: int32 [64, 16, 32, 1], P('tile', 'acq'), may hold values from 0 to 3; in each aligned block of 128 rows (0 to 127, 128 to 255, ..., all dimensions but the last counted through in order) at most 64 rows name the same one
- coherent: int32 [64, 16, 32], P('tile', 'acq'), may hold values 0 or 1
Outputs:
- received: bfloat16 [64, 1024, 2, 128], P('tile', 'acq')
Inputs may be any that keep to these rules, and one draw needn't show every extreme that they name: `match`: within each round, the entries of each aligned run of 4 acquisitions are a permutation of 0 to 3. `dest`: among the 128 rows of one device, at most 64 name the same owner.
All inputs are finite; a program needn't handle non-finite values. No bound on the sum of `coherent` on one device may be relied on, other than what follows from the above.
Results may differ from a plain program's by a relative error of at most 0.001.
Values may be sent and summed in bfloat16 or wider, within the bound.
No kernel may reach another device: no remote copies, remote signals or barrier semaphores. Data moves between devices by JAX's collectives and lax.ppermute only.
A program may use at most 128 MiB of HBM per device.

v0:
```python
import jax
import jax.numpy as jnp
from jax import lax
from jax.sharding import PartitionSpec as P

PATCH = 32
LOOK_L = 4
LOOK_S = 20
BLOCK_ROWS = 4
ROUNDS = 2


power_floor = 0.25
energy_eps = 1e-06


def swapped(x, axis, stride):
    return lax.ppermute(x, axis, [(i, i ^ 1 << stride) for i in range(lax.axis_size(axis))])


def dft_tables():
    counter = jnp.arange(PATCH)
    phase = counter[:, None] * counter[None, :] % PATCH
    angle = phase.astype(jnp.float32) * (2.0 * 3.141592653589793 / PATCH)
    return (jnp.cos(angle), jnp.sin(angle))


def along_axes(real_part, imag_part, cosine, sine_tab, sign, form):
    hold = lax.Precision.HIGHEST
    c_real = jnp.einsum(form, cosine, real_part, precision=hold)
    c_imag = jnp.einsum(form, cosine, imag_part, precision=hold)
    s_real = jnp.einsum(form, sine_tab, real_part, precision=hold)
    s_imag = jnp.einsum(form, sine_tab, imag_part, precision=hold)
    return (c_real - sign * s_imag, c_imag + sign * s_real)


def transform(real_part, imag_part, cosine, sine_tab, sign):
    real_part, imag_part = along_axes(
        real_part, imag_part, cosine, sine_tab, sign, "jk,aPkQl->aPjQl"
    )
    return along_axes(real_part, imag_part, cosine, sine_tab, sign, "lm,aPkQm->aPkQl")


def cross_looks(left, right, picks):
    acq_dev, _, line_count, sample_count = left.shape
    other = jnp.take(right, picks, axis=0)
    own_real = left[:, 0].astype(jnp.float32)
    own_imag = left[:, 1].astype(jnp.float32)
    other_real = other[:, 0].astype(jnp.float32)
    other_imag = other[:, 1].astype(jnp.float32)
    real_part = own_real * other_real + own_imag * other_imag
    imag_part = own_imag * other_real - own_real * other_imag
    stacked = jnp.stack([real_part, imag_part], axis=1)
    stacked = stacked.reshape(
        acq_dev, 2, line_count // LOOK_L, LOOK_L, sample_count // LOOK_S, LOOK_S
    )
    return jnp.sum(stacked, axis=(3, 5)) / (LOOK_L * LOOK_S)


def shards(slc, match, dest, coherent):
    acq_dev, _, lines_dev, samples_dev = slc.shape
    n_acq = lax.axis_size("acq")
    n_tile = lax.axis_size("tile")
    far_bit = n_acq.bit_length() - 2
    grid_count = lines_dev * n_tile // LOOK_L * (samples_dev // LOOK_S)
    patch_rows = lines_dev // LOOK_L // PATCH
    patch_cols = samples_dev // LOOK_S // PATCH
    cosine, sine_tab = dft_tables()
    my_group = lax.axis_index("acq")

    def swap_tiles(tiles, round_number):
        if round_number == 0:
            return swapped(tiles, "acq", 0)
        return swapped(tiles, "acq", far_bit)

    order_list = [0, 1]
    looked_all = {}
    filtered_all = {}
    for round_number in order_list:
        own_match = lax.dynamic_slice_in_dim(match[round_number], my_group * acq_dev, acq_dev)
        group_tiles = swap_tiles(slc, round_number)
        looked_all[round_number] = cross_looks(slc, group_tiles, own_match)
        local_looked = looked_all[round_number]
        total = lax.psum(
            jnp.sum(local_looked[:, 0] ** 2 + local_looked[:, 1] ** 2, axis=(1, 2)), "tile"
        )
        energy = total / grid_count + energy_eps
        looked = looked_all[round_number]
        shape_six = (acq_dev, patch_rows, PATCH, patch_cols, PATCH)
        real_part = looked[:, 0].reshape(shape_six)
        imag_part = looked[:, 1].reshape(shape_six)
        spec_real, spec_imag = transform(real_part, imag_part, cosine, sine_tab, -1.0)
        scale = energy[:, None, None, None, None]
        power = (spec_real**2 + spec_imag**2) / (PATCH * PATCH * scale)
        weight = (power + power_floor) ** 0.25
        back_real, back_imag = transform(
            weight * spec_real, weight * spec_imag, cosine, sine_tab, 1.0
        )
        norm_factor = 1.0 / (PATCH * PATCH * jnp.sqrt(scale))
        parts = jnp.stack([back_real * norm_factor, back_imag * norm_factor], axis=-1)
        parts = parts.reshape(
            acq_dev, patch_rows, PATCH // BLOCK_ROWS, BLOCK_ROWS, patch_cols, PATCH, 2
        )
        parts = jnp.transpose(parts, (0, 1, 2, 4, 6, 3, 5))
        filtered_all[round_number] = parts.reshape(
            acq_dev, patch_rows * (PATCH // BLOCK_ROWS) * patch_cols, 2, BLOCK_ROWS * PATCH
        )
    stacked = jnp.stack([filtered_all[round_number] for round_number in range(ROUNDS)], axis=1)
    block_len = BLOCK_ROWS * PATCH
    rows_dev = stacked.shape[0] * stacked.shape[1] * stacked.shape[2]
    cap_rows = max(3, 2 * ((rows_dev + n_acq - 1) // n_acq))
    stacked = stacked.reshape(rows_dev, 2, block_len)
    mask_rows = coherent.reshape(rows_dev).astype(jnp.float32)
    value = (stacked * mask_rows[:, None, None]).astype(jnp.bfloat16)
    owner = dest.reshape(rows_dev)
    onehot = (owner[:, None] == jnp.arange(n_acq)).astype(jnp.int32)
    rank = jnp.sum((jnp.cumsum(onehot, axis=0) - onehot) * onehot, axis=1)
    hits = (onehot[:, :, None] == 1) & (rank[:, None, None] == jnp.arange(cap_rows)[None, None, :])
    select = hits.astype(jnp.bfloat16).reshape(rows_dev, n_acq * cap_rows)
    outgoing = jnp.einsum("ks,kcp->scp", select, value, preferred_element_type=jnp.float32).astype(
        jnp.bfloat16
    )
    incoming = lax.all_to_all(outgoing, "acq", split_axis=0, concat_axis=0, tiled=True)
    return incoming[None]


def solution(mesh):
    return jax.shard_map(
        shards,
        mesh=mesh,
        in_specs=(
            P("acq", None, "tile", None),
            P(),
            P("tile", "acq", None, None),
            P("tile", "acq", None),
        ),
        out_specs=P("tile", "acq", None, None),
        check_vma=False,
    )
```

profile of v0, /device:TPU:1, one launch (start us, length us, event | category | flops | bytes accessed | tf_op | source)
XLA Modules:
  0.0 388.8 jit_solution(11845834372850043596)
XLA Ops:
  0.0 3.6 collective-permute-start.1
  3.6 0.3 collective-permute-start
  3.9 0.7 convert_element_type.142
  4.7 0.5 broadcast.327
  5.2 1.3 reduce.5
  6.7 0.2 reduce_window_sum.11
  6.9 0.8 fusion.240
  7.9 0.2 select_reduce_fusion
  8.1 51.3 %collective-permute-done.1 = bf16[4,2,128,1280]{3,2,1,0:T(8,128)(2,1)} collective-permute-done((bf16[4,2,128,1280]{3,2,1,0:T(8,128)(2,1)}, bf16[4,2,128,1280]{3,2,1,0:T(8,128)(2,1)}, u32[]{:S(2)}, u32[]{:S(2)}) %collective-permute-start.1) | collective-permute-done | bytes 2621472 | tf_op jit(solution)/shard_map/ppermute | solution.py:18
  59.4 2.5 gather_fusion.1
  61.9 1.8 broadcast_select_fusion
  63.7 52.9 %collective-permute-done = bf16[4,2,128,1280]{3,2,1,0:T(8,128)(2,1)} collective-permute-done((bf16[4,2,128,1280]{3,2,1,0:T(8,128)(2,1)}, bf16[4,2,128,1280]{3,2,1,0:T(8,128)(2,1)}, u32[]{:S(2)}, u32[]{:S(2)}) %collective-permute-start) | collective-permute-done | bytes 2621472 | tf_op jit(solution)/shard_map/ppermute | solution.py:18
  116.6 2.5 gather_fusion
  119.1 0.3 broadcast_select_fusion.1
  119.5 1.4 copy-done
  120.8 0.8 copy-done.1
  121.6 4.0 %fusion = (f32[4,1,128,1280]{3,2,1,0:T(8,128)}, f32[4,1,128,1280]{3,2,1,0:T(8,128)}, f32[4,1,128,1280]{3,2,1,0:T(8,128)S(1)}, f32[4,1,128,1280]{3,2,1,0:T(8,128)}) fusion(bf16[4,2,128,1280]{3,2,1,0:T(8,128)(2,1)S(1)} %broadcast_select_fusion.1, bf16[4,2,128,1280]{3,2,1,0:T(8,128)(2,1)S(1)} %copy-done.1, bf16[4,2,128,1280]{3,2,1,0:T(8,128)(2,1)S(1)} %copy-done), kind=kLoop, calls=%fused_computation.12 | loop fusion | flops 11796480 | bytes 18350080 | tf_op jit(solution)/shard_map/add | solution.py:51
  125.6 21.7 %stack.39 = f32[4,1,32,4,64,20]{5,4,3,2,0,1:T(8,128)} reshape(f32[4,1,128,1280]{3,2,1,0:T(8,128)} %get-tuple-element.12) | data formatting | bytes 5242880 | tf_op jit(solution)/shard_map/stack | solution.py:53
  147.3 21.7 %stack.40 = f32[4,1,32,4,64,20]{5,4,3,2,0,1:T(8,128)} reshape(f32[4,1,128,1280]{3,2,1,0:T(8,128)} %get-tuple-element.13) | data formatting | bytes 5242880 | tf_op jit(solution)/shard_map/stack | solution.py:53
  169.0 12.7 %maximum_reduce_fusion = f32[4,2,32,64]{3,2,0,1:T(8,128)S(1)} fusion(f32[4,1,32,4,64,20]{5,4,3,2,0,1:T(8,128)} %stack.40, f32[4,1,32,4,64,20]{5,4,3,2,0,1:T(8,128)} %stack.39), kind=kLoop, calls=%fused_computation.2 | loop fusion | flops 2605056 | bytes 5308416 | tf_op jit(solution)/shard_map/reduce_sum | solution.py:57
  181.7 0.1 fusion.239
  182.0 0.3 convolution_multiply_fusion.6
  182.4 0.3 convolution_multiply_fusion.7
  182.7 0.3 fusion.10
  183.1 0.4 convolution_multiply_fusion.5
  183.5 0.3 fusion.11
  183.8 0.4 convolution_multiply_fusion.4
  184.2 0.4 convolution_subtract_fusion.6
  184.6 0.4 convolution_add_fusion.6
  185.1 21.7 %stack.45 = f32[4,1,32,4,64,20]{5,4,3,2,0,1:T(8,128)} reshape(f32[4,1,128,1280]{3,2,1,0:T(8,128)} %get-tuple-element.17) | data formatting | bytes 5242880 | tf_op jit(solution)/shard_map/stack | solution.py:53
  206.7 20.9 %stack.46 = f32[4,1,32,4,64,20]{5,4,3,2,0,1:T(8,128)} reshape(f32[4,1,128,1280]{3,2,1,0:T(8,128)S(1)} %get-tuple-element.16) | data formatting | bytes 5242880 | tf_op jit(solution)/shard_map/stack | solution.py:53
  227.6 12.7 %maximum_reduce_fusion.1 = f32[4,2,32,64]{3,2,0,1:T(8,128)S(1)} fusion(f32[4,1,32,4,64,20]{5,4,3,2,0,1:T(8,128)} %stack.46, f32[4,1,32,4,64,20]{5,4,3,2,0,1:T(8,128)} %stack.45), kind=kLoop, calls=%fused_computation.3 | loop fusion | flops 2605056 | bytes 5308416 | tf_op jit(solution)/shard_map/reduce_sum | solution.py:57
  240.4 0.1 add_reduce_fusion
  240.5 128.5 %all-reduce = (f32[4]{0:T(128)S(1)}, f32[4]{0:T(128)S(1)}) all-reduce(f32[4]{0:T(128)S(1)} %get-tuple-element.21, f32[4]{0:T(128)S(1)} %get-tuple-element.19), channel_id=1, replica_groups=mesh['acq'=4,'tile'=64] {'tile'}, use_global_device_ids=true, to_apply=%region_7.9 | all-reduce | flops 8 | bytes 64 | tf_op jit(solution)/shard_map/psum | solution.py:84
  369.0 0.5 fusion.60
  369.5 0.5 fusion.56
  370.1 0.3 convolution_multiply_fusion.2
  370.6 0.3 convolution_multiply_fusion.3
  370.9 0.3 fusion.6
  371.3 0.4 convolution_multiply_fusion.1
  371.7 0.3 fusion.7
  372.0 0.4 convolution_multiply_fusion
  372.4 0.4 convolution_subtract_fusion.2
  372.8 0.4 convolution_add_fusion.2
  373.2 0.5 fusion.48
  373.7 0.5 fusion.44
  374.3 0.5 fusion.9
  374.8 0.4 fusion.58
  375.2 0.5 fusion.8
  375.7 0.4 fusion.54
  376.1 0.4 fusion.12
  376.5 0.4 fusion.13
  377.0 0.2 stack_reshape.6
  377.2 0.5 fusion.5
  377.7 0.4 fusion.46
  378.1 0.5 fusion.4
  378.6 0.4 fusion.42
  379.0 0.4 fusion.14
  379.4 0.4 fusion.15
  379.9 0.2 stack_reshape.7
  380.2 0.2 convolution_convert_fusion
  380.4 0.1 copy.171
  380.5 7.6 %all_to_all.5 = bf16[256,2,128]{2,1,0:T(2,128)(2,1)S(1)} all-to-all(bf16[256,2,128]{2,1,0:T(2,128)(2,1)S(1)} %copy.171), channel_id=1, replica_groups=mesh['acq'=4,'tile'=64] {'acq'}, dimensions={0} | all-to-all | bytes 262144 | tf_op jit(solution)/shard_map/all_to_all | solution.py:123
  388.2 0.7 copy.205
  (24 shorter events, 1.2 us)
Async XLA Ops:
  0.0 59.4 %collective-permute-start.1 = (bf16[4,2,128,1280]{3,2,1,0:T(8,128)(2,1)}, bf16[4,2,128,1280]{3,2,1,0:T(8,128)(2,1)}, u32[]{:S(2)}, u32[]{:S(2)}) collective-permute-start(bf16[4,2,128,1280]{3,2,1,0:T(8,128)(2,1)} %param.6), channel_id=1, source_target_pairs={{0,128},{64,192},{128,0},{192,64},{1,129},{65,193},{129,1},{193,65... | collective-permute-start | bytes 7864328 | tf_op jit(solution)/shard_map/ppermute | solution.py:18
  3.6 113.1 %collective-permute-start = (bf16[4,2,128,1280]{3,2,1,0:T(8,128)(2,1)}, bf16[4,2,128,1280]{3,2,1,0:T(8,128)(2,1)}, u32[]{:S(2)}, u32[]{:S(2)}) collective-permute-start(bf16[4,2,128,1280]{3,2,1,0:T(8,128)(2,1)} %param.6), channel_id=1, source_target_pairs={{0,64},{64,0},{128,192},{192,128},{1,65},{65,1},{129,193},{193,129... | collective-permute-start | bytes 7864328 | tf_op jit(solution)/shard_map/ppermute | solution.py:18
  119.1 1.7 copy-start
  119.1 2.5 copy-start.1
where the time goes:
time: 392 us; the launch traced here: 389 us
  blocking collectives  136 us (35%)
  waiting for transfers between devices  104 us (27%)
  local copies, waits for them, and re-layouts  96 us (24%)
  other arithmetic  34.8 us (9%)
  matrix products  13.3 us (3%)
    psum x1, blocking collectives, shards(): lax.psum(jnp.sum(local_looked[:, 0] ** 2 + local_looked[:, 1] ** 2, axis=...  128 us
    ppermute x2, waiting for transfers between devices, swapped(): lax.ppermute(x, axis, [(i, i ^ 1 << stride) for i in range(lax.axis_size(...  104 us
    another operation x4, local copies, waits for them, and re-layouts, cross_looks(): stacked = jnp.stack([real_part, imag_part], axis=1)  85.9 us
    reduce_sum x2, other arithmetic, cross_looks(): return jnp.sum(stacked, axis=(3, 5)) / (LOOK_L * LOOK_S)  25.5 us
  transfers between devices with their start and end apart: 2, of which 2 were waited for; matrix products, arithmetic and copies ran while one was open for 2% of the time, Pallas kernels for 0%

commit v1 on v0

v1 whole, which is shorter than its diff:
```python
import functools

import jax
import jax.numpy as jnp
import numpy as np
from jax import lax
from jax.experimental import pallas as pl
from jax.experimental.pallas import tpu as pltpu
from jax.sharding import PartitionSpec as P

PATCH = 32
LOOK_L = 4
LOOK_S = 20
BLOCK_ROWS = 4
ROUNDS = 2
ACQ_DEV = 4
SETS = 4
CAP = 64
CHUNKS = 2

power_floor = 0.25
energy_eps = 1e-06


def halves(x):
    head = x.astype(jnp.bfloat16)
    rest = (x - head.astype(np.float64)).astype(jnp.bfloat16)
    return head, rest


def tables(lines):
    k = np.arange(PATCH)
    angle = (k[:, None] * k[None, :] % PATCH) * (2.0 * np.pi / PATCH)
    cosine, sine = np.cos(angle), np.sin(angle)
    width = PATCH * LOOK_S
    looks = (np.arange(width)[:, None] // LOOK_S == np.arange(128)[None, :]).astype(jnp.bfloat16)
    rows = np.concatenate([cosine, sine], 0) / (LOOK_L * LOOK_S * PATCH)
    rows = np.repeat(rows, LOOK_L, axis=1)
    fwd = halves(rows)
    eye = np.eye(4)
    cols = np.concatenate([np.kron(eye, cosine), np.kron(eye, sine)], 1)
    head, rest = halves(cols)
    cols3 = np.concatenate([head, head, rest], 0)
    order = np.arange(PATCH).reshape(PATCH // BLOCK_ROWS, BLOCK_ROWS).T.reshape(-1)
    back = np.concatenate([cosine[order], sine[order]], 0) / PATCH
    head, rest = halves(back)
    back3 = np.concatenate([head, head, rest], 1)
    group = np.kron(eye, np.ones((PATCH, PATCH))).astype(np.float32)
    return looks, fwd, cols3, back3, group


def split(x):
    head = x.astype(jnp.bfloat16)
    return head, (x - head.astype(jnp.float32)).astype(jnp.bfloat16)


def dot(a, b):
    return jnp.dot(a, b, preferred_element_type=jnp.float32)


def forward_chunk(me_ref, match_ref, own, near, far, looks_ref, fwd_ref, prior, pieces):
    lines = own.shape[2]
    me = me_ref[0]
    one, three = me ^ 1, me ^ 3
    total = None
    for j in range(ACQ_DEV):
        pairs = (
            (own, j, near, match_ref[0, me * ACQ_DEV + j]),
            (near, j, own, match_ref[0, one * ACQ_DEV + j]),
            (near, j, far, match_ref[1, one * ACQ_DEV + j]),
            (far, j, near, match_ref[1, three * ACQ_DEV + j]),
        )
        for s, (left, i, right, m) in enumerate(pairs):
            a_re = left[i, 0].astype(jnp.float32)
            a_im = left[i, 1].astype(jnp.float32)
            b_re = right[m, 0].astype(jnp.float32)
            b_im = right[m, 1].astype(jnp.float32)
            re = split(a_re * b_re + a_im * b_im)
            im = split(a_im * b_re - a_re * b_im)
            for h in range(2):
                pieces[j, h, 0, s] = re[h]
                pieces[j, h, 1, s] = im[h]
        width = own.shape[3]
        summed = dot(pieces[j].reshape(2 * 2 * SETS * lines, width), looks_ref[...])
        half = 2 * SETS * lines
        summed = summed[:half] + summed[half:]
        if j:
            summed = pltpu.roll(summed, PATCH * j, 1)
        total = summed if total is None else total + summed
    wide = jnp.concatenate([total[n * lines : (n + 1) * lines] for n in range(2 * SETS)], axis=1)
    head, rest = split(wide)
    both = dot(fwd_ref[...], jnp.concatenate([head, rest, head], axis=0))
    half = SETS * 128
    re = both[:PATCH, :half] + both[PATCH:, half:]
    im = both[:PATCH, half:] - both[PATCH:, :half]
    if prior is not None:
        re, im = re + prior[0], im + prior[1]
    return re, im


def along_columns(re, im, cols_ref, sign):
    tall = jnp.concatenate(
        [x[:, s * 128 : (s + 1) * 128] for x in (re, im) for s in range(SETS)], axis=0
    )
    head, rest = split(tall)
    both = dot(jnp.concatenate([head, rest, head], axis=1), cols_ref[...])
    half = SETS * PATCH
    return (
        both[:half, :128] - sign * both[half:, 128:],
        both[half:, :128] + sign * both[:half, 128:],
    )


def looks_kernel(me_ref, match_ref, own, near, far, looks_ref, fwd_ref, out, pieces):
    re, im = forward_chunk(me_ref, match_ref, own, near, far, looks_ref, fwd_ref, None, pieces)
    out[0] = re
    out[1] = im


def spectrum_kernel(
    me_ref, match_ref, own, near, far, looks_ref, fwd_ref, prior, cols_ref, group_ref, spec, energy, pieces
):
    re, im = forward_chunk(me_ref, match_ref, own, near, far, looks_ref, fwd_ref, prior, pieces)
    re, im = along_columns(re, im, cols_ref, -1.0)
    spec[0] = re
    spec[1] = im
    power = re * re + im * im
    sums = jnp.concatenate(
        [jnp.sum(power[s * PATCH : (s + 1) * PATCH], axis=0, keepdims=True) for s in range(SETS)]
        + [jnp.zeros((8 - SETS, 128), jnp.float32)],
        axis=0,
    )
    sums = jnp.dot(sums, group_ref[...], precision=lax.Precision.HIGHEST, preferred_element_type=jnp.float32)
    lane = lax.broadcasted_iota(jnp.int32, (8, 128), 1) & (PATCH - 1)
    row = lax.broadcasted_iota(jnp.int32, (8, 128), 0)
    energy[0:1] = jnp.sum(jnp.where(lane == row, sums, 0.0), axis=0, keepdims=True)
    energy[1:2] = jnp.sum(jnp.where(lane == (row ^ 1), sums, 0.0), axis=0, keepdims=True)


def filter_kernel(grid_count, spec, parts, cols_ref, back_ref, group_ref, out):
    total = jnp.sum(parts[...], axis=0, keepdims=True)
    lane = lax.broadcasted_iota(jnp.int32, (8, 128), 1) & (PATCH - 1)
    row = lax.broadcasted_iota(jnp.int32, (8, 128), 0)
    spread = jnp.where(lane == row, jnp.broadcast_to(total, (8, 128)), 0.0)
    spread = jnp.dot(spread, group_ref[...], precision=lax.Precision.HIGHEST, preferred_element_type=jnp.float32)
    scale = spread * (1.0 / grid_count) + energy_eps
    inverse = 1.0 / scale
    root = lax.rsqrt(scale)
    re, im = spec[0], spec[1]
    power = re * re + im * im
    power = jnp.concatenate(
        [power[s * PATCH : (s + 1) * PATCH] * inverse[s : s + 1] for s in range(SETS)], axis=0
    )
    weight = jnp.sqrt(jnp.sqrt(power + power_floor))
    re, im = weight * re, weight * im
    re, im = (
        jnp.concatenate([x[s * PATCH : (s + 1) * PATCH] for s in range(SETS)], axis=1) for x in (re, im)
    )
    re, im = along_columns(re, im, cols_ref, 1.0)
    wide = jnp.concatenate([x[s * PATCH : (s + 1) * PATCH] for x in (re, im) for s in range(SETS)], axis=1)
    head, rest = split(wide)
    both = dot(back_ref[...], jnp.concatenate([head, rest, head], axis=0))
    half = SETS * 128
    blocks = PATCH // BLOCK_ROWS
    where = lax.broadcasted_iota(jnp.int32, (blocks, 128), 1) // PATCH
    final = (both[:PATCH, :half] - both[PATCH:, half:], both[:PATCH, half:] + both[PATCH:, :half])
    for part in range(2):
        for s in range(SETS):
            block = final[part][:, s * 128 : (s + 1) * 128] * root[s : s + 1]
            rows = [block[i * blocks : (i + 1) * blocks] for i in range(BLOCK_ROWS)]
            turned = []
            for j in range(ACQ_DEV):
                value = None
                for i in range(BLOCK_ROWS):
                    moved = rows[i] if i == j else pltpu.roll(rows[i], (PATCH * (i - j)) % 128, 1)
                    value = moved if value is None else jnp.where(where == i, moved, value)
                turned.append(value)
            out[s * 32 : (s + 1) * 32, part * 128 : (part + 1) * 128] = jnp.concatenate(
                turned, axis=0
            ).astype(jnp.bfloat16)


VMEM = pl.BlockSpec(memory_space=pltpu.VMEM)
SMEM = pl.BlockSpec(memory_space=pltpu.SMEM)
PARAMS = pltpu.CompilerParams(vmem_limit_bytes=48 * 2**20)


def swapped(x, bits):
    return lax.ppermute(x, "acq", [(i, i ^ bits) for i in range(lax.axis_size("acq"))])


def slot_choice(dest, coherent, me, column):
    rows = dest.size
    n_acq = lax.axis_size("acq")
    owner = dest.reshape(rows)
    onehot = (owner[None, :] == jnp.arange(n_acq)[:, None]).astype(jnp.float32)
    before = (jnp.arange(rows)[:, None] < jnp.arange(rows)[None, :]).astype(jnp.bfloat16)
    counts = jnp.dot(onehot.astype(jnp.bfloat16), before, preferred_element_type=jnp.float32)
    rank = jnp.sum(counts * onehot, axis=0).astype(jnp.int32)
    code = jnp.where(coherent.reshape(rows) > 0, owner * CAP + rank, n_acq * CAP)
    codes = [code] + [swapped(code, bits) for bits in range(1, n_acq)]
    slots = []
    for bits in range(n_acq):
        own_slot = codes[bits] - me * CAP
        own_slot = jnp.where((own_slot >= 0) & (own_slot < CAP), own_slot + (me ^ bits) * CAP, -1)
        slots.append(own_slot.reshape(ACQ_DEV, ROUNDS, PATCH // BLOCK_ROWS, 2))
    lines = []
    for holder in range(n_acq):
        side = column ^ (1 if holder in (1, 2) else 0)
        for bits, turn in ((holder, 0), (holder ^ 1, 0), (holder ^ 1, 1), (holder ^ 3, 1)):
            picked = jnp.where(side == 0, slots[bits][:, turn, :, 0], slots[bits][:, turn, :, 1])
            lines.append(picked.reshape(ACQ_DEV * PATCH // BLOCK_ROWS))
    chosen = jnp.concatenate(lines)
    return (jnp.arange(n_acq * CAP)[:, None] == chosen[None, :]).astype(jnp.bfloat16)


def shards(slc, match, dest, coherent):
    _, _, lines_dev, samples_dev = slc.shape
    n_acq = lax.axis_size("acq")
    n_tile = lax.axis_size("tile")
    grid_count = lines_dev * n_tile // LOOK_L * (samples_dev // LOOK_S)
    me = lax.axis_index("acq").astype(jnp.int32)
    me_arr = me.reshape(1)
    column = 1 - ((me ^ (me >> 1)) & 1)
    looks, (fwd_head, fwd_rest), cols3, back3, group = tables(lines_dev)
    width = samples_dev // 2
    step = lines_dev // CHUNKS

    chunks = []
    for n in range(CHUNKS):
        part = slc[:, :, n * step : (n + 1) * step]
        left, right = part[..., :width], part[..., width:]
        own = jnp.where(column == 0, left, right)
        other = jnp.where(column == 0, right, left)
        chunks.append((own, swapped(other, 1), swapped(own, 3)))

    choice = slot_choice(dest, coherent, me, column)

    prior = None
    for n in range(CHUNKS):
        own, near, far = chunks[n]
        span = slice(n * step, (n + 1) * step)
        fwd3 = np.concatenate([fwd_head[:, span], fwd_head[:, span], fwd_rest[:, span]], axis=1)
        scratch = [pltpu.VMEM((ACQ_DEV, 2, 2, SETS, step, width), jnp.bfloat16)]
        if n < CHUNKS - 1:
            body = looks_kernel if prior is None else more_looks_kernel
            args = [me_arr, match, own, near, far, looks, fwd3] + ([] if prior is None else [prior])
            prior = pl.pallas_call(
                body,
                out_shape=jax.ShapeDtypeStruct((2, PATCH, SETS * 128), jnp.float32),
                in_specs=[SMEM, SMEM] + [VMEM] * (len(args) - 2),
                out_specs=VMEM,
                scratch_shapes=scratch,
                compiler_params=PARAMS,
                name="looks",
            )(*args)
        else:
            spec, energy = pl.pallas_call(
                spectrum_kernel,
                out_shape=(
                    jax.ShapeDtypeStruct((2, SETS * PATCH, 128), jnp.float32),
                    jax.ShapeDtypeStruct((2, 128), jnp.float32),
                ),
                in_specs=[SMEM, SMEM] + [VMEM] * 8,
                out_specs=(VMEM, VMEM),
                scratch_shapes=scratch,
                compiler_params=PARAMS,
                name="spectrum",
            )(me_arr, match, own, near, far, looks, fwd3, prior, cols3, group)

    crossed = energy[1]
    near_energy, far_energy = swapped(crossed, 1), swapped(crossed, 2)
    lane = jnp.arange(128) & (PATCH - 1)
    pair_energy = energy[0] + jnp.where(lane < 2, near_energy, far_energy)
    copies = lax.optimization_barrier(jnp.broadcast_to(pair_energy[None], (n_tile, 128)))
    parts = lax.all_to_all(copies, "tile", split_axis=0, concat_axis=0, tiled=True)

    value = pl.pallas_call(
        functools.partial(filter_kernel, float(grid_count)),
        out_shape=jax.ShapeDtypeStruct((SETS * 32, 256), jnp.bfloat16),
        in_specs=[VMEM] * 5,
        out_specs=VMEM,
        compiler_params=PARAMS,
        name="goldstein",
    )(spec, parts, cols3, back3, group)

    held = [value] + [swapped(value, bits) for bits in range(1, n_acq)]
    held = jnp.concatenate(held, axis=0)
    out = jnp.dot(choice, held, preferred_element_type=jnp.float32).astype(jnp.bfloat16)
    return out.reshape(1, n_acq * CAP, 2, 128)


def more_looks_kernel(me_ref, match_ref, own, near, far, looks_ref, fwd_ref, prior, out, pieces):
    re, im = forward_chunk(me_ref, match_ref, own, near, far, looks_ref, fwd_ref, prior, pieces)
    out[0] = re
    out[1] = im


def solution(mesh):
    return jax.shard_map(
        shards,
        mesh=mesh,
        in_specs=(
            P("acq", None, "tile", None),
            P(),
            P("tile", "acq", None, None),
            P("tile", "acq", None),
        ),
        out_specs=P("tile", "acq", None, None),
        check_vma=False,
    )
```

time: 392 us -> 87.5 us (0.22)
  blocking collectives: 136 us -> 0 us
  local copies, waits for them, and re-layouts: 96 us -> 4.48 us
  waiting for transfers between devices: 104 us -> 37.4 us
  other arithmetic: 34.8 us -> 6.61 us
  starting transfers between devices: 3.89 us -> 30 us
  matrix products: 13.3 us -> 0.46 us
  Pallas kernels: 0 us -> 8.01 us
    psum x1 -> x0, blocking collectives: 128 us -> none  [shards(): lax.psum(jnp.sum(local_looked[:, 0] ** 2 + local_looked[:, 1] ** 2, axis=...]
    another operation x6 -> x0, local copies, waits for them, and re-layouts: 86.2 us -> none  [the longest x4 85.9 us: cross_looks(): stacked = jnp.stack([real_part, imag_part], axis=1)]
    ppermute x2 -> x12, waiting for transfers between devices: 104 us -> 29.7 us  [swapped(): lax.ppermute(x, 'acq', [(i, i ^ bits) for i in range(lax.axis_size('acq'))])]
    reduce_sum x4 -> x0, other arithmetic: 25.8 us -> none  [the longest x2 25.5 us: cross_looks(): return jnp.sum(stacked, axis=(3, 5)) / (LOOK_L * LOOK_S)]
    all_to_all x0 -> x1, starting transfers between devices: none -> 15.8 us  [shards(): lax.all_to_all(copies, 'tile', split_axis=0, concat_axis=0, tiled=True)]
    dot_general x33 -> x2, matrix products: 13.3 us -> 0.46 us  [the longest x1 0.31 us: shards(): jnp.dot(choice, held, preferred_element_type=jnp.float32)]
    ppermute x2 -> x12, starting transfers between devices: 3.89 us -> 14.2 us  [swapped(): lax.ppermute(x, 'acq', [(i, i ^ bits) for i in range(lax.axis_size('acq'))])]
    pallas_call x0 -> x3, Pallas kernels: none -> 8.01 us  [the longest x1 4.18 us: shards(): pl.pallas_call(spectrum_kernel, out_shape=(jax.ShapeDtypeStruct((2, SETS...]
  transfers between devices with their start and end apart: 2 -> 13, of which waited for: 2 -> 5; matrix products, arithmetic and copies ran while one was open for 2% -> 8% of each run, Pallas kernels for 0% -> 8%
where the time goes in v1:
time: 87.5 us; the launch traced here: 87.3 us
  waiting for transfers between devices  37.4 us (43%)
  starting transfers between devices  30 us (34%)
  Pallas kernels  8.01 us (9%)
  other arithmetic  6.61 us (8%)
  local copies, waits for them, and re-layouts  4.48 us (5%)
    ppermute x12, waiting for transfers between devices, swapped(): lax.ppermute(x, 'acq', [(i, i ^ bits) for i in range(lax.axis_size('acq'))])  29.7 us
    all_to_all x1, starting transfers between devices, shards(): lax.all_to_all(copies, 'tile', split_axis=0, concat_axis=0, tiled=True)  15.8 us
    ppermute x12, starting transfers between devices, swapped(): lax.ppermute(x, 'acq', [(i, i ^ bits) for i in range(lax.axis_size('acq'))])  14.2 us
    all_to_all x1, waiting for transfers between devices, shards(): lax.all_to_all(copies, 'tile', split_axis=0, concat_axis=0, tiled=True)  7.77 us
    pallas_call x1, Pallas kernels, shards(): pl.pallas_call(spectrum_kernel, out_shape=(jax.ShapeDtypeStruct((2, SETS...  4.18 us
    select_n x1, other arithmetic, shards(): other = jnp.where(column == 0, right, left)  3.12 us
    pallas_call x1, Pallas kernels, shards(): pl.pallas_call(body, out_shape=jax.ShapeDtypeStruct((2, PATCH, SETS * 128...  3.05 us
  transfers between devices with their start and end apart: 13, of which 5 were waited for; matrix products, arithmetic and copies ran while one was open for 8% of the time, Pallas kernels for 8%

profile of v1, /device:TPU:1, one launch (start us, length us, event | category | flops | bytes accessed | tf_op | source)
XLA Modules:
  0.0 87.3 jit_solution(17826862293393256690)
XLA Ops:
  0.0 0.7 broadcast_compare_fusion
  0.7 0.1 gt.12
  0.8 0.5 broadcast.104
  1.3 1.3 %reduce.35 = s32[4,32]{1,0:T(4,128)S(1)} reduce(s32[1,4,32,1]{2,3,1,0:T(1,128)} %param.12, s32[]{:T(128)} %broadcast.104), dimensions={0,3}, to_apply=%param.12.reduce_sub_computation.3 | reduce | bytes 1028 | tf_op args[2]
  2.6 0.1 eq.20
  2.7 0.1 fusion
  2.9 3.7 %collective-permute-start.2 = (s32[128]{0:T(128)S(1)}, s32[128]{0:T(128)S(1)}, u32[]{:S(2)}, u32[]{:S(2)}) collective-permute-start(s32[128]{0:T(128)S(1)} %add_select_fusion.1), channel_id=1, source_target_pairs={{0,128},{64,192},{128,0},{192,64},{1,129},{65,193},{129,1},{193,65... | collective-permute-start | bytes 1544 | tf_op jit(solution)/shard_map/ppermute | solution.py:189
  6.5 0.0 copy-start
  6.6 0.0 copy-start.2
  6.6 0.0 copy-start.4
  6.6 3.1 %broadcast_select_fusion = (bf16[4,2,64,640]{3,2,1,0:T(8,128)(2,1)}, bf16[4,2,64,640]{3,2,1,0:T(8,128)(2,1)}, bf16[4,2,64,640]{3,2,1,0:T(8,128)(2,1)S(1)}, bf16[4,2,64,640]{3,2,1,0:T(8,128)(2,1)S(1)}) fusion(pred[]{:T(512)S(6)} %eq.19, bf16[4,2,128,1280]{3,2,1,0:T(8,128)(2,1)} %param.10), kind=kLoop, calls=%fused_computation.3 | loop fusion | flops 1310720 | bytes 5242881 | tf_op jit(solution)/shard_map/jit(_where)/select_n | solution.py:234
  9.7 0.3 collective-permute-start.5
  10.0 1.2 %collective-permute-start.3 = (bf16[4,2,64,640]{3,2,1,0:T(8,128)(2,1)}, bf16[4,2,64,640]{3,2,1,0:T(8,128)(2,1)}, u32[]{:S(2)}, u32[]{:S(2)}) collective-permute-start(bf16[4,2,64,640]{3,2,1,0:T(8,128)(2,1)} %get-tuple-element.26), channel_id=1, source_target_pairs={{0,64},{64,0},{128,192},{192,128},{1,65},{65,1},{129,193},{193,129... | collective-permute-start | bytes 1966088 | tf_op jit(solution)/shard_map/ppermute | solution.py:189
  11.2 0.9 collective-permute-start.6
  12.0 1.8 %collective-permute-start.4 = (bf16[4,2,64,640]{3,2,1,0:T(8,128)(2,1)S(1)}, bf16[4,2,64,640]{3,2,1,0:T(8,128)(2,1)}, u32[]{:S(2)}, u32[]{:S(2)}) collective-permute-start(bf16[4,2,64,640]{3,2,1,0:T(8,128)(2,1)S(1)} %get-tuple-element.28.own), channel_id=1, source_target_pairs={{0,192},{64,128},{128,64},{192,0},{1,193},{65,129},{129,65},{193,1... | collective-permute-start | bytes 1966088 | tf_op jit(solution)/shard_map/ppermute | solution.py:189
  13.9 0.1 gt.11
  14.0 0.1 copy.17
  14.1 0.2 copy.18
  14.3 0.1 convert_element_type.21
  14.4 0.0 collective-permute-done.2
  14.4 0.9 %collective-permute-start.1 = (s32[128]{0:T(128)S(1)}, s32[128]{0:T(128)S(1)}, u32[]{:S(2)}, u32[]{:S(2)}) collective-permute-start(s32[128]{0:T(128)S(1)} %add_select_fusion.1), channel_id=1, source_target_pairs={{0,192},{64,128},{128,64},{192,0},{1,193},{65,129},{129,65},{193,1... | collective-permute-start | bytes 1544 | tf_op jit(solution)/shard_map/ppermute | solution.py:189
  15.4 25.8 %collective-permute-done.1 = s32[128]{0:T(128)S(1)} collective-permute-done((s32[128]{0:T(128)S(1)}, s32[128]{0:T(128)S(1)}, u32[]{:S(2)}, u32[]{:S(2)}) %collective-permute-start.1) | collective-permute-done | bytes 544 | tf_op jit(solution)/shard_map/ppermute | solution.py:189
  41.2 0.0 collective-permute-start
  41.2 0.0 collective-permute-done.5.near
  41.3 0.0 copy-start.5
  41.3 3.1 %looks.1.prior = f32[2,32,512]{2,1,0:T(8,128)S(1)} custom-call(s32[1]{0:T(128)} %bitcast.1.me_ref, s32[2,16]{1,0:T(2,128)S(1)} %copy-done.6, bf16[4,2,64,640]{3,2,1,0:T(8,128)(2,1)S(1)} %get-tuple-element.27.own, bf16[4,2,64,640]{3,2,1,0:T(8,128)(2,1)S(1)} %collective-permute-done.5.near, bf16[4,2,64,640]{3,2,1,0:T(8,128)(2,1)S(1)} %collective-permute-done.6.far, ...), custom_call_target="tpu_custom_call" | custom-call | tf_op jit(solution)/shard_map/looks/pallas_call | solution.py:248
  44.4 0.0 collective-permute-done.4.far
  44.4 4.2 %spectrum.1 = (f32[2,128,128]{2,1,0:T(8,128)S(1)}, f32[2,128]{1,0:T(2,128)S(1)}) custom-call(s32[1]{0:T(128)} %bitcast.1.me_ref, s32[2,16]{1,0:T(2,128)S(1)} %copy-done.6, bf16[4,2,64,640]{3,2,1,0:T(8,128)(2,1)S(1)} %get-tuple-element.28.own, bf16[4,2,64,640]{3,2,1,0:T(8,128)(2,1)} %collective-permute-done.3.near, ...), custom_call_target="tpu_custom_call" | custom-call | tf_op jit(solution)/shard_map/spectrum/pallas_call | solution.py:258
  48.6 2.1 %collective-permute-start.8 = (f32[128]{0:T(128)S(1)}, f32[128]{0:T(128)S(1)}, u32[]{:S(2)}, u32[]{:S(2)}) collective-permute-start(f32[128]{0:T(128)S(1)} %slice_bitcast_fusion), channel_id=1, source_target_pairs={{0,128},{64,192},{128,0},{192,64},{1,129},{65,193},{129,1},{193,65... | collective-permute-start | bytes 1544 | tf_op jit(solution)/shard_map/ppermute | solution.py:189
  50.7 0.0 collective-permute-start.7
  50.7 0.1 reshape.113
  50.9 0.1 reshape.114
  51.0 1.6 %collective-permute-done.8 = f32[128]{0:T(128)S(1)} collective-permute-done((f32[128]{0:T(128)S(1)}, f32[128]{0:T(128)S(1)}, u32[]{:S(2)}, u32[]{:S(2)}) %collective-permute-start.8) | collective-permute-done | bytes 544 | tf_op jit(solution)/shard_map/ppermute | solution.py:189
  52.6 0.5 collective-permute-done.7
  53.1 0.6 broadcast_in_dim.29
  53.8 15.8 %all-to-all-start = ((f32[64,1,128]{2,1,0:T(1,128)}), f32[64,1,128]{2,1,0:T(1,128)S(1)}, u32[]{:S(2)}, u32[]{:S(2)}) async-start(f32[64,1,128]{2,1,0:T(1,128)} %bitcast.4), calls=%async_computation | async-start | bytes 65536 | tf_op jit(solution)/shard_map/all_to_all | solution.py:276
  69.6 0.7 select_reduce_fusion.3
  70.3 0.1 select_n.211
  70.4 0.1 select_n.205
  70.4 0.1 select_n.191
  70.5 0.1 select_n.207
  70.6 0.1 select_n.194
  70.7 0.1 select_n.186
  70.8 0.1 select_n.188
  70.9 0.1 select_n.209
  70.9 0.1 reshape.115
  71.1 7.8 %all-to-all-done = f32[64,1,128]{2,1,0:T(1,128)S(1)} async-done(((f32[64,1,128]{2,1,0:T(1,128)}), f32[64,1,128]{2,1,0:T(1,128)S(1)}, u32[]{:S(2)}, u32[]{:S(2)}) %all-to-all-start) | async-done | bytes 32800 | tf_op jit(solution)/shard_map/all_to_all | solution.py:276
  78.9 0.8 goldstein.1
  79.7 1.9 %collective-permute-start.11 = (bf16[128,256]{1,0:T(8,128)(2,1)S(1)}, bf16[128,256]{1,0:T(8,128)(2,1)S(1)}, u32[]{:S(2)}, u32[]{:S(2)}) collective-permute-start(bf16[128,256]{1,0:T(8,128)(2,1)S(1)} %goldstein.1), channel_id=1, source_target_pairs={{0,192},{64,128},{128,64},{192,0},{1,193},{65,129},{129,65},{193,1... | collective-permute-start | bytes 196616 | tf_op jit(solution)/shard_map/ppermute | solution.py:189
  81.6 0.6 collective-permute-start.10
  82.2 0.8 collective-permute-start.9
  83.0 0.7 select_reduce_fusion
  83.7 0.1 select_n.217
  83.8 0.1 select_n.198
  83.9 0.1 select_n.182
  84.0 0.1 select_n.196
  84.0 0.1 select_n.201
  84.1 0.1 select_n.213
  84.2 0.1 select_n.203
  84.3 0.1 select_n.215
  84.4 0.1 concatenate.6
  84.5 1.7 %collective-permute-done.10 = bf16[128,256]{1,0:T(8,128)(2,1)S(1)} collective-permute-done((bf16[128,256]{1,0:T(8,128)(2,1)S(1)}, bf16[128,256]{1,0:T(8,128)(2,1)S(1)}, u32[]{:S(2)}, u32[]{:S(2)}) %collective-permute-start.10) | collective-permute-done | bytes 65568 | tf_op jit(solution)/shard_map/ppermute | solution.py:189
  86.2 0.3 convolution_convert_fusion
  86.5 0.8 copy.19
  (26 shorter events, 0.1 us)
Async XLA Ops:
  2.9 11.6 %collective-permute-start.2 = (s32[128]{0:T(128)S(1)}, s32[128]{0:T(128)S(1)}, u32[]{:S(2)}, u32[]{:S(2)}) collective-permute-start(s32[128]{0:T(128)S(1)} %add_select_fusion.1), channel_id=1, source_target_pairs={{0,128},{64,192},{128,0},{192,64},{1,129},{65,193},{129,1},{193,65... | collective-permute-start | bytes 1544 | tf_op jit(solution)/shard_map/ppermute | solution.py:189
  6.5 7.4 %copy-start.7 = (s32[1,4,32,1]{2,3,1,0:T(1,128)S(1)}, s32[1,4,32,1]{2,3,1,0:T(1,128)}, u32[]{:S(2)}) copy-start(s32[1,4,32,1]{2,3,1,0:T(1,128)} %param.12) | copy-start | bytes 1540
  6.5 34.7 %copy-start.1 = (bf16[640,128]{1,0:T(8,128)(2,1)S(1)}, bf16[640,128]{1,0:T(8,128)(2,1)}, u32[]{:S(2)}) copy-start(bf16[640,128]{1,0:T(8,128)(2,1)} %constant.40.clone.looks_ref) | copy-start | bytes 491524
  6.5 34.7 %copy-start.3 = (bf16[64,192]{1,0:T(8,128)(2,1)S(1)}, bf16[64,192]{1,0:T(8,128)(2,1)}, u32[]{:S(2)}) copy-start(bf16[64,192]{1,0:T(8,128)(2,1)} %constant.41.clone.fwd_ref) | copy-start | bytes 73732
  6.5 34.7 %copy-start.6 = (s32[2,16]{1,0:T(2,128)S(1)}, s32[2,16]{1,0:T(2,128)}, u32[]{:S(2)}) copy-start(s32[2,16]{1,0:T(2,128)} %match_ref.3) | copy-start | bytes 388
  6.5 37.8 %copy-start = (bf16[384,256]{1,0:T(8,128)(2,1)S(1)}, bf16[384,256]{1,0:T(8,128)(2,1)}, u32[]{:S(2)}) copy-start(bf16[384,256]{1,0:T(8,128)(2,1)} %constant.43.clone.cols_ref) | copy-start | bytes 589828
  6.6 37.8 %copy-start.2 = (f32[128,128]{1,0:T(8,128)S(1)}, f32[128,128]{1,0:T(8,128)}, u32[]{:S(2)}) copy-start(f32[128,128]{1,0:T(8,128)} %constant.44.clone.group_ref) | copy-start | bytes 196612
  6.6 37.8 %copy-start.4 = (bf16[64,192]{1,0:T(8,128)(2,1)S(1)}, bf16[64,192]{1,0:T(8,128)(2,1)}, u32[]{:S(2)}) copy-start(bf16[64,192]{1,0:T(8,128)(2,1)} %constant.42.clone.fwd_ref) | copy-start | bytes 73732
  9.7 31.5 %collective-permute-start.5 = (bf16[4,2,64,640]{3,2,1,0:T(8,128)(2,1)}, bf16[4,2,64,640]{3,2,1,0:T(8,128)(2,1)S(1)}, u32[]{:S(2)}, u32[]{:S(2)}) collective-permute-start(bf16[4,2,64,640]{3,2,1,0:T(8,128)(2,1)} %get-tuple-element.25), channel_id=1, source_target_pairs={{0,64},{64,0},{128,192},{192,128},{1,65},{65,1},{129,193},{193,129... | collective-permute-start | bytes 1966088 | tf_op jit(solution)/shard_map/ppermute | solution.py:189
  10.0 34.4 %collective-permute-start.3 = (bf16[4,2,64,640]{3,2,1,0:T(8,128)(2,1)}, bf16[4,2,64,640]{3,2,1,0:T(8,128)(2,1)}, u32[]{:S(2)}, u32[]{:S(2)}) collective-permute-start(bf16[4,2,64,640]{3,2,1,0:T(8,128)(2,1)} %get-tuple-element.26), channel_id=1, source_target_pairs={{0,64},{64,0},{128,192},{192,128},{1,65},{65,1},{129,193},{193,129... | collective-permute-start | bytes 1966088 | tf_op jit(solution)/shard_map/ppermute | solution.py:189
  11.2 30.1 %collective-permute-start.6 = (bf16[4,2,64,640]{3,2,1,0:T(8,128)(2,1)S(1)}, bf16[4,2,64,640]{3,2,1,0:T(8,128)(2,1)S(1)}, u32[]{:S(2)}, u32[]{:S(2)}) collective-permute-start(bf16[4,2,64,640]{3,2,1,0:T(8,128)(2,1)S(1)} %get-tuple-element.27.own), channel_id=1, source_target_pairs={{0,192},{64,128},{128,64},{192,0},{1,193},{65,129},{129,65},{193,1... | collective-permute-start | bytes 1966088 | tf_op jit(solution)/shard_map/ppermute | solution.py:189
  12.0 32.3 %collective-permute-start.4 = (bf16[4,2,64,640]{3,2,1,0:T(8,128)(2,1)S(1)}, bf16[4,2,64,640]{3,2,1,0:T(8,128)(2,1)}, u32[]{:S(2)}, u32[]{:S(2)}) collective-permute-start(bf16[4,2,64,640]{3,2,1,0:T(8,128)(2,1)S(1)} %get-tuple-element.28.own), channel_id=1, source_target_pairs={{0,192},{64,128},{128,64},{192,0},{1,193},{65,129},{129,65},{193,1... | collective-permute-start | bytes 1966088 | tf_op jit(solution)/shard_map/ppermute | solution.py:189
  14.4 26.8 %collective-permute-start.1 = (s32[128]{0:T(128)S(1)}, s32[128]{0:T(128)S(1)}, u32[]{:S(2)}, u32[]{:S(2)}) collective-permute-start(s32[128]{0:T(128)S(1)} %add_select_fusion.1), channel_id=1, source_target_pairs={{0,192},{64,128},{128,64},{192,0},{1,193},{65,129},{129,65},{193,1... | collective-permute-start | bytes 1544 | tf_op jit(solution)/shard_map/ppermute | solution.py:189
  41.2 9.5 %collective-permute-start = (s32[128]{0:T(128)S(1)}, s32[128]{0:T(128)S(1)}, u32[]{:S(2)}, u32[]{:S(2)}) collective-permute-start(s32[128]{0:T(128)S(1)} %add_select_fusion.1), channel_id=1, source_target_pairs={{0,64},{64,0},{128,192},{192,128},{1,65},{65,1},{129,193},{193,129... | collective-permute-start | bytes 1544 | tf_op jit(solution)/shard_map/ppermute | solution.py:189
  41.3 37.6 %copy-start.5 = (bf16[64,96]{1,0:T(8,128)(2,1)S(1)}, bf16[64,96]{1,0:T(8,128)(2,1)}, u32[]{:S(2)}) copy-start(bf16[64,96]{1,0:T(8,128)(2,1)} %constant.45.clone.back_ref) | copy-start | bytes 36868
  48.6 4.0 %collective-permute-start.8 = (f32[128]{0:T(128)S(1)}, f32[128]{0:T(128)S(1)}, u32[]{:S(2)}, u32[]{:S(2)}) collective-permute-start(f32[128]{0:T(128)S(1)} %slice_bitcast_fusion), channel_id=1, source_target_pairs={{0,128},{64,192},{128,0},{192,64},{1,129},{65,193},{129,1},{193,65... | collective-permute-start | bytes 1544 | tf_op jit(solution)/shard_map/ppermute | solution.py:189
  50.7 2.4 %collective-permute-start.7 = (f32[128]{0:T(128)S(1)}, f32[128]{0:T(128)S(1)}, u32[]{:S(2)}, u32[]{:S(2)}) collective-permute-start(f32[128]{0:T(128)S(1)} %slice_bitcast_fusion), channel_id=1, source_target_pairs={{0,64},{64,0},{128,192},{192,128},{1,65},{65,1},{129,193},{193,129... | collective-permute-start | bytes 1544 | tf_op jit(solution)/shard_map/ppermute | solution.py:189
  53.8 25.1 %all-to-all-start = ((f32[64,1,128]{2,1,0:T(1,128)}), f32[64,1,128]{2,1,0:T(1,128)S(1)}, u32[]{:S(2)}, u32[]{:S(2)}) async-start(f32[64,1,128]{2,1,0:T(1,128)} %bitcast.4), calls=%async_computation | async-start | bytes 65536 | tf_op jit(solution)/shard_map/all_to_all | solution.py:276
  79.7 4.8 %collective-permute-start.11 = (bf16[128,256]{1,0:T(8,128)(2,1)S(1)}, bf16[128,256]{1,0:T(8,128)(2,1)S(1)}, u32[]{:S(2)}, u32[]{:S(2)}) collective-permute-start(bf16[128,256]{1,0:T(8,128)(2,1)S(1)} %goldstein.1), channel_id=1, source_target_pairs={{0,192},{64,128},{128,64},{192,0},{1,193},{65,129},{129,65},{193,1... | collective-permute-start | bytes 196616 | tf_op jit(solution)/shard_map/ppermute | solution.py:189
  81.6 4.6 %collective-permute-start.10 = (bf16[128,256]{1,0:T(8,128)(2,1)S(1)}, bf16[128,256]{1,0:T(8,128)(2,1)S(1)}, u32[]{:S(2)}, u32[]{:S(2)}) collective-permute-start(bf16[128,256]{1,0:T(8,128)(2,1)S(1)} %goldstein.1), channel_id=1, source_target_pairs={{0,128},{64,192},{128,0},{192,64},{1,129},{65,193},{129,1},{193,65... | collective-permute-start | bytes 196616 | tf_op jit(solution)/shard_map/ppermute | solution.py:189
  82.2 4.0 %collective-permute-start.9 = (bf16[128,256]{1,0:T(8,128)(2,1)S(1)}, bf16[128,256]{1,0:T(8,128)(2,1)S(1)}, u32[]{:S(2)}, u32[]{:S(2)}) collective-permute-start(bf16[128,256]{1,0:T(8,128)(2,1)S(1)} %goldstein.1), channel_id=1, source_target_pairs={{0,64},{64,0},{128,192},{192,128},{1,65},{65,1},{129,193},{193,129... | collective-permute-start | bytes 196616 | tf_op jit(solution)/shard_map/ppermute | solution.py:189

commit v2 on v1

v2 whole, which is shorter than its diff:
```python
import functools

import jax
import jax.numpy as jnp
import numpy as np
from jax import lax
from jax.experimental import pallas as pl
from jax.experimental.pallas import tpu as pltpu
from jax.sharding import PartitionSpec as P

PATCH = 32
LOOK_L = 4
LOOK_S = 20
BLOCK_ROWS = 4
ROUNDS = 2
ACQ_DEV = 4
SETS = 4
CAP = 64
CHUNKS = (32, 64, 32)

power_floor = 0.25
energy_eps = 1e-06


def halves(x):
    head = x.astype(jnp.bfloat16)
    rest = (x - head.astype(np.float64)).astype(jnp.bfloat16)
    return head, rest


def tables():
    k = np.arange(PATCH)
    angle = (k[:, None] * k[None, :] % PATCH) * (2.0 * np.pi / PATCH)
    cosine, sine = np.cos(angle), np.sin(angle)
    width = PATCH * LOOK_S
    looks = (np.arange(width)[:, None] // LOOK_S == np.arange(128)[None, :]).astype(jnp.bfloat16)
    rows = np.concatenate([cosine, sine], 0) / (LOOK_L * LOOK_S * PATCH)
    rows = np.repeat(rows, LOOK_L, axis=1)
    fwd = halves(rows)
    eye = np.eye(4)
    cols = np.concatenate([np.kron(eye, cosine), np.kron(eye, sine)], 1)
    head, rest = halves(cols)
    cols3 = np.concatenate([head, head, rest], 0)
    order = np.arange(PATCH).reshape(PATCH // BLOCK_ROWS, BLOCK_ROWS).T.reshape(-1)
    back = np.concatenate([cosine[order], sine[order]], 0) / PATCH
    head, rest = halves(back)
    back3 = np.concatenate([head, head, rest], 1)
    group = np.kron(eye, np.ones((PATCH, PATCH))).astype(np.float32)
    row, place = np.arange(128)[:, None], np.arange(128)[None, :] % 32
    pick = [
        row == place // 8 * 32 + turn * 16 + place % 8 * 2 + side for turn in range(ROUNDS) for side in range(2)
    ]
    pick = np.concatenate(pick, 1).astype(jnp.bfloat16)
    return looks, fwd, cols3, back3, group, pick


def forward_table(head, rest):
    pieces, offsets, first, at = [], [], 0, 0
    for step in CHUNKS:
        span = slice(first, first + step)
        piece = np.concatenate([head[:, span], head[:, span], rest[:, span]], axis=1)
        piece = np.pad(piece, ((0, 0), (0, -piece.shape[1] % 128)))
        pieces.append(piece)
        offsets.append(at)
        first, at = first + step, at + piece.shape[1]
    return np.concatenate(pieces, axis=1), offsets


def split(x):
    head = x.astype(jnp.bfloat16)
    return head, (x - head.astype(jnp.float32)).astype(jnp.bfloat16)


def dot(a, b):
    return jnp.dot(a, b, preferred_element_type=jnp.float32)


def forward_chunk(offset, me_ref, match_ref, own, near, far, looks_ref, fwd_ref, prior, pieces):
    lines = own.shape[2]
    me = me_ref[0]
    one, three = me ^ 1, me ^ 3
    total = None
    for j in range(ACQ_DEV):
        pairs = (
            (own, j, near, match_ref[0, me * ACQ_DEV + j]),
            (near, j, own, match_ref[0, one * ACQ_DEV + j]),
            (near, j, far, match_ref[1, one * ACQ_DEV + j]),
            (far, j, near, match_ref[1, three * ACQ_DEV + j]),
        )
        for s, (left, i, right, m) in enumerate(pairs):
            a_re = left[i, 0].astype(jnp.float32)
            a_im = left[i, 1].astype(jnp.float32)
            b_re = right[m, 0].astype(jnp.float32)
            b_im = right[m, 1].astype(jnp.float32)
            re = split(a_re * b_re + a_im * b_im)
            im = split(a_im * b_re - a_re * b_im)
            for h in range(2):
                pieces[j, h, 0, s] = re[h]
                pieces[j, h, 1, s] = im[h]
        width = own.shape[3]
        summed = dot(pieces[j].reshape(2 * 2 * SETS * lines, width), looks_ref[...])
        half = 2 * SETS * lines
        summed = summed[:half] + summed[half:]
        if j:
            summed = pltpu.roll(summed, PATCH * j, 1)
        total = summed if total is None else total + summed
    wide = jnp.concatenate([total[n * lines : (n + 1) * lines] for n in range(2 * SETS)], axis=1)
    head, rest = split(wide)
    both = dot(fwd_ref[:, offset : offset + 3 * lines], jnp.concatenate([head, rest, head], axis=0))
    half = SETS * 128
    re = both[:PATCH, :half] + both[PATCH:, half:]
    im = both[:PATCH, half:] - both[PATCH:, :half]
    if prior is not None:
        re, im = re + prior[0], im + prior[1]
    return re, im


def along_columns(re, im, cols_ref, sign):
    head, rest = split(jnp.concatenate([re, im], axis=0))
    both = dot(jnp.concatenate([head, rest, head], axis=1), cols_ref[...])
    half = re.shape[0]
    return (
        both[:half, :128] - sign * both[half:, 128:],
        both[half:, :128] + sign * both[:half, 128:],
    )


def looks_kernel(offset, me_ref, match_ref, own, near, far, looks_ref, fwd_ref, *rest):
    prior, out, pieces = rest if len(rest) == 3 else (None, *rest)
    re, im = forward_chunk(offset, me_ref, match_ref, own, near, far, looks_ref, fwd_ref, prior, pieces)
    out[0] = re
    out[1] = im


def spectrum_kernel(
    offset, me_ref, match_ref, own, near, far, looks_ref, fwd_ref, prior, cols_ref, group_ref, code, spec, energy, pieces
):
    re, im = forward_chunk(offset, me_ref, match_ref, own, near, far, looks_ref, fwd_ref, prior, pieces)
    re, im = (
        jnp.concatenate([x[:, s * 128 : (s + 1) * 128] for s in range(SETS)], axis=0) for x in (re, im)
    )
    re, im = along_columns(re, im, cols_ref, -1.0)
    half = SETS * PATCH
    spec[:half] = re
    spec[half : 2 * half] = im
    power = re * re + im * im
    sums = jnp.concatenate(
        [jnp.sum(power[s * PATCH : (s + 1) * PATCH], axis=0, keepdims=True) for s in range(SETS)]
        + [jnp.zeros((8 - SETS, 128), jnp.float32)],
        axis=0,
    )
    sums = jnp.dot(sums, group_ref[...], precision=lax.Precision.HIGHEST, preferred_element_type=jnp.float32)
    lane = lax.broadcasted_iota(jnp.int32, (8, 128), 1) & (PATCH - 1)
    row = lax.broadcasted_iota(jnp.int32, (8, 128), 0)
    mine = jnp.sum(jnp.where(lane == row, sums, 0.0), axis=0, keepdims=True)
    spec[2 * half :] = jnp.broadcast_to(code[...], (8, 128))
    energy[...] = jnp.broadcast_to(mine, energy.shape)


def finish_kernel(grid_count, me_ref, held0, held1, held2, held3, parts, cols_ref, back_ref, group_ref, pick_ref, out, values):
    held = (held0, held1, held2, held3)
    n = len(held)
    me = me_ref[0]
    half = SETS * PATCH
    lane = lax.broadcasted_iota(jnp.int32, (1, 128), 1)
    place = lane & (PATCH - 1)
    n_tile = parts.shape[0] // n
    shares = [
        jnp.sum(parts[pl.ds(pl.multiple_of((me ^ k) * n_tile, 8), n_tile), :], axis=0, keepdims=True)
        for k in range(n)
    ]
    row = lax.broadcasted_iota(jnp.int32, (8, 128), 0)
    spread = []
    for k in range(n):
        other = jnp.where(place < 2, shares[k ^ 1], shares[k ^ 2])
        other = jnp.broadcast_to(other, (8, 128))
        other = jnp.where(lane & 1 == 0, pltpu.roll(other, 127, 1), pltpu.roll(other, 1, 1))
        spread.append(jnp.where(place == row, shares[k] + other, 0.0))
    spread = jnp.concatenate(spread, axis=0)
    spread = jnp.dot(spread, group_ref[...], precision=lax.Precision.HIGHEST, preferred_element_type=jnp.float32)
    scale = spread * (1.0 / grid_count) + energy_eps
    inverse = 1.0 / scale
    root = lax.rsqrt(scale)
    res, ims = [], []
    for k in range(n):
        for s in range(SETS):
            re = held[k][s * PATCH : (s + 1) * PATCH]
            im = held[k][half + s * PATCH : half + (s + 1) * PATCH]
            power = (re * re + im * im) * inverse[8 * k + s : 8 * k + s + 1]
            weight = jnp.sqrt(jnp.sqrt(power + power_floor))
            res.append(weight * re)
            ims.append(weight * im)
    re, im = along_columns(jnp.concatenate(res, axis=0), jnp.concatenate(ims, axis=0), cols_ref, 1.0)
    wide = jnp.concatenate(
        [x[m * PATCH : (m + 1) * PATCH] for x in (re, im) for m in range(n * SETS)], axis=1
    )
    head, rest = split(wide)
    both = dot(back_ref[...], jnp.concatenate([head, rest, head], axis=0))
    whole = n * SETS * 128
    final = (both[:PATCH, :whole] - both[PATCH:, whole:], both[:PATCH, whole:] + both[PATCH:, :whole])
    blocks = PATCH // BLOCK_ROWS
    where = lax.broadcasted_iota(jnp.int32, (blocks, 128), 1) // PATCH
    for part in range(2):
        for m in range(n * SETS):
            at = m // SETS * 8 + m % SETS
            block = final[part][:, m * 128 : (m + 1) * 128] * root[at : at + 1]
            rows = [block[i * blocks : (i + 1) * blocks] for i in range(BLOCK_ROWS)]
            turned = []
            for j in range(ACQ_DEV):
                value = None
                for i in range(BLOCK_ROWS):
                    moved = rows[i] if i == j else pltpu.roll(rows[i], (PATCH * (i - j)) % 128, 1)
                    value = moved if value is None else jnp.where(where == i, moved, value)
                turned.append(value)
            values[m * 32 : (m + 1) * 32, part * 128 : (part + 1) * 128] = jnp.concatenate(
                turned, axis=0
            ).astype(jnp.bfloat16)

    slots = []
    for k in range(n):
        slot = held[k][2 * half : 2 * half + 1].astype(jnp.int32) - me * CAP
        slots.append(jnp.where((slot >= 0) & (slot < CAP), slot + (me ^ k) * CAP, -1))
    slots = jnp.concatenate(slots + slots, axis=0).astype(jnp.float32).astype(jnp.bfloat16)
    picked = dot(slots, pick_ref[...])
    side_me = 1 - ((me ^ (me >> 1)) & 1)
    chosen = []
    for k in range(n):
        side = side_me ^ (1 if k in (1, 2) else 0)
        line = None
        for s, (e, turn) in enumerate(((k, 0), (k ^ 1, 0), (k ^ 1, 1), (k ^ 3, 1))):
            zero = picked[e : e + 1, 2 * turn * 128 : (2 * turn + 1) * 128]
            one = picked[e : e + 1, (2 * turn + 1) * 128 : (2 * turn + 2) * 128]
            both_sides = jnp.where(side == 0, zero, one)
            line = both_sides if line is None else jnp.where(lane // PATCH == s, both_sides, line)
        chosen.append(line)
    chosen = jnp.concatenate(chosen, axis=1).astype(jnp.int32)
    n_slots = n * CAP
    choice = lax.broadcasted_iota(jnp.int32, (n_slots, chosen.shape[1]), 0) == chosen
    choice = jnp.where(choice, 1.0, 0.0).astype(jnp.bfloat16)
    result = dot(choice, values[...])
    out[...] = result.astype(jnp.bfloat16)


VMEM = pl.BlockSpec(memory_space=pltpu.VMEM)
SMEM = pl.BlockSpec(memory_space=pltpu.SMEM)
PARAMS = pltpu.CompilerParams(vmem_limit_bytes=48 * 2**20)


def swapped(x, bits):
    return lax.ppermute(x, "acq", [(i, i ^ bits) for i in range(lax.axis_size("acq"))])


def slot_codes(dest, coherent):
    rows = dest.size
    n_acq = lax.axis_size("acq")
    owner = dest.reshape(rows)
    onehot = (owner[None, :] == jnp.arange(n_acq)[:, None]).astype(jnp.float32)
    before = (jnp.arange(rows)[:, None] < jnp.arange(rows)[None, :]).astype(jnp.bfloat16)
    counts = jnp.dot(onehot.astype(jnp.bfloat16), before, preferred_element_type=jnp.float32)
    rank = jnp.sum(counts * onehot, axis=0).astype(jnp.int32)
    code = jnp.where(coherent.reshape(rows) > 0, owner * CAP + rank, n_acq * CAP)
    return code.astype(jnp.float32).reshape(1, rows)


def shards(slc, match, dest, coherent):
    _, _, lines_dev, samples_dev = slc.shape
    n_acq = lax.axis_size("acq")
    n_tile = lax.axis_size("tile")
    grid_count = lines_dev * n_tile // LOOK_L * (samples_dev // LOOK_S)
    me = lax.axis_index("acq").astype(jnp.int32)
    me_arr = me.reshape(1)
    column = 1 - ((me ^ (me >> 1)) & 1)
    looks, (fwd_head, fwd_rest), cols3, back3, group, pick = tables()
    width = samples_dev // 2

    chunks = []
    first = 0
    for step in CHUNKS:
        if len(chunks) > 1:
            arrived = chunks[-2][2:]
            slc, *arrived = lax.optimization_barrier((slc, *arrived))
            chunks[-2] = chunks[-2][:2] + tuple(arrived)
        part = slc[:, :, first : first + step]
        left, right = part[..., :width], part[..., width:]
        own = jnp.where(column == 0, left, right)
        other = jnp.where(column == 0, right, left)
        own, other, slc, dest, coherent = lax.optimization_barrier((own, other, slc, dest, coherent))
        chunks.append((first, own, swapped(other, 1), swapped(own, 3)))
        first += step

    code = slot_codes(dest, coherent)

    forward, offsets = forward_table(fwd_head, fwd_rest)
    prior = None
    for n, (first, own, near, far) in enumerate(chunks):
        step = own.shape[2]
        scratch = [pltpu.VMEM((ACQ_DEV, 2, 2, SETS, step, width), jnp.bfloat16)]
        args = [me_arr, match, own, near, far, looks, forward] + ([] if prior is None else [prior])
        if n < len(chunks) - 1:
            prior = pl.pallas_call(
                functools.partial(looks_kernel, offsets[n]),
                out_shape=jax.ShapeDtypeStruct((2, PATCH, SETS * 128), jnp.float32),
                in_specs=[SMEM, SMEM] + [VMEM] * (len(args) - 2),
                out_specs=VMEM,
                scratch_shapes=scratch,
                compiler_params=PARAMS,
                name="looks",
            )(*args)
        else:
            spec, energy = pl.pallas_call(
                functools.partial(spectrum_kernel, offsets[n]),
                out_shape=(
                    jax.ShapeDtypeStruct((2 * SETS * PATCH + 8, 128), jnp.float32),
                    jax.ShapeDtypeStruct((n_acq * n_tile, 128), jnp.float32),
                ),
                in_specs=[SMEM, SMEM] + [VMEM] * (len(args) + 1),
                out_specs=(VMEM, VMEM),
                scratch_shapes=scratch,
                compiler_params=PARAMS,
                name="spectrum",
            )(*args, cols3, group, code)

    parts = lax.all_to_all(energy, ("acq", "tile"), split_axis=0, concat_axis=0, tiled=True)
    held = [spec] + [swapped(spec, bits) for bits in range(1, n_acq)]
    out = pl.pallas_call(
        functools.partial(finish_kernel, float(grid_count)),
        out_shape=jax.ShapeDtypeStruct((n_acq * CAP, 256), jnp.bfloat16),
        in_specs=[SMEM] + [VMEM] * 9,
        out_specs=VMEM,
        scratch_shapes=[pltpu.VMEM((n_acq * SETS * 32, 256), jnp.bfloat16)],
        compiler_params=PARAMS,
        name="goldstein",
    )(me_arr, *held, parts, cols3, back3, group, pick)
    return out.reshape(1, n_acq * CAP, 2, 128)


def solution(mesh):
    return jax.shard_map(
        shards,
        mesh=mesh,
        in_specs=(
            P("acq", None, "tile", None),
            P(),
            P("tile", "acq", None, None),
            P("tile", "acq", None),
        ),
        out_specs=P("tile", "acq", None, None),
        check_vma=False,
    )
```

time: 87.5 us -> 67.6 us (0.77)
  waiting for transfers between devices: 37.4 us -> 23.1 us
  starting transfers between devices: 30 us -> 25.1 us
  Pallas kernels: 8.01 us -> 9.75 us
  local copies, waits for them, and re-layouts: 4.48 us -> 3.21 us
    all_to_all x1, waiting for transfers between devices: 7.77 us -> 0.01 us  [shards(): lax.all_to_all(energy, ('acq', 'tile'), split_axis=0, concat_axis=0, tile...]
    ppermute x12 -> x9, waiting for transfers between devices: 29.7 us -> 23.1 us  [swapped(): lax.ppermute(x, 'acq', [(i, i ^ bits) for i in range(lax.axis_size('acq'))])]
    ppermute x12 -> x9, starting transfers between devices: 14.2 us -> 10.6 us  [swapped(): lax.ppermute(x, 'acq', [(i, i ^ bits) for i in range(lax.axis_size('acq'))])]
    select_n x1 -> x3, other arithmetic: 3.12 us -> 5.37 us  [shards(): other = jnp.where(column == 0, right, left)]
    pallas_call x3 -> x4, Pallas kernels: 8.01 us -> 9.75 us  [the longest x2 4.98 us: shards(): pl.pallas_call(functools.partial(looks_kernel, offsets[n]), out_shape=jax...]
    select_n x7 -> x0, other arithmetic: 1.45 us -> none  [the longest x2 1.41 us: slot_choice(): jnp.where(side == 0, slots[bits][:, turn, :, 0], slots[bits][:, turn, :, 1])]
    unnamed x1 -> x0, other arithmetic: 1.34 us -> none
    all_to_all x1, starting transfers between devices: 15.8 us -> 14.5 us  [shards(): lax.all_to_all(energy, ('acq', 'tile'), split_axis=0, concat_axis=0, tile...]
  transfers between devices with their start and end apart: 13 -> 10, of which waited for: 5 -> 7; matrix products, arithmetic and copies ran while one was open for 8% -> 9% of each run, Pallas kernels for 8% -> 7%
where the time goes in v2:
time: 67.6 us; the launch traced here: 67.4 us
  starting transfers between devices  25.1 us (37%)
  waiting for transfers between devices  23.1 us (34%)
  Pallas kernels  9.75 us (14%)
  other arithmetic  6.05 us (9%)
  local copies, waits for them, and re-layouts  3.21 us (5%)
    ppermute x9, waiting for transfers between devices, swapped(): lax.ppermute(x, 'acq', [(i, i ^ bits) for i in range(lax.axis_size('acq'))])  23.1 us
    all_to_all x1, starting transfers between devices, shards(): lax.all_to_all(energy, ('acq', 'tile'), split_axis=0, concat_axis=0, tile...  14.5 us
    ppermute x9, starting transfers between devices, swapped(): lax.ppermute(x, 'acq', [(i, i ^ bits) for i in range(lax.axis_size('acq'))])  10.6 us
    select_n x3, other arithmetic, shards(): other = jnp.where(column == 0, right, left)  5.37 us
    pallas_call x2, Pallas kernels, shards(): pl.pallas_call(functools.partial(looks_kernel, offsets[n]), out_shape=jax...  4.98 us
    pallas_call x1, Pallas kernels, shards(): pl.pallas_call(functools.partial(spectrum_kernel, offsets[n]), out_shape=...  3.08 us
    unnamed x22, local copies, waits for them, and re-layouts  1.75 us
    pallas_call x1, Pallas kernels, shards(): pl.pallas_call(functools.partial(finish_kernel, float(grid_count)), out_s...  1.68 us
  transfers between devices with their start and end apart: 10, of which 7 were waited for; matrix products, arithmetic and copies ran while one was open for 9% of the time, Pallas kernels for 7%

profile of v2, /device:TPU:1, one launch (start us, length us, event | category | flops | bytes accessed | tf_op | source)
XLA Modules:
  0.0 67.4 jit_solution(14160257202368466390)
XLA Ops:
  0.0 0.0 copy-start.10
  0.0 0.0 copy-start.9
  0.0 0.0 copy-start
  0.0 0.0 copy-start.2
  0.0 0.0 copy-start.8
  0.0 1.2 %broadcast_select_fusion.4 = (bf16[4,2,32,640]{3,2,1,0:T(8,128)(2,1)S(1)}, bf16[4,2,32,640]{3,2,1,0:T(8,128)(2,1)S(1)}) fusion(pred[]{:T(512)S(6)} %eq.10, bf16[4,2,128,1280]{3,2,1,0:T(8,128)(2,1)} %param.10), kind=kLoop, calls=%fused_computation.6 | loop fusion | flops 327680 | bytes 1310721 | tf_op jit(solution)/shard_map/jit(_where)/select_n | solution.py:286
  1.3 3.4 %collective-permute-start.1 = (bf16[4,2,32,640]{3,2,1,0:T(8,128)(2,1)S(1)}, bf16[4,2,32,640]{3,2,1,0:T(8,128)(2,1)S(1)}, u32[]{:S(2)}, u32[]{:S(2)}) collective-permute-start(bf16[4,2,32,640]{3,2,1,0:T(8,128)(2,1)S(1)} %get-tuple-element.29.own), channel_id=1, source_target_pairs={{0,192},{64,128},{128,64},{192,0},{1,193},{65,129},{129,65},{193,1... | collective-permute-start | bytes 983048 | tf_op jit(solution)/shard_map/ppermute | solution.py:250
  4.7 0.0 collective-permute-start
  4.7 2.3 %broadcast_select_fusion = (bf16[4,2,64,640]{3,2,1,0:T(8,128)(2,1)}, bf16[4,2,64,640]{3,2,1,0:T(8,128)(2,1)S(1)}) fusion(pred[]{:T(512)S(6)} %eq.10, bf16[4,2,128,1280]{3,2,1,0:T(8,128)(2,1)} %param.10), kind=kLoop, calls=%fused_computation.2 | loop fusion | flops 655360 | bytes 2621441 | tf_op jit(solution)/shard_map/jit(_where)/select_n | solution.py:286
  6.9 0.0 copy-start.1
  6.9 0.0 copy-start.5
  6.9 1.5 %collective-permute-start.4 = (bf16[4,2,64,640]{3,2,1,0:T(8,128)(2,1)}, bf16[4,2,64,640]{3,2,1,0:T(8,128)(2,1)S(1)}, u32[]{:S(2)}, u32[]{:S(2)}) collective-permute-start(bf16[4,2,64,640]{3,2,1,0:T(8,128)(2,1)} %get-tuple-element.36), channel_id=1, source_target_pairs={{0,64},{64,0},{128,192},{192,128},{1,65},{65,1},{129,193},{193,129... | collective-permute-start | bytes 1966088 | tf_op jit(solution)/shard_map/ppermute | solution.py:250
  8.4 0.1 collective-permute-start.5
  8.5 2.5 %collective-permute-done.1.far = bf16[4,2,32,640]{3,2,1,0:T(8,128)(2,1)S(1)} collective-permute-done((bf16[4,2,32,640]{3,2,1,0:T(8,128)(2,1)S(1)}, bf16[4,2,32,640]{3,2,1,0:T(8,128)(2,1)S(1)}, u32[]{:S(2)}, u32[]{:S(2)}) %collective-permute-start.1) | collective-permute-done | bytes 327712 | tf_op jit(solution)/shard_map/ppermute | solution.py:250
  11.0 1.9 %collective-permute-done.near = bf16[4,2,32,640]{3,2,1,0:T(8,128)(2,1)S(1)} collective-permute-done((bf16[4,2,32,640]{3,2,1,0:T(8,128)(2,1)S(1)}, bf16[4,2,32,640]{3,2,1,0:T(8,128)(2,1)S(1)}, u32[]{:S(2)}, u32[]{:S(2)}) %collective-permute-start) | collective-permute-done | bytes 327712 | tf_op jit(solution)/shard_map/ppermute | solution.py:250
  12.9 0.0 copy-start.3
  12.9 0.7 %copy-done.3 = bf16[4,2,32,640]{3,2,1,0:T(8,128)(2,1)} copy-done((bf16[4,2,32,640]{3,2,1,0:T(8,128)(2,1)}, bf16[4,2,32,640]{3,2,1,0:T(8,128)(2,1)S(1)}, u32[]{:S(2)}) %copy-start.3) | copy-done | bytes 327704
  13.7 1.9 %broadcast_select_fusion.2 = (bf16[4,2,32,640]{3,2,1,0:T(8,128)(2,1)}, bf16[4,2,32,640]{3,2,1,0:T(8,128)(2,1)S(1)}) fusion(pred[]{:T(512)S(6)} %eq.10, bf16[4,2,128,1280]{3,2,1,0:T(8,128)(2,1)} %param.10), kind=kLoop, calls=%fused_computation.4 | loop fusion | flops 327680 | bytes 1310721 | tf_op jit(solution)/shard_map/jit(_where)/select_n | solution.py:286
  15.5 0.5 broadcast.36
  16.1 0.0 copy-done.10
  16.1 0.7 fusion.4
  16.7 0.1 eq.11
  16.8 0.1 mul.21
  16.9 0.0 copy-done.9
  16.9 0.1 gt.18
  17.0 0.1 collective-permute-start.2
  17.1 1.6 %collective-permute-start.3 = (bf16[4,2,32,640]{3,2,1,0:T(8,128)(2,1)S(1)}, bf16[4,2,32,640]{3,2,1,0:T(8,128)(2,1)S(1)}, u32[]{:S(2)}, u32[]{:S(2)}) collective-permute-start(bf16[4,2,32,640]{3,2,1,0:T(8,128)(2,1)S(1)} %get-tuple-element.33.own), channel_id=1, source_target_pairs={{0,192},{64,128},{128,64},{192,0},{1,193},{65,129},{129,65},{193,1... | collective-permute-start | bytes 983048 | tf_op jit(solution)/shard_map/ppermute | solution.py:250
  18.6 0.0 copy-done
  18.6 0.0 copy-done.2
  18.6 0.0 copy-done.8
  18.6 0.0 copy-start.4
  18.7 1.0 %copy-done.4 = bf16[4,2,32,640]{3,2,1,0:T(8,128)(2,1)S(1)} copy-done((bf16[4,2,32,640]{3,2,1,0:T(8,128)(2,1)S(1)}, bf16[4,2,32,640]{3,2,1,0:T(8,128)(2,1)}, u32[]{:S(2)}) %copy-start.4) | copy-done | bytes 327704
  19.6 0.0 copy-start.7
  19.6 1.9 %looks.2.rest_0_ = f32[2,32,512]{2,1,0:T(8,128)S(1)} custom-call(s32[1]{0:T(128)} %bitcast.me_ref, s32[2,16]{1,0:T(2,128)S(1)} %copy-done.8, bf16[4,2,32,640]{3,2,1,0:T(8,128)(2,1)S(1)} %get-tuple-element.29.own, bf16[4,2,32,640]{3,2,1,0:T(8,128)(2,1)S(1)} %copy-done.4, bf16[4,2,32,640]{3,2,1,0:T(8,128)(2,1)S(1)} %collective-permute-done.1.far, ...), custom_call_target="tpu_custom_call" | custom-call | tf_op jit(solution)/shard_map/looks/pallas_call | solution.py:300
  21.6 0.0 copy-start.6
  21.6 0.1 fusion
  21.7 5.2 %collective-permute-done.4.near = bf16[4,2,64,640]{3,2,1,0:T(8,128)(2,1)S(1)} collective-permute-done((bf16[4,2,64,640]{3,2,1,0:T(8,128)(2,1)}, bf16[4,2,64,640]{3,2,1,0:T(8,128)(2,1)S(1)}, u32[]{:S(2)}, u32[]{:S(2)}) %collective-permute-start.4) | collective-permute-done | bytes 655392 | tf_op jit(solution)/shard_map/ppermute | solution.py:250
  27.0 0.0 collective-permute-done.5.far
  27.0 3.1 %looks.3.prior = f32[2,32,512]{2,1,0:T(8,128)S(1)} custom-call(s32[1]{0:T(128)} %bitcast.me_ref, s32[2,16]{1,0:T(2,128)S(1)} %copy-done.8, bf16[4,2,64,640]{3,2,1,0:T(8,128)(2,1)S(1)} %get-tuple-element.35.own, bf16[4,2,64,640]{3,2,1,0:T(8,128)(2,1)S(1)} %collective-permute-done.4.near, bf16[4,2,64,640]{3,2,1,0:T(8,128)(2,1)S(1)} %collective-permute-done.5.far, ...), custom_call_target="tpu_custom_call" | custom-call | tf_op jit(solution)/shard_map/looks/pallas_call | solution.py:300
  30.0 4.0 %collective-permute-done.2.near = bf16[4,2,32,640]{3,2,1,0:T(8,128)(2,1)S(1)} collective-permute-done((bf16[4,2,32,640]{3,2,1,0:T(8,128)(2,1)}, bf16[4,2,32,640]{3,2,1,0:T(8,128)(2,1)S(1)}, u32[]{:S(2)}, u32[]{:S(2)}) %collective-permute-start.2) | collective-permute-done | bytes 327712 | tf_op jit(solution)/shard_map/ppermute | solution.py:250
  34.0 0.0 collective-permute-done.3.far
  34.0 0.0 copy-done.1
  34.0 0.0 copy-done.5
  34.0 3.1 %spectrum.1 = (f32[264,128]{1,0:T(8,128)S(1)}, f32[256,128]{1,0:T(8,128)}) custom-call(s32[1]{0:T(128)} %bitcast.me_ref, s32[2,16]{1,0:T(2,128)S(1)} %copy-done.8, bf16[4,2,32,640]{3,2,1,0:T(8,128)(2,1)S(1)} %get-tuple-element.33.own, bf16[4,2,32,640]{3,2,1,0:T(8,128)(2,1)S(1)} %collective-permute-done.2.near, ...), custom_call_target="tpu_custom_call" | custom-call | tf_op jit(solution)/shard_map/spectrum/pallas_call | solution.py:310
  37.1 14.5 %all-to-all-start = ((f32[256,1,128]{2,1,0:T(1,128)}), f32[256,1,128]{2,1,0:T(1,128)S(1)}, u32[]{:S(2)}, u32[]{:S(2)}) async-start(f32[256,1,128]{2,1,0:T(1,128)} %bitcast.3), calls=%async_computation | async-start | bytes 262144 | tf_op jit(solution)/shard_map/all_to_all | solution.py:323
  51.6 1.5 %collective-permute-start.6 = (f32[264,128]{1,0:T(8,128)S(1)}, f32[264,128]{1,0:T(8,128)S(1)}, u32[]{:S(2)}, u32[]{:S(2)}) collective-permute-start(f32[264,128]{1,0:T(8,128)S(1)} %get-tuple-element.41.held0), channel_id=1, source_target_pairs={{0,64},{64,0},{128,192},{192,128},{1,65},{65,1},{129,193},{193,129... | collective-permute-start | bytes 405512 | tf_op jit(solution)/shard_map/ppermute | solution.py:250
  53.0 2.4 %collective-permute-start.7 = (f32[264,128]{1,0:T(8,128)S(1)}, f32[264,128]{1,0:T(8,128)S(1)}, u32[]{:S(2)}, u32[]{:S(2)}) collective-permute-start(f32[264,128]{1,0:T(8,128)S(1)} %get-tuple-element.41.held0), channel_id=1, source_target_pairs={{0,128},{64,192},{128,0},{192,64},{1,129},{65,193},{129,1},{193,65... | collective-permute-start | bytes 405512 | tf_op jit(solution)/shard_map/ppermute | solution.py:250
  55.4 0.1 collective-permute-start.8
  55.5 0.5 collective-permute-done.6.held1
  56.1 6.8 %collective-permute-done.7.held2 = f32[264,128]{1,0:T(8,128)S(1)} collective-permute-done((f32[264,128]{1,0:T(8,128)S(1)}, f32[264,128]{1,0:T(8,128)S(1)}, u32[]{:S(2)}, u32[]{:S(2)}) %collective-permute-start.7) | collective-permute-done | bytes 135200 | tf_op jit(solution)/shard_map/ppermute | solution.py:250
  62.9 2.1 %collective-permute-done.8.held3 = f32[264,128]{1,0:T(8,128)S(1)} collective-permute-done((f32[264,128]{1,0:T(8,128)S(1)}, f32[264,128]{1,0:T(8,128)S(1)}, u32[]{:S(2)}, u32[]{:S(2)}) %collective-permute-start.8) | collective-permute-done | bytes 135200 | tf_op jit(solution)/shard_map/ppermute | solution.py:250
  65.0 0.0 all-to-all-done
  65.0 0.0 copy-done.7
  65.0 0.0 copy-done.6
  65.0 1.7 %goldstein.1 = bf16[256,256]{1,0:T(8,128)(2,1)S(1)} custom-call(s32[1]{0:T(128)} %bitcast.me_ref, f32[264,128]{1,0:T(8,128)S(1)} %get-tuple-element.41.held0, f32[264,128]{1,0:T(8,128)S(1)} %collective-permute-done.6.held1, f32[264,128]{1,0:T(8,128)S(1)} %collective-permute-done.7.held2, f32[264,128]{1,0:T(8,128)S(1)} %collective-permute-done.8.held3, ...), custom_call_target="tpu_custom_call" | custom-call | tf_op jit(solution)/shard_map/goldstein/pallas_call | solution.py:325
  66.7 0.7 %reshape.54 = bf16[1,256,2,128]{3,2,1,0:T(2,128)(2,1)} reshape(bf16[256,256]{1,0:T(8,128)(2,1)S(1)} %goldstein.1) | data formatting | bytes 262144 | tf_op jit(solution)/shard_map/reshape | solution.py:334
  (2 shorter events, 0.0 us)
Async XLA Ops:
  0.0 16.1 %copy-start.10 = (s32[1,4,32,1]{2,3,1,0:T(1,128)S(1)}, s32[1,4,32,1]{2,3,1,0:T(1,128)}, u32[]{:S(2)}) copy-start(s32[1,4,32,1]{2,3,1,0:T(1,128)} %param.12) | copy-start | bytes 1540
  0.0 16.9 %copy-start.9 = (s32[1,4,32]{2,1,0:T(4,128)S(1)}, s32[1,4,32]{2,1,0:T(4,128)}, u32[]{:S(2)}) copy-start(s32[1,4,32]{2,1,0:T(4,128)} %param.13) | copy-start | bytes 1540
  0.0 18.6 %copy-start = (bf16[640,128]{1,0:T(8,128)(2,1)S(1)}, bf16[640,128]{1,0:T(8,128)(2,1)}, u32[]{:S(2)}) copy-start(bf16[640,128]{1,0:T(8,128)(2,1)} %constant.30.clone.looks_ref) | copy-start | bytes 491524
  0.0 18.6 %copy-start.2 = (bf16[64,512]{1,0:T(8,128)(2,1)S(1)}, bf16[64,512]{1,0:T(8,128)(2,1)}, u32[]{:S(2)}) copy-start(bf16[64,512]{1,0:T(8,128)(2,1)} %constant.31.clone.fwd_ref) | copy-start | bytes 196612
  0.0 18.6 %copy-start.8 = (s32[2,16]{1,0:T(2,128)S(1)}, s32[2,16]{1,0:T(2,128)}, u32[]{:S(2)}) copy-start(s32[2,16]{1,0:T(2,128)} %match_ref.5) | copy-start | bytes 388
  1.3 9.8 %collective-permute-start.1 = (bf16[4,2,32,640]{3,2,1,0:T(8,128)(2,1)S(1)}, bf16[4,2,32,640]{3,2,1,0:T(8,128)(2,1)S(1)}, u32[]{:S(2)}, u32[]{:S(2)}) collective-permute-start(bf16[4,2,32,640]{3,2,1,0:T(8,128)(2,1)S(1)} %get-tuple-element.29.own), channel_id=1, source_target_pairs={{0,192},{64,128},{128,64},{192,0},{1,193},{65,129},{129,65},{193,1... | collective-permute-start | bytes 983048 | tf_op jit(solution)/shard_map/ppermute | solution.py:250
  4.7 8.3 %collective-permute-start = (bf16[4,2,32,640]{3,2,1,0:T(8,128)(2,1)S(1)}, bf16[4,2,32,640]{3,2,1,0:T(8,128)(2,1)S(1)}, u32[]{:S(2)}, u32[]{:S(2)}) collective-permute-start(bf16[4,2,32,640]{3,2,1,0:T(8,128)(2,1)S(1)} %get-tuple-element.28), channel_id=1, source_target_pairs={{0,64},{64,0},{128,192},{192,128},{1,65},{65,1},{129,193},{193,129... | collective-permute-start | bytes 983048 | tf_op jit(solution)/shard_map/ppermute | solution.py:250
  6.9 27.1 %copy-start.1 = (bf16[384,256]{1,0:T(8,128)(2,1)S(1)}, bf16[384,256]{1,0:T(8,128)(2,1)}, u32[]{:S(2)}) copy-start(bf16[384,256]{1,0:T(8,128)(2,1)} %constant.32.clone.cols_ref) | copy-start | bytes 589828
  6.9 27.1 %copy-start.5 = (f32[128,128]{1,0:T(8,128)S(1)}, f32[128,128]{1,0:T(8,128)}, u32[]{:S(2)}) copy-start(f32[128,128]{1,0:T(8,128)} %constant.33.clone.group_ref) | copy-start | bytes 196612
  6.9 20.0 %collective-permute-start.4 = (bf16[4,2,64,640]{3,2,1,0:T(8,128)(2,1)}, bf16[4,2,64,640]{3,2,1,0:T(8,128)(2,1)S(1)}, u32[]{:S(2)}, u32[]{:S(2)}) collective-permute-start(bf16[4,2,64,640]{3,2,1,0:T(8,128)(2,1)} %get-tuple-element.36), channel_id=1, source_target_pairs={{0,64},{64,0},{128,192},{192,128},{1,65},{65,1},{129,193},{193,129... | collective-permute-start | bytes 1966088 | tf_op jit(solution)/shard_map/ppermute | solution.py:250
  8.4 18.6 %collective-permute-start.5 = (bf16[4,2,64,640]{3,2,1,0:T(8,128)(2,1)S(1)}, bf16[4,2,64,640]{3,2,1,0:T(8,128)(2,1)S(1)}, u32[]{:S(2)}, u32[]{:S(2)}) collective-permute-start(bf16[4,2,64,640]{3,2,1,0:T(8,128)(2,1)S(1)} %get-tuple-element.35.own), channel_id=1, source_target_pairs={{0,192},{64,128},{128,64},{192,0},{1,193},{65,129},{129,65},{193,1... | collective-permute-start | bytes 1966088 | tf_op jit(solution)/shard_map/ppermute | solution.py:250
  12.9 0.7 %copy-start.3 = (bf16[4,2,32,640]{3,2,1,0:T(8,128)(2,1)}, bf16[4,2,32,640]{3,2,1,0:T(8,128)(2,1)S(1)}, u32[]{:S(2)}) copy-start(bf16[4,2,32,640]{3,2,1,0:T(8,128)(2,1)S(1)} %collective-permute-done.near) | copy-start | bytes 983044
  17.0 17.0 %collective-permute-start.2 = (bf16[4,2,32,640]{3,2,1,0:T(8,128)(2,1)}, bf16[4,2,32,640]{3,2,1,0:T(8,128)(2,1)S(1)}, u32[]{:S(2)}, u32[]{:S(2)}) collective-permute-start(bf16[4,2,32,640]{3,2,1,0:T(8,128)(2,1)} %get-tuple-element.34), channel_id=1, source_target_pairs={{0,64},{64,0},{128,192},{192,128},{1,65},{65,1},{129,193},{193,129... | collective-permute-start | bytes 983048 | tf_op jit(solution)/shard_map/ppermute | solution.py:250
  17.1 16.9 %collective-permute-start.3 = (bf16[4,2,32,640]{3,2,1,0:T(8,128)(2,1)S(1)}, bf16[4,2,32,640]{3,2,1,0:T(8,128)(2,1)S(1)}, u32[]{:S(2)}, u32[]{:S(2)}) collective-permute-start(bf16[4,2,32,640]{3,2,1,0:T(8,128)(2,1)S(1)} %get-tuple-element.33.own), channel_id=1, source_target_pairs={{0,192},{64,128},{128,64},{192,0},{1,193},{65,129},{129,65},{193,1... | collective-permute-start | bytes 983048 | tf_op jit(solution)/shard_map/ppermute | solution.py:250
  18.6 1.0 %copy-start.4 = (bf16[4,2,32,640]{3,2,1,0:T(8,128)(2,1)S(1)}, bf16[4,2,32,640]{3,2,1,0:T(8,128)(2,1)}, u32[]{:S(2)}) copy-start(bf16[4,2,32,640]{3,2,1,0:T(8,128)(2,1)} %copy-done.3) | copy-start | bytes 983044
  19.6 45.4 %copy-start.7 = (bf16[64,96]{1,0:T(8,128)(2,1)S(1)}, bf16[64,96]{1,0:T(8,128)(2,1)}, u32[]{:S(2)}) copy-start(bf16[64,96]{1,0:T(8,128)(2,1)} %constant.34.clone.back_ref) | copy-start | bytes 36868
  21.6 43.5 %copy-start.6 = (bf16[128,512]{1,0:T(8,128)(2,1)S(1)}, bf16[128,512]{1,0:T(8,128)(2,1)}, u32[]{:S(2)}) copy-start(bf16[128,512]{1,0:T(8,128)(2,1)} %constant.35.clone.pick_ref) | copy-start | bytes 393220
  37.1 27.9 %all-to-all-start = ((f32[256,1,128]{2,1,0:T(1,128)}), f32[256,1,128]{2,1,0:T(1,128)S(1)}, u32[]{:S(2)}, u32[]{:S(2)}) async-start(f32[256,1,128]{2,1,0:T(1,128)} %bitcast.3), calls=%async_computation | async-start | bytes 262144 | tf_op jit(solution)/shard_map/all_to_all | solution.py:323
  51.6 4.5 %collective-permute-start.6 = (f32[264,128]{1,0:T(8,128)S(1)}, f32[264,128]{1,0:T(8,128)S(1)}, u32[]{:S(2)}, u32[]{:S(2)}) collective-permute-start(f32[264,128]{1,0:T(8,128)S(1)} %get-tuple-element.41.held0), channel_id=1, source_target_pairs={{0,64},{64,0},{128,192},{192,128},{1,65},{65,1},{129,193},{193,129... | collective-permute-start | bytes 405512 | tf_op jit(solution)/shard_map/ppermute | solution.py:250
  53.0 9.8 %collective-permute-start.7 = (f32[264,128]{1,0:T(8,128)S(1)}, f32[264,128]{1,0:T(8,128)S(1)}, u32[]{:S(2)}, u32[]{:S(2)}) collective-permute-start(f32[264,128]{1,0:T(8,128)S(1)} %get-tuple-element.41.held0), channel_id=1, source_target_pairs={{0,128},{64,192},{128,0},{192,64},{1,129},{65,193},{129,1},{193,65... | collective-permute-start | bytes 405512 | tf_op jit(solution)/shard_map/ppermute | solution.py:250
  55.4 9.6 %collective-permute-start.8 = (f32[264,128]{1,0:T(8,128)S(1)}, f32[264,128]{1,0:T(8,128)S(1)}, u32[]{:S(2)}, u32[]{:S(2)}) collective-permute-start(f32[264,128]{1,0:T(8,128)S(1)} %get-tuple-element.41.held0), channel_id=1, source_target_pairs={{0,192},{64,128},{128,64},{192,0},{1,193},{65,129},{129,65},{193,1... | collective-permute-start | bytes 405512 | tf_op jit(solution)/shard_map/ppermute | solution.py:250

commit v3 on v2

--- a/solution.py
+++ b/solution.py
@@ -34,9 +34,8 @@
     cosine, sine = np.cos(angle), np.sin(angle)
     width = PATCH * LOOK_S
     looks = (np.arange(width)[:, None] // LOOK_S == np.arange(128)[None, :]).astype(jnp.bfloat16)
-    rows = np.concatenate([cosine, sine], 0) / (LOOK_L * LOOK_S * PATCH)
-    rows = np.repeat(rows, LOOK_L, axis=1)
-    fwd = halves(rows)
+    head, rest = halves(np.concatenate([cosine, sine], 0) / (LOOK_L * LOOK_S * PATCH))
+    fwd3 = np.concatenate([head, head, rest], 1)
     eye = np.eye(4)
     cols = np.concatenate([np.kron(eye, cosine), np.kron(eye, sine)], 1)
     head, rest = halves(cols)
@@ -51,19 +50,7 @@
         row == place // 8 * 32 + turn * 16 + place % 8 * 2 + side for turn in range(ROUNDS) for side in range(2)
     ]
     pick = np.concatenate(pick, 1).astype(jnp.bfloat16)
-    return looks, fwd, cols3, back3, group, pick
-
-
-def forward_table(head, rest):
-    pieces, offsets, first, at = [], [], 0, 0
-    for step in CHUNKS:
-        span = slice(first, first + step)
-        piece = np.concatenate([head[:, span], head[:, span], rest[:, span]], axis=1)
-        piece = np.pad(piece, ((0, 0), (0, -piece.shape[1] % 128)))
-        pieces.append(piece)
-        offsets.append(at)
-        first, at = first + step, at + piece.shape[1]
-    return np.concatenate(pieces, axis=1), offsets
+    return looks, fwd3, cols3, back3, group, pick
 
 
 def split(x):
@@ -75,7 +62,7 @@
     return jnp.dot(a, b, preferred_element_type=jnp.float32)
 
 
-def forward_chunk(offset, me_ref, match_ref, own, near, far, looks_ref, fwd_ref, prior, pieces):
+def look_sums(me_ref, match_ref, own, near, far, looks_ref, products):
     lines = own.shape[2]
     me = me_ref[0]
     one, three = me ^ 1, me ^ 3
@@ -87,32 +74,29 @@
             (near, j, far, match_ref[1, one * ACQ_DEV + j]),
             (far, j, near, match_ref[1, three * ACQ_DEV + j]),
         )
+        here = products.at[j % 2]
         for s, (left, i, right, m) in enumerate(pairs):
             a_re = left[i, 0].astype(jnp.float32)
             a_im = left[i, 1].astype(jnp.float32)
             b_re = right[m, 0].astype(jnp.float32)
             b_im = right[m, 1].astype(jnp.float32)
-            re = split(a_re * b_re + a_im * b_im)
-            im = split(a_im * b_re - a_re * b_im)
-            for h in range(2):
-                pieces[j, h, 0, s] = re[h]
-                pieces[j, h, 1, s] = im[h]
-        width = own.shape[3]
-        summed = dot(pieces[j].reshape(2 * 2 * SETS * lines, width), looks_ref[...])
-        half = 2 * SETS * lines
-        summed = summed[:half] + summed[half:]
+            re = a_re * b_re + a_im * b_im
+            im = a_im * b_re - a_re * b_im
+            for c in range(here.shape[0]):
+                here[c, s * lines : (s + 1) * lines] = re[:, c * 128 : (c + 1) * 128]
+                here[c, (SETS + s) * lines : (SETS + s + 1) * lines] = im[:, c * 128 : (c + 1) * 128]
+        rows = 2 * SETS * lines // LOOK_L
+        looked = []
+        for c in range(here.shape[0]):
+            x = [here.at[c][pl.ds(i, rows, stride=LOOK_L), :] for i in range(LOOK_L)]
+            looked.append((x[0] + x[1]) + (x[2] + x[3]))
+        head, rest = split(jnp.concatenate(looked, axis=1))
+        summed = dot(jnp.concatenate([head, rest], axis=0), looks_ref[...])
+        summed = summed[:rows] + summed[rows:]
         if j:
             summed = pltpu.roll(summed, PATCH * j, 1)
         total = summed if total is None else total + summed
-    wide = jnp.concatenate([total[n * lines : (n + 1) * lines] for n in range(2 * SETS)], axis=1)
-    head, rest = split(wide)
-    both = dot(fwd_ref[:, offset : offset + 3 * lines], jnp.concatenate([head, rest, head], axis=0))
-    half = SETS * 128
-    re = both[:PATCH, :half] + both[PATCH:, half:]
-    im = both[:PATCH, half:] - both[PATCH:, :half]
-    if prior is not None:
-        re, im = re + prior[0], im + prior[1]
-    return re, im
+    return total
 
 
 def along_columns(re, im, cols_ref, sign):
@@ -125,39 +109,57 @@
     )
 
 
-def looks_kernel(offset, me_ref, match_ref, own, near, far, looks_ref, fwd_ref, *rest):
-    prior, out, pieces = rest if len(rest) == 3 else (None, *rest)
-    re, im = forward_chunk(offset, me_ref, match_ref, own, near, far, looks_ref, fwd_ref, prior, pieces)
-    out[0] = re
-    out[1] = im
-
-
-def spectrum_kernel(
-    offset, me_ref, match_ref, own, near, far, looks_ref, fwd_ref, prior, cols_ref, group_ref, code, spec, energy, pieces
-):
-    re, im = forward_chunk(offset, me_ref, match_ref, own, near, far, looks_ref, fwd_ref, prior, pieces)
-    re, im = (
-        jnp.concatenate([x[:, s * 128 : (s + 1) * 128] for s in range(SETS)], axis=0) for x in (re, im)
-    )
+def looks_kernel(me_ref, match_ref, own, near, far, looks_ref, *rest):
+    before, out, products = rest if len(rest) == 3 else (None, *rest)
+    looked = look_sums(me_ref, match_ref, own, near, far, looks_ref, products)
+    done = 0
+    if before is not None:
+        done = before.shape[1]
+        out[:, :done] = before[...]
+    out[:, done:] = looked.reshape(out.shape[0], -1, 128)
+
+
+def spectrum_kernel(me_ref, match_ref, own, near, far, looks_ref, before, code, fwd_ref, cols_ref, spec, energy, products):
+    looked = look_sums(me_ref, match_ref, own, near, far, looks_ref, products)
+    n = looked.shape[0]
+    rows = n // (2 * SETS)
+    sums = []
+    for s in range(SETS):
+        power = None
+        for part in range(2):
+            at = part * SETS + s
+            for x in (before[at], looked[at * rows : (at + 1) * rows]):
+                mean = x * (1.0 / (LOOK_L * LOOK_S))
+                mean = jnp.sum(mean * mean, axis=0, keepdims=True)
+                power = mean if power is None else power + mean
+        sums.append(power)
+    sums = jnp.concatenate(sums + [jnp.zeros((8 - SETS, 128), jnp.float32)], axis=0)
+    place = lax.broadcasted_iota(jnp.int32, (8, 128), 1) & (PATCH - 1)
+    sums = (sums + pltpu.roll(sums, 120, 1)) + (pltpu.roll(sums, 112, 1) + pltpu.roll(sums, 104, 1))
+    sums = jnp.where(place < 8, sums, 0.0)
+    mine = sums
+    for s in range(1, SETS):
+        mine = mine + pltpu.roll(pltpu.roll(sums, 8 - s, 0), 8 * s, 1)
+    mine = mine[:1]
+    energy[...] = jnp.broadcast_to(mine, energy.shape)
+
+    wide = [
+        jnp.concatenate([before[at], looked[at * rows : (at + 1) * rows]], axis=0) for at in range(2 * SETS)
+    ]
+    head, rest = split(jnp.concatenate(wide, axis=1))
+    both = dot(fwd_ref[...], jnp.concatenate([head, rest, head], axis=0))
+    half = SETS * 128
+    re = both[:PATCH, :half] + both[PATCH:, half:]
+    im = both[:PATCH, half:] - both[PATCH:, :half]
+    re, im = (jnp.concatenate([x[:, s * 128 : (s + 1) * 128] for s in range(SETS)], axis=0) for x in (re, im))
     re, im = along_columns(re, im, cols_ref, -1.0)
     half = SETS * PATCH
     spec[:half] = re
     spec[half : 2 * half] = im
-    power = re * re + im * im
-    sums = jnp.concatenate(
-        [jnp.sum(power[s * PATCH : (s + 1) * PATCH], axis=0, keepdims=True) for s in range(SETS)]
-        + [jnp.zeros((8 - SETS, 128), jnp.float32)],
-        axis=0,
-    )
-    sums = jnp.dot(sums, group_ref[...], precision=lax.Precision.HIGHEST, preferred_element_type=jnp.float32)
-    lane = lax.broadcasted_iota(jnp.int32, (8, 128), 1) & (PATCH - 1)
-    row = lax.broadcasted_iota(jnp.int32, (8, 128), 0)
-    mine = jnp.sum(jnp.where(lane == row, sums, 0.0), axis=0, keepdims=True)
     spec[2 * half :] = jnp.broadcast_to(code[...], (8, 128))
-    energy[...] = jnp.broadcast_to(mine, energy.shape)
-
-
-def finish_kernel(grid_count, me_ref, held0, held1, held2, held3, parts, cols_ref, back_ref, group_ref, pick_ref, out, values):
+
+
+def finish_kernel(grid_count, me_ref, held0, held1, held2, held3, parts, cols_ref, back_ref, group_ref, pick_ref, out, values, woven):
     held = (held0, held1, held2, held3)
     n = len(held)
     me = me_ref[0]
@@ -172,10 +174,10 @@
     row = lax.broadcasted_iota(jnp.int32, (8, 128), 0)
     spread = []
     for k in range(n):
-        other = jnp.where(place < 2, shares[k ^ 1], shares[k ^ 2])
+        other = jnp.where(place < 16, shares[k ^ 1], shares[k ^ 2])
         other = jnp.broadcast_to(other, (8, 128))
-        other = jnp.where(lane & 1 == 0, pltpu.roll(other, 127, 1), pltpu.roll(other, 1, 1))
-        spread.append(jnp.where(place == row, shares[k] + other, 0.0))
+        other = jnp.where(lane & 8 == 0, pltpu.roll(other, 120, 1), pltpu.roll(other, 8, 1))
+        spread.append(jnp.where(place // 8 == row, shares[k] + other, 0.0))
     spread = jnp.concatenate(spread, axis=0)
     spread = jnp.dot(spread, group_ref[...], precision=lax.Precision.HIGHEST, preferred_element_type=jnp.float32)
     scale = spread * (1.0 / grid_count) + energy_eps
@@ -187,7 +189,7 @@
             re = held[k][s * PATCH : (s + 1) * PATCH]
             im = held[k][half + s * PATCH : half + (s + 1) * PATCH]
             power = (re * re + im * im) * inverse[8 * k + s : 8 * k + s + 1]
-            weight = jnp.sqrt(jnp.sqrt(power + power_floor))
+            weight = lax.rsqrt(lax.rsqrt(power + power_floor))
             res.append(weight * re)
             ims.append(weight * im)
     re, im = along_columns(jnp.concatenate(res, axis=0), jnp.concatenate(ims, axis=0), cols_ref, 1.0)
@@ -238,7 +240,9 @@
     choice = lax.broadcasted_iota(jnp.int32, (n_slots, chosen.shape[1]), 0) == chosen
     choice = jnp.where(choice, 1.0, 0.0).astype(jnp.bfloat16)
     result = dot(choice, values[...])
-    out[...] = result.astype(jnp.bfloat16)
+    for part in range(2):
+        woven[pl.ds(part, n_slots, stride=2), :] = result[:, part * 128 : (part + 1) * 128]
+    out[...] = woven[...].astype(jnp.bfloat16)
 
 
 VMEM = pl.BlockSpec(memory_space=pltpu.VMEM)
@@ -270,7 +274,7 @@
     me = lax.axis_index("acq").astype(jnp.int32)
     me_arr = me.reshape(1)
     column = 1 - ((me ^ (me >> 1)) & 1)
-    looks, (fwd_head, fwd_rest), cols3, back3, group, pick = tables()
+    looks, fwd3, cols3, back3, group, pick = tables()
     width = samples_dev // 2
 
     chunks = []
@@ -290,16 +294,15 @@
 
     code = slot_codes(dest, coherent)
 
-    forward, offsets = forward_table(fwd_head, fwd_rest)
-    prior = None
+    before = None
     for n, (first, own, near, far) in enumerate(chunks):
         step = own.shape[2]
-        scratch = [pltpu.VMEM((ACQ_DEV, 2, 2, SETS, step, width), jnp.bfloat16)]
-        args = [me_arr, match, own, near, far, looks, forward] + ([] if prior is None else [prior])
+        scratch = [pltpu.VMEM((2, width // 128, 2 * SETS * step, 128), jnp.float32)]
+        args = [me_arr, match, own, near, far, looks] + ([] if before is None else [before])
         if n < len(chunks) - 1:
-            prior = pl.pallas_call(
-                functools.partial(looks_kernel, offsets[n]),
-                out_shape=jax.ShapeDtypeStruct((2, PATCH, SETS * 128), jnp.float32),
+            before = pl.pallas_call(
+                looks_kernel,
+                out_shape=jax.ShapeDtypeStruct((2 * SETS, (first + step) // LOOK_L, 128), jnp.float32),
                 in_specs=[SMEM, SMEM] + [VMEM] * (len(args) - 2),
                 out_specs=VMEM,
                 scratch_shapes=scratch,
@@ -308,7 +311,7 @@
             )(*args)
         else:
             spec, energy = pl.pallas_call(
-                functools.partial(spectrum_kernel, offsets[n]),
+                spectrum_kernel,
                 out_shape=(
                     jax.ShapeDtypeStruct((2 * SETS * PATCH + 8, 128), jnp.float32),
                     jax.ShapeDtypeStruct((n_acq * n_tile, 128), jnp.float32),
@@ -318,16 +321,19 @@
                 scratch_shapes=scratch,
                 compiler_params=PARAMS,
                 name="spectrum",
-            )(*args, cols3, group, code)
+            )(*args, code, fwd3, cols3)
 
     parts = lax.all_to_all(energy, ("acq", "tile"), split_axis=0, concat_axis=0, tiled=True)
     held = [spec] + [swapped(spec, bits) for bits in range(1, n_acq)]
     out = pl.pallas_call(
         functools.partial(finish_kernel, float(grid_count)),
-        out_shape=jax.ShapeDtypeStruct((n_acq * CAP, 256), jnp.bfloat16),
+        out_shape=jax.ShapeDtypeStruct((2 * n_acq * CAP, 128), jnp.bfloat16),
         in_specs=[SMEM] + [VMEM] * 9,
         out_specs=VMEM,
-        scratch_shapes=[pltpu.VMEM((n_acq * SETS * 32, 256), jnp.bfloat16)],
+        scratch_shapes=[
+            pltpu.VMEM((n_acq * SETS * 32, 256), jnp.bfloat16),
+            pltpu.VMEM((2 * n_acq * CAP, 128), jnp.float32),
+        ],
         compiler_params=PARAMS,
         name="goldstein",
     )(me_arr, *held, parts, cols3, back3, group, pick)

time: 67.6 us -> 67 us (level)
  waiting for transfers between devices: 23.1 us -> 20.8 us
  other arithmetic: 6.05 us -> 7.38 us
  matrix products: 0.15 us -> 0.89 us
    ppermute x9, waiting for transfers between devices: 23.1 us -> 20.8 us  [swapped(): lax.ppermute(x, 'acq', [(i, i ^ bits) for i in range(lax.axis_size('acq'))])]
    pallas_call x3, Pallas kernels: 8.07 us -> 6.78 us  [the longest x2 4.26 us: shards(): pl.pallas_call(looks_kernel, out_shape=jax.ShapeDtypeStruct((2 * SETS, (f...]
    dot_general x1, matrix products: 0.15 us -> 0.89 us  [slot_codes(): jnp.dot(onehot.astype(jnp.bfloat16), before, preferred_element_type=jnp.f...]
    reshape x1 -> x0, local copies, waits for them, and re-layouts: 0.69 us -> none  [shards(): return out.reshape(1, n_acq * CAP, 2, 128)]
    optimization_barrier x1, other arithmetic: 0.67 us -> 1.35 us  [shards(): lax.optimization_barrier((own, other, slc, dest, coherent))]
    unnamed x22 -> x20, local copies, waits for them, and re-layouts: 1.75 us -> 1.74 us
  transfers between devices with their start and end apart: 10 -> 10, of which waited for: 7 -> 7; matrix products, arithmetic and copies ran while one was open for 9% -> 13% of each run, Pallas kernels for 7% -> 6%
where the time goes in v3:
time: 67 us; the launch traced here: 66.7 us
  starting transfers between devices  24.9 us (37%)
  waiting for transfers between devices  20.8 us (31%)
  Pallas kernels  9.09 us (14%)
  other arithmetic  7.38 us (11%)
  local copies, waits for them, and re-layouts  3.6 us (5%)
  matrix products  0.89 us (1%)
    ppermute x9, waiting for transfers between devices, swapped(): lax.ppermute(x, 'acq', [(i, i ^ bits) for i in range(lax.axis_size('acq'))])  20.8 us
    all_to_all x1, starting transfers between devices, shards(): lax.all_to_all(energy, ('acq', 'tile'), split_axis=0, concat_axis=0, tile...  14.5 us
    ppermute x9, starting transfers between devices, swapped(): lax.ppermute(x, 'acq', [(i, i ^ bits) for i in range(lax.axis_size('acq'))])  10.5 us
    select_n x3, other arithmetic, shards(): other = jnp.where(column == 0, right, left)  5.36 us
    pallas_call x2, Pallas kernels, shards(): pl.pallas_call(looks_kernel, out_shape=jax.ShapeDtypeStruct((2 * SETS, (f...  4.26 us
    pallas_call x1, Pallas kernels, shards(): pl.pallas_call(spectrum_kernel, out_shape=(jax.ShapeDtypeStruct((2 * SETS...  2.52 us
    pallas_call x1, Pallas kernels, shards(): pl.pallas_call(functools.partial(finish_kernel, float(grid_count)), out_s...  2.3 us
    unnamed x20, local copies, waits for them, and re-layouts  1.74 us
  transfers between devices with their start and end apart: 10, of which 7 were waited for; matrix products, arithmetic and copies ran while one was open for 13% of the time, Pallas kernels for 6%

profile of v3, /device:TPU:1, one launch (start us, length us, event | category | flops | bytes accessed | tf_op | source)
XLA Modules:
  0.0 66.7 jit_solution(11816024337169319324)
XLA Ops:
  0.0 0.0 copy-start.9
  0.0 0.0 copy-start
  0.0 0.0 copy-start.8
  0.0 1.2 %broadcast_select_fusion.4 = (bf16[4,2,32,640]{3,2,1,0:T(8,128)(2,1)S(1)}, bf16[4,2,32,640]{3,2,1,0:T(8,128)(2,1)S(1)}) fusion(pred[]{:T(512)S(6)} %eq.10, bf16[4,2,128,1280]{3,2,1,0:T(8,128)(2,1)} %param.10), kind=kLoop, calls=%fused_computation.6 | loop fusion | flops 327680 | bytes 1310721 | tf_op jit(solution)/shard_map/jit(_where)/select_n | solution.py:290
  1.2 3.4 %collective-permute-start.1 = (bf16[4,2,32,640]{3,2,1,0:T(8,128)(2,1)S(1)}, bf16[4,2,32,640]{3,2,1,0:T(8,128)(2,1)S(1)}, u32[]{:S(2)}, u32[]{:S(2)}) collective-permute-start(bf16[4,2,32,640]{3,2,1,0:T(8,128)(2,1)S(1)} %get-tuple-element.29.own), channel_id=1, source_target_pairs={{0,192},{64,128},{128,64},{192,0},{1,193},{65,129},{129,65},{193,1... | collective-permute-start | bytes 983048 | tf_op jit(solution)/shard_map/ppermute | solution.py:254
  4.6 0.0 collective-permute-start
  4.6 2.3 %broadcast_select_fusion = (bf16[4,2,64,640]{3,2,1,0:T(8,128)(2,1)}, bf16[4,2,64,640]{3,2,1,0:T(8,128)(2,1)S(1)}) fusion(pred[]{:T(512)S(6)} %eq.10, bf16[4,2,128,1280]{3,2,1,0:T(8,128)(2,1)} %param.10), kind=kLoop, calls=%fused_computation.2 | loop fusion | flops 655360 | bytes 2621441 | tf_op jit(solution)/shard_map/jit(_where)/select_n | solution.py:290
  6.9 0.0 copy-start.1
  6.9 0.0 copy-start.7
  6.9 1.5 %collective-permute-start.4 = (bf16[4,2,64,640]{3,2,1,0:T(8,128)(2,1)}, bf16[4,2,64,640]{3,2,1,0:T(8,128)(2,1)S(1)}, u32[]{:S(2)}, u32[]{:S(2)}) collective-permute-start(bf16[4,2,64,640]{3,2,1,0:T(8,128)(2,1)} %get-tuple-element.36), channel_id=1, source_target_pairs={{0,64},{64,0},{128,192},{192,128},{1,65},{65,1},{129,193},{193,129... | collective-permute-start | bytes 1966088 | tf_op jit(solution)/shard_map/ppermute | solution.py:254
  8.3 0.1 collective-permute-start.5
  8.4 2.5 %collective-permute-done.1.far = bf16[4,2,32,640]{3,2,1,0:T(8,128)(2,1)S(1)} collective-permute-done((bf16[4,2,32,640]{3,2,1,0:T(8,128)(2,1)S(1)}, bf16[4,2,32,640]{3,2,1,0:T(8,128)(2,1)S(1)}, u32[]{:S(2)}, u32[]{:S(2)}) %collective-permute-start.1) | collective-permute-done | bytes 327712 | tf_op jit(solution)/shard_map/ppermute | solution.py:254
  11.0 1.9 %collective-permute-done.near = bf16[4,2,32,640]{3,2,1,0:T(8,128)(2,1)S(1)} collective-permute-done((bf16[4,2,32,640]{3,2,1,0:T(8,128)(2,1)S(1)}, bf16[4,2,32,640]{3,2,1,0:T(8,128)(2,1)S(1)}, u32[]{:S(2)}, u32[]{:S(2)}) %collective-permute-start) | collective-permute-done | bytes 327712 | tf_op jit(solution)/shard_map/ppermute | solution.py:254
  12.9 0.0 copy-start.2
  12.9 0.7 %copy-done.2 = bf16[4,2,32,640]{3,2,1,0:T(8,128)(2,1)} copy-done((bf16[4,2,32,640]{3,2,1,0:T(8,128)(2,1)}, bf16[4,2,32,640]{3,2,1,0:T(8,128)(2,1)S(1)}, u32[]{:S(2)}) %copy-start.2) | copy-done | bytes 327704
  13.6 0.0 copy-start.4
  13.6 0.0 copy-start.5
  13.6 1.9 %broadcast_select_fusion.2 = (bf16[4,2,32,640]{3,2,1,0:T(8,128)(2,1)}, bf16[4,2,32,640]{3,2,1,0:T(8,128)(2,1)S(1)}) fusion(pred[]{:T(512)S(6)} %eq.10, bf16[4,2,128,1280]{3,2,1,0:T(8,128)(2,1)} %param.10), kind=kLoop, calls=%fused_computation.4 | loop fusion | flops 327680 | bytes 1310721 | tf_op jit(solution)/shard_map/jit(_where)/select_n | solution.py:290
  15.5 0.0 copy-start.6
  15.5 0.5 broadcast.36
  16.0 1.3 %fusion.4 = (s32[4,32]{1,0:T(4,128)S(1)}, s32[4,32]{1,0:T(4,128)S(1)}) fusion(s32[1,4,32,1]{2,3,1,0:T(1,128)} %param.12, s32[]{:T(128)} %broadcast.36), kind=kLoop, calls=%fused_computation.17 | loop fusion | flops 128 | bytes 1540 | tf_op jit(solution)/shard_map/optimization_barrier | solution.py:291
  17.4 0.7 eq.11
  18.0 0.1 mul.21
  18.1 0.0 copy-done.9
  18.1 0.6 gt.18
  18.7 0.1 collective-permute-start.2
  18.8 1.5 %collective-permute-start.3 = (bf16[4,2,32,640]{3,2,1,0:T(8,128)(2,1)S(1)}, bf16[4,2,32,640]{3,2,1,0:T(8,128)(2,1)S(1)}, u32[]{:S(2)}, u32[]{:S(2)}) collective-permute-start(bf16[4,2,32,640]{3,2,1,0:T(8,128)(2,1)S(1)} %get-tuple-element.33.own), channel_id=1, source_target_pairs={{0,192},{64,128},{128,64},{192,0},{1,193},{65,129},{129,65},{193,1... | collective-permute-start | bytes 983048 | tf_op jit(solution)/shard_map/ppermute | solution.py:254
  20.3 0.0 copy-done
  20.3 0.0 copy-done.8
  20.3 0.0 copy-start.3
  20.3 1.0 %copy-done.3 = bf16[4,2,32,640]{3,2,1,0:T(8,128)(2,1)S(1)} copy-done((bf16[4,2,32,640]{3,2,1,0:T(8,128)(2,1)S(1)}, bf16[4,2,32,640]{3,2,1,0:T(8,128)(2,1)}, u32[]{:S(2)}) %copy-start.3) | copy-done | bytes 327704
  21.2 1.7 %looks.2.rest_0_ = f32[8,8,128]{2,1,0:T(8,128)S(1)} custom-call(s32[1]{0:T(128)} %bitcast.me_ref, s32[2,16]{1,0:T(2,128)S(1)} %copy-done.8, bf16[4,2,32,640]{3,2,1,0:T(8,128)(2,1)S(1)} %get-tuple-element.29.own, bf16[4,2,32,640]{3,2,1,0:T(8,128)(2,1)S(1)} %copy-done.3, bf16[4,2,32,640]{3,2,1,0:T(8,128)(2,1)S(1)} %collective-permute-done.1.far, ...), custom_call_target="tpu_custom_call" | custom-call | tf_op jit(solution)/shard_map/looks/pallas_call | solution.py:303
  22.9 0.9 %fusion = f32[128]{0:T(128)S(1)} fusion(s32[128]{0:T(128)} %eq.11), kind=kOutput, calls=%fused_computation.1 | convolution fusion | flops 150400 | bytes 1024 | tf_op jit(solution)/shard_map/dot_general | solution.py:263
  23.8 0.7 fusion.3.code
  24.5 2.4 %collective-permute-done.4.near = bf16[4,2,64,640]{3,2,1,0:T(8,128)(2,1)S(1)} collective-permute-done((bf16[4,2,64,640]{3,2,1,0:T(8,128)(2,1)}, bf16[4,2,64,640]{3,2,1,0:T(8,128)(2,1)S(1)}, u32[]{:S(2)}, u32[]{:S(2)}) %collective-permute-start.4) | collective-permute-done | bytes 655392 | tf_op jit(solution)/shard_map/ppermute | solution.py:254
  26.9 0.0 collective-permute-done.5.far
  26.9 2.6 %looks.3.before = f32[8,24,128]{2,1,0:T(8,128)S(1)} custom-call(s32[1]{0:T(128)} %bitcast.me_ref, s32[2,16]{1,0:T(2,128)S(1)} %copy-done.8, bf16[4,2,64,640]{3,2,1,0:T(8,128)(2,1)S(1)} %get-tuple-element.35.own, bf16[4,2,64,640]{3,2,1,0:T(8,128)(2,1)S(1)} %collective-permute-done.4.near, bf16[4,2,64,640]{3,2,1,0:T(8,128)(2,1)S(1)} %collective-permute-done.5.far, ...), custom_call_target="tpu_custom_call" | custom-call | tf_op jit(solution)/shard_map/looks/pallas_call | solution.py:303
  29.5 4.4 %collective-permute-done.2.near = bf16[4,2,32,640]{3,2,1,0:T(8,128)(2,1)S(1)} collective-permute-done((bf16[4,2,32,640]{3,2,1,0:T(8,128)(2,1)}, bf16[4,2,32,640]{3,2,1,0:T(8,128)(2,1)S(1)}, u32[]{:S(2)}, u32[]{:S(2)}) %collective-permute-start.2) | collective-permute-done | bytes 327712 | tf_op jit(solution)/shard_map/ppermute | solution.py:254
  33.9 0.0 collective-permute-done.3.far
  33.9 0.0 copy-done.1
  33.9 0.0 copy-done.7
  33.9 2.5 %spectrum.1 = (f32[264,128]{1,0:T(8,128)S(1)}, f32[256,128]{1,0:T(8,128)}) custom-call(s32[1]{0:T(128)} %bitcast.me_ref, s32[2,16]{1,0:T(2,128)S(1)} %copy-done.8, bf16[4,2,32,640]{3,2,1,0:T(8,128)(2,1)S(1)} %get-tuple-element.33.own, bf16[4,2,32,640]{3,2,1,0:T(8,128)(2,1)S(1)} %collective-permute-done.2.near, ...), custom_call_target="tpu_custom_call" | custom-call | tf_op jit(solution)/shard_map/spectrum/pallas_call | solution.py:313
  36.5 14.5 %all-to-all-start = ((f32[256,1,128]{2,1,0:T(1,128)}), f32[256,1,128]{2,1,0:T(1,128)S(1)}, u32[]{:S(2)}, u32[]{:S(2)}) async-start(f32[256,1,128]{2,1,0:T(1,128)} %bitcast.3), calls=%async_computation | async-start | bytes 262144 | tf_op jit(solution)/shard_map/all_to_all | solution.py:326
  50.9 1.5 %collective-permute-start.6 = (f32[264,128]{1,0:T(8,128)S(1)}, f32[264,128]{1,0:T(8,128)S(1)}, u32[]{:S(2)}, u32[]{:S(2)}) collective-permute-start(f32[264,128]{1,0:T(8,128)S(1)} %get-tuple-element.41.held0), channel_id=1, source_target_pairs={{0,64},{64,0},{128,192},{192,128},{1,65},{65,1},{129,193},{193,129... | collective-permute-start | bytes 405512 | tf_op jit(solution)/shard_map/ppermute | solution.py:254
  52.4 2.4 %collective-permute-start.7 = (f32[264,128]{1,0:T(8,128)S(1)}, f32[264,128]{1,0:T(8,128)S(1)}, u32[]{:S(2)}, u32[]{:S(2)}) collective-permute-start(f32[264,128]{1,0:T(8,128)S(1)} %get-tuple-element.41.held0), channel_id=1, source_target_pairs={{0,128},{64,192},{128,0},{192,64},{1,129},{65,193},{129,1},{193,65... | collective-permute-start | bytes 405512 | tf_op jit(solution)/shard_map/ppermute | solution.py:254
  54.8 0.1 collective-permute-start.8
  54.9 0.5 collective-permute-done.6.held1
  55.4 6.8 %collective-permute-done.7.held2 = f32[264,128]{1,0:T(8,128)S(1)} collective-permute-done((f32[264,128]{1,0:T(8,128)S(1)}, f32[264,128]{1,0:T(8,128)S(1)}, u32[]{:S(2)}, u32[]{:S(2)}) %collective-permute-start.7) | collective-permute-done | bytes 135200 | tf_op jit(solution)/shard_map/ppermute | solution.py:254
  62.3 2.1 %collective-permute-done.8.held3 = f32[264,128]{1,0:T(8,128)S(1)} collective-permute-done((f32[264,128]{1,0:T(8,128)S(1)}, f32[264,128]{1,0:T(8,128)S(1)}, u32[]{:S(2)}, u32[]{:S(2)}) %collective-permute-start.8) | collective-permute-done | bytes 135200 | tf_op jit(solution)/shard_map/ppermute | solution.py:254
  64.4 0.0 all-to-all-done
  64.4 0.0 copy-done.4
  64.4 0.0 copy-done.5
  64.4 0.0 copy-done.6
  64.4 2.3 %goldstein.1 = bf16[512,128]{1,0:T(8,128)(2,1)} custom-call(s32[1]{0:T(128)} %bitcast.me_ref, f32[264,128]{1,0:T(8,128)S(1)} %get-tuple-element.41.held0, f32[264,128]{1,0:T(8,128)S(1)} %collective-permute-done.6.held1, f32[264,128]{1,0:T(8,128)S(1)} %collective-permute-done.7.held2, f32[264,128]{1,0:T(8,128)S(1)} %collective-permute-done.8.held3, ...), custom_call_target="tpu_custom_call" | custom-call | tf_op jit(solution)/shard_map/goldstein/pallas_call | solution.py:328
  (1 shorter events, 0.0 us)
Async XLA Ops:
  0.0 18.1 %copy-start.9 = (s32[1,4,32]{2,1,0:T(4,128)S(1)}, s32[1,4,32]{2,1,0:T(4,128)}, u32[]{:S(2)}) copy-start(s32[1,4,32]{2,1,0:T(4,128)} %param.13) | copy-start | bytes 1540
  0.0 20.3 %copy-start = (bf16[640,128]{1,0:T(8,128)(2,1)S(1)}, bf16[640,128]{1,0:T(8,128)(2,1)}, u32[]{:S(2)}) copy-start(bf16[640,128]{1,0:T(8,128)(2,1)} %constant.30.clone.looks_ref) | copy-start | bytes 491524
  0.0 20.3 %copy-start.8 = (s32[2,16]{1,0:T(2,128)S(1)}, s32[2,16]{1,0:T(2,128)}, u32[]{:S(2)}) copy-start(s32[2,16]{1,0:T(2,128)} %match_ref.5) | copy-start | bytes 388
  1.2 9.8 %collective-permute-start.1 = (bf16[4,2,32,640]{3,2,1,0:T(8,128)(2,1)S(1)}, bf16[4,2,32,640]{3,2,1,0:T(8,128)(2,1)S(1)}, u32[]{:S(2)}, u32[]{:S(2)}) collective-permute-start(bf16[4,2,32,640]{3,2,1,0:T(8,128)(2,1)S(1)} %get-tuple-element.29.own), channel_id=1, source_target_pairs={{0,192},{64,128},{128,64},{192,0},{1,193},{65,129},{129,65},{193,1... | collective-permute-start | bytes 983048 | tf_op jit(solution)/shard_map/ppermute | solution.py:254
  4.6 8.3 %collective-permute-start = (bf16[4,2,32,640]{3,2,1,0:T(8,128)(2,1)S(1)}, bf16[4,2,32,640]{3,2,1,0:T(8,128)(2,1)S(1)}, u32[]{:S(2)}, u32[]{:S(2)}) collective-permute-start(bf16[4,2,32,640]{3,2,1,0:T(8,128)(2,1)S(1)} %get-tuple-element.28), channel_id=1, source_target_pairs={{0,64},{64,0},{128,192},{192,128},{1,65},{65,1},{129,193},{193,129... | collective-permute-start | bytes 983048 | tf_op jit(solution)/shard_map/ppermute | solution.py:254
  6.9 27.1 %copy-start.1 = (bf16[384,256]{1,0:T(8,128)(2,1)S(1)}, bf16[384,256]{1,0:T(8,128)(2,1)}, u32[]{:S(2)}) copy-start(bf16[384,256]{1,0:T(8,128)(2,1)} %constant.32.clone.cols_ref) | copy-start | bytes 589828
  6.9 27.1 %copy-start.7 = (bf16[64,96]{1,0:T(8,128)(2,1)S(1)}, bf16[64,96]{1,0:T(8,128)(2,1)}, u32[]{:S(2)}) copy-start(bf16[64,96]{1,0:T(8,128)(2,1)} %constant.31.clone.fwd_ref) | copy-start | bytes 36868
  6.9 20.0 %collective-permute-start.4 = (bf16[4,2,64,640]{3,2,1,0:T(8,128)(2,1)}, bf16[4,2,64,640]{3,2,1,0:T(8,128)(2,1)S(1)}, u32[]{:S(2)}, u32[]{:S(2)}) collective-permute-start(bf16[4,2,64,640]{3,2,1,0:T(8,128)(2,1)} %get-tuple-element.36), channel_id=1, source_target_pairs={{0,64},{64,0},{128,192},{192,128},{1,65},{65,1},{129,193},{193,129... | collective-permute-start | bytes 1966088 | tf_op jit(solution)/shard_map/ppermute | solution.py:254
  8.3 18.6 %collective-permute-start.5 = (bf16[4,2,64,640]{3,2,1,0:T(8,128)(2,1)S(1)}, bf16[4,2,64,640]{3,2,1,0:T(8,128)(2,1)S(1)}, u32[]{:S(2)}, u32[]{:S(2)}) collective-permute-start(bf16[4,2,64,640]{3,2,1,0:T(8,128)(2,1)S(1)} %get-tuple-element.35.own), channel_id=1, source_target_pairs={{0,192},{64,128},{128,64},{192,0},{1,193},{65,129},{129,65},{193,1... | collective-permute-start | bytes 1966088 | tf_op jit(solution)/shard_map/ppermute | solution.py:254
  12.9 0.7 %copy-start.2 = (bf16[4,2,32,640]{3,2,1,0:T(8,128)(2,1)}, bf16[4,2,32,640]{3,2,1,0:T(8,128)(2,1)S(1)}, u32[]{:S(2)}) copy-start(bf16[4,2,32,640]{3,2,1,0:T(8,128)(2,1)S(1)} %collective-permute-done.near) | copy-start | bytes 983044
  13.6 50.8 %copy-start.4 = (bf16[128,512]{1,0:T(8,128)(2,1)S(1)}, bf16[128,512]{1,0:T(8,128)(2,1)}, u32[]{:S(2)}) copy-start(bf16[128,512]{1,0:T(8,128)(2,1)} %constant.35.clone.pick_ref) | copy-start | bytes 393220
  13.6 50.8 %copy-start.5 = (f32[128,128]{1,0:T(8,128)S(1)}, f32[128,128]{1,0:T(8,128)}, u32[]{:S(2)}) copy-start(f32[128,128]{1,0:T(8,128)} %constant.34.clone.group_ref) | copy-start | bytes 196612
  15.5 48.9 %copy-start.6 = (bf16[64,96]{1,0:T(8,128)(2,1)S(1)}, bf16[64,96]{1,0:T(8,128)(2,1)}, u32[]{:S(2)}) copy-start(bf16[64,96]{1,0:T(8,128)(2,1)} %constant.33.clone.back_ref) | copy-start | bytes 36868
  18.7 15.2 %collective-permute-start.2 = (bf16[4,2,32,640]{3,2,1,0:T(8,128)(2,1)}, bf16[4,2,32,640]{3,2,1,0:T(8,128)(2,1)S(1)}, u32[]{:S(2)}, u32[]{:S(2)}) collective-permute-start(bf16[4,2,32,640]{3,2,1,0:T(8,128)(2,1)} %get-tuple-element.34), channel_id=1, source_target_pairs={{0,64},{64,0},{128,192},{192,128},{1,65},{65,1},{129,193},{193,129... | collective-permute-start | bytes 983048 | tf_op jit(solution)/shard_map/ppermute | solution.py:254
  18.8 15.1 %collective-permute-start.3 = (bf16[4,2,32,640]{3,2,1,0:T(8,128)(2,1)S(1)}, bf16[4,2,32,640]{3,2,1,0:T(8,128)(2,1)S(1)}, u32[]{:S(2)}, u32[]{:S(2)}) collective-permute-start(bf16[4,2,32,640]{3,2,1,0:T(8,128)(2,1)S(1)} %get-tuple-element.33.own), channel_id=1, source_target_pairs={{0,192},{64,128},{128,64},{192,0},{1,193},{65,129},{129,65},{193,1... | collective-permute-start | bytes 983048 | tf_op jit(solution)/shard_map/ppermute | solution.py:254
  20.3 1.0 %copy-start.3 = (bf16[4,2,32,640]{3,2,1,0:T(8,128)(2,1)S(1)}, bf16[4,2,32,640]{3,2,1,0:T(8,128)(2,1)}, u32[]{:S(2)}) copy-start(bf16[4,2,32,640]{3,2,1,0:T(8,128)(2,1)} %copy-done.2) | copy-start | bytes 983044
  36.5 27.9 %all-to-all-start = ((f32[256,1,128]{2,1,0:T(1,128)}), f32[256,1,128]{2,1,0:T(1,128)S(1)}, u32[]{:S(2)}, u32[]{:S(2)}) async-start(f32[256,1,128]{2,1,0:T(1,128)} %bitcast.3), calls=%async_computation | async-start | bytes 262144 | tf_op jit(solution)/shard_map/all_to_all | solution.py:326
  50.9 4.5 %collective-permute-start.6 = (f32[264,128]{1,0:T(8,128)S(1)}, f32[264,128]{1,0:T(8,128)S(1)}, u32[]{:S(2)}, u32[]{:S(2)}) collective-permute-start(f32[264,128]{1,0:T(8,128)S(1)} %get-tuple-element.41.held0), channel_id=1, source_target_pairs={{0,64},{64,0},{128,192},{192,128},{1,65},{65,1},{129,193},{193,129... | collective-permute-start | bytes 405512 | tf_op jit(solution)/shard_map/ppermute | solution.py:254
  52.4 9.8 %collective-permute-start.7 = (f32[264,128]{1,0:T(8,128)S(1)}, f32[264,128]{1,0:T(8,128)S(1)}, u32[]{:S(2)}, u32[]{:S(2)}) collective-permute-start(f32[264,128]{1,0:T(8,128)S(1)} %get-tuple-element.41.held0), channel_id=1, source_target_pairs={{0,128},{64,192},{128,0},{192,64},{1,129},{65,193},{129,1},{193,65... | collective-permute-start | bytes 405512 | tf_op jit(solution)/shard_map/ppermute | solution.py:254
  54.8 9.6 %collective-permute-start.8 = (f32[264,128]{1,0:T(8,128)S(1)}, f32[264,128]{1,0:T(8,128)S(1)}, u32[]{:S(2)}, u32[]{:S(2)}) collective-permute-start(f32[264,128]{1,0:T(8,128)S(1)} %get-tuple-element.41.held0), channel_id=1, source_target_pairs={{0,192},{64,128},{128,64},{192,0},{1,193},{65,129},{129,65},{193,1... | collective-permute-start | bytes 405512 | tf_op jit(solution)/shard_map/ppermute | solution.py:254

commit v4 on v3

--- a/solution.py
+++ b/solution.py
@@ -62,9 +62,9 @@
     return jnp.dot(a, b, preferred_element_type=jnp.float32)
 
 
-def look_sums(me_ref, match_ref, own, near, far, looks_ref, products):
+def look_sums(match_ref, own, near, far, looks_ref, products):
     lines = own.shape[2]
-    me = me_ref[0]
+    me = lax.axis_index("acq")
     one, three = me ^ 1, me ^ 3
     total = None
     for j in range(ACQ_DEV):
@@ -109,9 +109,9 @@
     )
 
 
-def looks_kernel(me_ref, match_ref, own, near, far, looks_ref, *rest):
+def looks_kernel(match_ref, own, near, far, looks_ref, *rest):
     before, out, products = rest if len(rest) == 3 else (None, *rest)
-    looked = look_sums(me_ref, match_ref, own, near, far, looks_ref, products)
+    looked = look_sums(match_ref, own, near, far, looks_ref, products)
     done = 0
     if before is not None:
         done = before.shape[1]
@@ -119,8 +119,8 @@
     out[:, done:] = looked.reshape(out.shape[0], -1, 128)
 
 
-def spectrum_kernel(me_ref, match_ref, own, near, far, looks_ref, before, code, fwd_ref, cols_ref, spec, energy, products):
-    looked = look_sums(me_ref, match_ref, own, near, far, looks_ref, products)
+def spectrum_kernel(match_ref, own, near, far, looks_ref, before, code, fwd_ref, cols_ref, spec, energy, products):
+    looked = look_sums(match_ref, own, near, far, looks_ref, products)
     n = looked.shape[0]
     rows = n // (2 * SETS)
     sums = []
@@ -159,16 +159,16 @@
     spec[2 * half :] = jnp.broadcast_to(code[...], (8, 128))
 
 
-def finish_kernel(grid_count, me_ref, held0, held1, held2, held3, parts, cols_ref, back_ref, group_ref, pick_ref, out, values, woven):
+def finish_kernel(grid_count, held0, held1, held2, held3, parts, cols_ref, back_ref, group_ref, pick_ref, out, values, woven):
     held = (held0, held1, held2, held3)
     n = len(held)
-    me = me_ref[0]
+    me = lax.axis_index("acq")
     half = SETS * PATCH
     lane = lax.broadcasted_iota(jnp.int32, (1, 128), 1)
     place = lane & (PATCH - 1)
     n_tile = parts.shape[0] // n
     shares = [
-        jnp.sum(parts[pl.ds(pl.multiple_of((me ^ k) * n_tile, 8), n_tile), :], axis=0, keepdims=True)
+        jnp.sum(parts[pl.ds(me ^ k, n_tile, stride=n), :], axis=0, keepdims=True)
         for k in range(n)
     ]
     row = lax.broadcasted_iota(jnp.int32, (8, 128), 0)
@@ -272,7 +272,6 @@
     n_tile = lax.axis_size("tile")
     grid_count = lines_dev * n_tile // LOOK_L * (samples_dev // LOOK_S)
     me = lax.axis_index("acq").astype(jnp.int32)
-    me_arr = me.reshape(1)
     column = 1 - ((me ^ (me >> 1)) & 1)
     looks, fwd3, cols3, back3, group, pick = tables()
     width = samples_dev // 2
@@ -298,12 +297,12 @@
     for n, (first, own, near, far) in enumerate(chunks):
         step = own.shape[2]
         scratch = [pltpu.VMEM((2, width // 128, 2 * SETS * step, 128), jnp.float32)]
-        args = [me_arr, match, own, near, far, looks] + ([] if before is None else [before])
+        args = [match, own, near, far, looks] + ([] if before is None else [before])
         if n < len(chunks) - 1:
             before = pl.pallas_call(
                 looks_kernel,
                 out_shape=jax.ShapeDtypeStruct((2 * SETS, (first + step) // LOOK_L, 128), jnp.float32),
-                in_specs=[SMEM, SMEM] + [VMEM] * (len(args) - 2),
+                in_specs=[SMEM] + [VMEM] * (len(args) - 1),
                 out_specs=VMEM,
                 scratch_shapes=scratch,
                 compiler_params=PARAMS,
@@ -316,19 +315,19 @@
                     jax.ShapeDtypeStruct((2 * SETS * PATCH + 8, 128), jnp.float32),
                     jax.ShapeDtypeStruct((n_acq * n_tile, 128), jnp.float32),
                 ),
-                in_specs=[SMEM, SMEM] + [VMEM] * (len(args) + 1),
+                in_specs=[SMEM] + [VMEM] * (len(args) + 2),
                 out_specs=(VMEM, VMEM),
                 scratch_shapes=scratch,
                 compiler_params=PARAMS,
                 name="spectrum",
             )(*args, code, fwd3, cols3)
 
-    parts = lax.all_to_all(energy, ("acq", "tile"), split_axis=0, concat_axis=0, tiled=True)
+    parts = lax.all_to_all(energy, ("tile", "acq"), split_axis=0, concat_axis=0, tiled=True)
     held = [spec] + [swapped(spec, bits) for bits in range(1, n_acq)]
     out = pl.pallas_call(
         functools.partial(finish_kernel, float(grid_count)),
         out_shape=jax.ShapeDtypeStruct((2 * n_acq * CAP, 128), jnp.bfloat16),
-        in_specs=[SMEM] + [VMEM] * 9,
+        in_specs=[VMEM] * 9,
         out_specs=VMEM,
         scratch_shapes=[
             pltpu.VMEM((n_acq * SETS * 32, 256), jnp.bfloat16),
@@ -336,7 +335,7 @@
         ],
         compiler_params=PARAMS,
         name="goldstein",
-    )(me_arr, *held, parts, cols3, back3, group, pick)
+    )(*held, parts, cols3, back3, group, pick)
     return out.reshape(1, n_acq * CAP, 2, 128)
 
 

time: 67 us -> 66.8 us (level)
  starting transfers between devices: 24.9 us -> 25.9 us
  waiting for transfers between devices: 20.8 us -> 21.6 us
  matrix products: 0.89 us -> 0.15 us
    all_to_all x1, waiting for transfers between devices: 0.01 us -> 3.09 us  [shards(): lax.all_to_all(energy, ('tile', 'acq'), split_axis=0, concat_axis=0, tile...]
    ppermute x9, waiting for transfers between devices: 20.8 us -> 18.5 us  [swapped(): lax.ppermute(x, 'acq', [(i, i ^ bits) for i in range(lax.axis_size('acq'))])]
    all_to_all x1, starting transfers between devices: 14.5 us -> 15.4 us  [shards(): lax.all_to_all(energy, ('tile', 'acq'), split_axis=0, concat_axis=0, tile...]
    dot_general x1, matrix products: 0.89 us -> 0.15 us  [slot_codes(): jnp.dot(onehot.astype(jnp.bfloat16), before, preferred_element_type=jnp.f...]
    optimization_barrier x1, other arithmetic: 1.35 us -> 0.65 us  [shards(): lax.optimization_barrier((own, other, slc, dest, coherent))]
    unnamed x20 -> x22, local copies, waits for them, and re-layouts: 1.74 us -> 1.75 us
  transfers between devices with their start and end apart: 10 -> 10, of which waited for: 7 -> 9; matrix products, arithmetic and copies ran while one was open for 13% -> 10% of each run, Pallas kernels for 6% -> 6%
where the time goes in v4:
time: 66.8 us; the launch traced here: 66.6 us
  starting transfers between devices  25.9 us (39%)
  waiting for transfers between devices  21.6 us (32%)
  Pallas kernels  9.08 us (14%)
  other arithmetic  6.72 us (10%)
  local copies, waits for them, and re-layouts  3.08 us (5%)
    ppermute x9, waiting for transfers between devices, swapped(): lax.ppermute(x, 'acq', [(i, i ^ bits) for i in range(lax.axis_size('acq'))])  18.5 us
    all_to_all x1, starting transfers between devices, shards(): lax.all_to_all(energy, ('tile', 'acq'), split_axis=0, concat_axis=0, tile...  15.4 us
    ppermute x9, starting transfers between devices, swapped(): lax.ppermute(x, 'acq', [(i, i ^ bits) for i in range(lax.axis_size('acq'))])  10.5 us
    select_n x3, other arithmetic, shards(): other = jnp.where(column == 0, right, left)  5.39 us
    pallas_call x2, Pallas kernels, shards(): pl.pallas_call(looks_kernel, out_shape=jax.ShapeDtypeStruct((2 * SETS, (f...  4.24 us
    all_to_all x1, waiting for transfers between devices, shards(): lax.all_to_all(energy, ('tile', 'acq'), split_axis=0, concat_axis=0, tile...  3.09 us
    pallas_call x1, Pallas kernels, shards(): pl.pallas_call(spectrum_kernel, out_shape=(jax.ShapeDtypeStruct((2 * SETS...  2.52 us
    pallas_call x1, Pallas kernels, shards(): pl.pallas_call(functools.partial(finish_kernel, float(grid_count)), out_s...  2.32 us
  transfers between devices with their start and end apart: 10, of which 9 were waited for; matrix products, arithmetic and copies ran while one was open for 10% of the time, Pallas kernels for 6%

profile of v4, /device:TPU:1, one launch (start us, length us, event | category | flops | bytes accessed | tf_op | source)
XLA Modules:
  0.0 66.6 jit_solution(8334043659141184696)
XLA Ops:
  0.0 0.0 copy-start.9
  0.0 0.0 copy-start.10
  0.0 0.0 copy-start
  0.0 0.0 copy-start.8
  0.0 1.2 %broadcast_select_fusion.4 = (bf16[4,2,32,640]{3,2,1,0:T(8,128)(2,1)S(1)}, bf16[4,2,32,640]{3,2,1,0:T(8,128)(2,1)S(1)}) fusion(pred[]{:T(512)S(6)} %eq.10, bf16[4,2,128,1280]{3,2,1,0:T(8,128)(2,1)} %param.10), kind=kLoop, calls=%fused_computation.6 | loop fusion | flops 327680 | bytes 1310721 | tf_op jit(solution)/shard_map/jit(_where)/select_n | solution.py:289
  1.2 2.1 %collective-permute-start = (bf16[4,2,32,640]{3,2,1,0:T(8,128)(2,1)S(1)}, bf16[4,2,32,640]{3,2,1,0:T(8,128)(2,1)S(1)}, u32[]{:S(2)}, u32[]{:S(2)}) collective-permute-start(bf16[4,2,32,640]{3,2,1,0:T(8,128)(2,1)S(1)} %get-tuple-element.28), channel_id=1, source_target_pairs={{0,64},{64,0},{128,192},{192,128},{1,65},{65,1},{129,193},{193,129... | collective-permute-start | bytes 983048 | tf_op jit(solution)/shard_map/ppermute | solution.py:254
  3.4 1.8 %collective-permute-start.1 = (bf16[4,2,32,640]{3,2,1,0:T(8,128)(2,1)S(1)}, bf16[4,2,32,640]{3,2,1,0:T(8,128)(2,1)S(1)}, u32[]{:S(2)}, u32[]{:S(2)}) collective-permute-start(bf16[4,2,32,640]{3,2,1,0:T(8,128)(2,1)S(1)} %get-tuple-element.29.own), channel_id=1, source_target_pairs={{0,192},{64,128},{128,64},{192,0},{1,193},{65,129},{129,65},{193,1... | collective-permute-start | bytes 983048 | tf_op jit(solution)/shard_map/ppermute | solution.py:254
  5.2 2.3 %broadcast_select_fusion = (bf16[4,2,64,640]{3,2,1,0:T(8,128)(2,1)}, bf16[4,2,64,640]{3,2,1,0:T(8,128)(2,1)S(1)}) fusion(pred[]{:T(512)S(6)} %eq.10, bf16[4,2,128,1280]{3,2,1,0:T(8,128)(2,1)} %param.10), kind=kLoop, calls=%fused_computation.2 | loop fusion | flops 655360 | bytes 2621441 | tf_op jit(solution)/shard_map/jit(_where)/select_n | solution.py:289
  7.4 0.0 copy-start.1
  7.4 0.0 copy-start.7
  7.4 0.3 collective-permute-start.4
  7.8 0.6 collective-permute-start.5
  8.4 1.1 %collective-permute-done.near = bf16[4,2,32,640]{3,2,1,0:T(8,128)(2,1)S(1)} collective-permute-done((bf16[4,2,32,640]{3,2,1,0:T(8,128)(2,1)S(1)}, bf16[4,2,32,640]{3,2,1,0:T(8,128)(2,1)S(1)}, u32[]{:S(2)}, u32[]{:S(2)}) %collective-permute-start) | collective-permute-done | bytes 327712 | tf_op jit(solution)/shard_map/ppermute | solution.py:254
  9.5 3.0 %collective-permute-done.1.far = bf16[4,2,32,640]{3,2,1,0:T(8,128)(2,1)S(1)} collective-permute-done((bf16[4,2,32,640]{3,2,1,0:T(8,128)(2,1)S(1)}, bf16[4,2,32,640]{3,2,1,0:T(8,128)(2,1)S(1)}, u32[]{:S(2)}, u32[]{:S(2)}) %collective-permute-start.1) | collective-permute-done | bytes 327712 | tf_op jit(solution)/shard_map/ppermute | solution.py:254
  12.5 0.0 copy-start.2
  12.5 0.7 %copy-done.2 = bf16[4,2,32,640]{3,2,1,0:T(8,128)(2,1)} copy-done((bf16[4,2,32,640]{3,2,1,0:T(8,128)(2,1)}, bf16[4,2,32,640]{3,2,1,0:T(8,128)(2,1)S(1)}, u32[]{:S(2)}) %copy-start.2) | copy-done | bytes 327704
  13.2 0.0 copy-start.4
  13.3 0.0 copy-start.5
  13.3 1.9 %broadcast_select_fusion.2 = (bf16[4,2,32,640]{3,2,1,0:T(8,128)(2,1)}, bf16[4,2,32,640]{3,2,1,0:T(8,128)(2,1)S(1)}) fusion(pred[]{:T(512)S(6)} %eq.10, bf16[4,2,128,1280]{3,2,1,0:T(8,128)(2,1)} %param.10), kind=kLoop, calls=%fused_computation.4 | loop fusion | flops 327680 | bytes 1310721 | tf_op jit(solution)/shard_map/jit(_where)/select_n | solution.py:289
  15.2 0.0 copy-start.6
  15.2 0.0 copy-done.9
  15.2 0.6 gt.18
  15.8 0.6 broadcast.36
  16.4 0.0 copy-done.10
  16.4 0.7 fusion.4
  17.0 0.1 eq.11
  17.1 0.1 mul.21
  17.2 0.0 collective-permute-start.2
  17.2 2.2 %collective-permute-start.3 = (bf16[4,2,32,640]{3,2,1,0:T(8,128)(2,1)S(1)}, bf16[4,2,32,640]{3,2,1,0:T(8,128)(2,1)S(1)}, u32[]{:S(2)}, u32[]{:S(2)}) collective-permute-start(bf16[4,2,32,640]{3,2,1,0:T(8,128)(2,1)S(1)} %get-tuple-element.33.own), channel_id=1, source_target_pairs={{0,192},{64,128},{128,64},{192,0},{1,193},{65,129},{129,65},{193,1... | collective-permute-start | bytes 983048 | tf_op jit(solution)/shard_map/ppermute | solution.py:254
  19.4 0.0 copy-done
  19.4 0.0 copy-done.8
  19.4 0.0 copy-start.3
  19.4 1.0 %copy-done.3 = bf16[4,2,32,640]{3,2,1,0:T(8,128)(2,1)S(1)} copy-done((bf16[4,2,32,640]{3,2,1,0:T(8,128)(2,1)S(1)}, bf16[4,2,32,640]{3,2,1,0:T(8,128)(2,1)}, u32[]{:S(2)}) %copy-start.3) | copy-done | bytes 327704
  20.4 1.6 %looks.2.rest_0_ = f32[8,8,128]{2,1,0:T(8,128)S(1)} custom-call(s32[2,16]{1,0:T(2,128)S(1)} %copy-done.8, bf16[4,2,32,640]{3,2,1,0:T(8,128)(2,1)S(1)} %get-tuple-element.29.own, bf16[4,2,32,640]{3,2,1,0:T(8,128)(2,1)S(1)} %collective-permute-done.near, bf16[4,2,32,640]{3,2,1,0:T(8,128)(2,1)S(1)} %copy-done.3, bf16[640,128]{1,0:T(8,128)(2,1)S(1)} %copy-done), custom_call_target="tpu_custom_call" | custom-call | tf_op jit(solution)/shard_map/looks/pallas_call | solution.py:302
  22.1 0.1 fusion
  22.2 0.7 %fusion.3.code = f32[1,128]{1,0:T(1,128)S(1)} fusion(pred[1,128]{1,0:T(4,128)(4,1)} %gt.18, s32[1,128]{1,0:T(1,128)S(1)} %mul.21, f32[128]{0:T(128)S(1)} %fusion), kind=kLoop, calls=%fused_computation.16 | loop fusion | flops 512 | bytes 1664 | tf_op jit(solution)/shard_map/convert_element_type | solution.py:266
  22.9 1.6 %collective-permute-done.4.near = bf16[4,2,64,640]{3,2,1,0:T(8,128)(2,1)S(1)} collective-permute-done((bf16[4,2,64,640]{3,2,1,0:T(8,128)(2,1)}, bf16[4,2,64,640]{3,2,1,0:T(8,128)(2,1)S(1)}, u32[]{:S(2)}, u32[]{:S(2)}) %collective-permute-start.4) | collective-permute-done | bytes 655392 | tf_op jit(solution)/shard_map/ppermute | solution.py:254
  24.5 2.1 %collective-permute-done.5.far = bf16[4,2,64,640]{3,2,1,0:T(8,128)(2,1)S(1)} collective-permute-done((bf16[4,2,64,640]{3,2,1,0:T(8,128)(2,1)S(1)}, bf16[4,2,64,640]{3,2,1,0:T(8,128)(2,1)S(1)}, u32[]{:S(2)}, u32[]{:S(2)}) %collective-permute-start.5) | collective-permute-done | bytes 655392 | tf_op jit(solution)/shard_map/ppermute | solution.py:254
  26.6 2.6 %looks.3.before = f32[8,24,128]{2,1,0:T(8,128)S(1)} custom-call(s32[2,16]{1,0:T(2,128)S(1)} %copy-done.8, bf16[4,2,64,640]{3,2,1,0:T(8,128)(2,1)S(1)} %get-tuple-element.35.own, bf16[4,2,64,640]{3,2,1,0:T(8,128)(2,1)S(1)} %collective-permute-done.4.near, bf16[4,2,64,640]{3,2,1,0:T(8,128)(2,1)S(1)} %collective-permute-done.5.far, ...), custom_call_target="tpu_custom_call" | custom-call | tf_op jit(solution)/shard_map/looks/pallas_call | solution.py:302
  29.2 2.3 %collective-permute-done.2.near = bf16[4,2,32,640]{3,2,1,0:T(8,128)(2,1)S(1)} collective-permute-done((bf16[4,2,32,640]{3,2,1,0:T(8,128)(2,1)}, bf16[4,2,32,640]{3,2,1,0:T(8,128)(2,1)S(1)}, u32[]{:S(2)}, u32[]{:S(2)}) %collective-permute-start.2) | collective-permute-done | bytes 327712 | tf_op jit(solution)/shard_map/ppermute | solution.py:254
  31.5 2.1 %collective-permute-done.3.far = bf16[4,2,32,640]{3,2,1,0:T(8,128)(2,1)S(1)} collective-permute-done((bf16[4,2,32,640]{3,2,1,0:T(8,128)(2,1)S(1)}, bf16[4,2,32,640]{3,2,1,0:T(8,128)(2,1)S(1)}, u32[]{:S(2)}, u32[]{:S(2)}) %collective-permute-start.3) | collective-permute-done | bytes 327712 | tf_op jit(solution)/shard_map/ppermute | solution.py:254
  33.6 0.0 copy-done.1
  33.6 0.0 copy-done.7
  33.6 2.5 %spectrum.1 = (f32[264,128]{1,0:T(8,128)S(1)}, f32[256,128]{1,0:T(8,128)}) custom-call(s32[2,16]{1,0:T(2,128)S(1)} %copy-done.8, bf16[4,2,32,640]{3,2,1,0:T(8,128)(2,1)S(1)} %get-tuple-element.33.own, bf16[4,2,32,640]{3,2,1,0:T(8,128)(2,1)S(1)} %collective-permute-done.2.near, bf16[4,2,32,640]{3,2,1,0:T(8,128)(2,1)S(1)} %collective-permute-done.3.far, ...), custom_call_target="tpu_custom_call" | custom-call | tf_op jit(solution)/shard_map/spectrum/pallas_call | solution.py:312
  36.1 15.4 %all-to-all-start = ((f32[256,1,128]{2,1,0:T(1,128)}), f32[256,1,128]{2,1,0:T(1,128)S(1)}, u32[]{:S(2)}, u32[]{:S(2)}) async-start(f32[256,1,128]{2,1,0:T(1,128)} %bitcast.2), calls=%async_computation | async-start | bytes 262144 | tf_op jit(solution)/shard_map/all_to_all | solution.py:325
  51.5 2.7 %collective-permute-start.8 = (f32[264,128]{1,0:T(8,128)S(1)}, f32[264,128]{1,0:T(8,128)S(1)}, u32[]{:S(2)}, u32[]{:S(2)}) collective-permute-start(f32[264,128]{1,0:T(8,128)S(1)} %get-tuple-element.41.held0), channel_id=1, source_target_pairs={{0,192},{64,128},{128,64},{192,0},{1,193},{65,129},{129,65},{193,1... | collective-permute-start | bytes 405512 | tf_op jit(solution)/shard_map/ppermute | solution.py:254
  54.2 0.6 collective-permute-start.7
  54.8 0.1 collective-permute-start.6
  54.9 6.1 %collective-permute-done.8.held3 = f32[264,128]{1,0:T(8,128)S(1)} collective-permute-done((f32[264,128]{1,0:T(8,128)S(1)}, f32[264,128]{1,0:T(8,128)S(1)}, u32[]{:S(2)}, u32[]{:S(2)}) %collective-permute-start.8) | collective-permute-done | bytes 135200 | tf_op jit(solution)/shard_map/ppermute | solution.py:254
  60.9 0.2 collective-permute-done.7.held2
  61.1 0.0 collective-permute-done.6.held1
  61.2 3.1 %all-to-all-done = f32[256,1,128]{2,1,0:T(1,128)S(1)} async-done(((f32[256,1,128]{2,1,0:T(1,128)}), f32[256,1,128]{2,1,0:T(1,128)S(1)}, u32[]{:S(2)}, u32[]{:S(2)}) %all-to-all-start) | async-done | bytes 131104 | tf_op jit(solution)/shard_map/all_to_all | solution.py:325
  64.2 0.0 copy-done.4
  64.2 0.0 copy-done.5
  64.2 0.0 copy-done.6
  64.2 2.3 %goldstein.1 = bf16[512,128]{1,0:T(8,128)(2,1)} custom-call(f32[264,128]{1,0:T(8,128)S(1)} %get-tuple-element.41.held0, f32[264,128]{1,0:T(8,128)S(1)} %collective-permute-done.6.held1, f32[264,128]{1,0:T(8,128)S(1)} %collective-permute-done.7.held2, f32[264,128]{1,0:T(8,128)S(1)} %collective-permute-done.8.held3, f32[256,128]{1,0:T(8,128)S(1)} %bitcast.12, ...), custom_call_target="tpu_custom_call" | custom-call | tf_op jit(solution)/shard_map/goldstein/pallas_call | solution.py:327
  (1 shorter events, 0.0 us)
Async XLA Ops:
  0.0 15.2 %copy-start.9 = (s32[1,4,32]{2,1,0:T(4,128)S(1)}, s32[1,4,32]{2,1,0:T(4,128)}, u32[]{:S(2)}) copy-start(s32[1,4,32]{2,1,0:T(4,128)} %param.13) | copy-start | bytes 1540
  0.0 16.4 %copy-start.10 = (s32[1,4,32,1]{2,3,1,0:T(1,128)S(1)}, s32[1,4,32,1]{2,3,1,0:T(1,128)}, u32[]{:S(2)}) copy-start(s32[1,4,32,1]{2,3,1,0:T(1,128)} %param.12) | copy-start | bytes 1540
  0.0 19.4 %copy-start = (bf16[640,128]{1,0:T(8,128)(2,1)S(1)}, bf16[640,128]{1,0:T(8,128)(2,1)}, u32[]{:S(2)}) copy-start(bf16[640,128]{1,0:T(8,128)(2,1)} %constant.30.clone.looks_ref) | copy-start | bytes 491524
  0.0 19.4 %copy-start.8 = (s32[2,16]{1,0:T(2,128)S(1)}, s32[2,16]{1,0:T(2,128)}, u32[]{:S(2)}) copy-start(s32[2,16]{1,0:T(2,128)} %match_ref.5) | copy-start | bytes 388
  1.2 8.3 %collective-permute-start = (bf16[4,2,32,640]{3,2,1,0:T(8,128)(2,1)S(1)}, bf16[4,2,32,640]{3,2,1,0:T(8,128)(2,1)S(1)}, u32[]{:S(2)}, u32[]{:S(2)}) collective-permute-start(bf16[4,2,32,640]{3,2,1,0:T(8,128)(2,1)S(1)} %get-tuple-element.28), channel_id=1, source_target_pairs={{0,64},{64,0},{128,192},{192,128},{1,65},{65,1},{129,193},{193,129... | collective-permute-start | bytes 983048 | tf_op jit(solution)/shard_map/ppermute | solution.py:254
  3.4 9.1 %collective-permute-start.1 = (bf16[4,2,32,640]{3,2,1,0:T(8,128)(2,1)S(1)}, bf16[4,2,32,640]{3,2,1,0:T(8,128)(2,1)S(1)}, u32[]{:S(2)}, u32[]{:S(2)}) collective-permute-start(bf16[4,2,32,640]{3,2,1,0:T(8,128)(2,1)S(1)} %get-tuple-element.29.own), channel_id=1, source_target_pairs={{0,192},{64,128},{128,64},{192,0},{1,193},{65,129},{129,65},{193,1... | collective-permute-start | bytes 983048 | tf_op jit(solution)/shard_map/ppermute | solution.py:254
  7.4 26.1 %copy-start.1 = (bf16[384,256]{1,0:T(8,128)(2,1)S(1)}, bf16[384,256]{1,0:T(8,128)(2,1)}, u32[]{:S(2)}) copy-start(bf16[384,256]{1,0:T(8,128)(2,1)} %constant.32.clone.cols_ref) | copy-start | bytes 589828
  7.4 26.1 %copy-start.7 = (bf16[64,96]{1,0:T(8,128)(2,1)S(1)}, bf16[64,96]{1,0:T(8,128)(2,1)}, u32[]{:S(2)}) copy-start(bf16[64,96]{1,0:T(8,128)(2,1)} %constant.31.clone.fwd_ref) | copy-start | bytes 36868
  7.4 17.0 %collective-permute-start.4 = (bf16[4,2,64,640]{3,2,1,0:T(8,128)(2,1)}, bf16[4,2,64,640]{3,2,1,0:T(8,128)(2,1)S(1)}, u32[]{:S(2)}, u32[]{:S(2)}) collective-permute-start(bf16[4,2,64,640]{3,2,1,0:T(8,128)(2,1)} %get-tuple-element.36), channel_id=1, source_target_pairs={{0,64},{64,0},{128,192},{192,128},{1,65},{65,1},{129,193},{193,129... | collective-permute-start | bytes 1966088 | tf_op jit(solution)/shard_map/ppermute | solution.py:254
  7.8 18.8 %collective-permute-start.5 = (bf16[4,2,64,640]{3,2,1,0:T(8,128)(2,1)S(1)}, bf16[4,2,64,640]{3,2,1,0:T(8,128)(2,1)S(1)}, u32[]{:S(2)}, u32[]{:S(2)}) collective-permute-start(bf16[4,2,64,640]{3,2,1,0:T(8,128)(2,1)S(1)} %get-tuple-element.35.own), channel_id=1, source_target_pairs={{0,192},{64,128},{128,64},{192,0},{1,193},{65,129},{129,65},{193,1... | collective-permute-start | bytes 1966088 | tf_op jit(solution)/shard_map/ppermute | solution.py:254
  12.5 0.7 %copy-start.2 = (bf16[4,2,32,640]{3,2,1,0:T(8,128)(2,1)}, bf16[4,2,32,640]{3,2,1,0:T(8,128)(2,1)S(1)}, u32[]{:S(2)}) copy-start(bf16[4,2,32,640]{3,2,1,0:T(8,128)(2,1)S(1)} %collective-permute-done.1.far) | copy-start | bytes 983044
  13.2 51.0 %copy-start.4 = (bf16[128,512]{1,0:T(8,128)(2,1)S(1)}, bf16[128,512]{1,0:T(8,128)(2,1)}, u32[]{:S(2)}) copy-start(bf16[128,512]{1,0:T(8,128)(2,1)} %constant.35.clone.pick_ref) | copy-start | bytes 393220
  13.3 51.0 %copy-start.5 = (f32[128,128]{1,0:T(8,128)S(1)}, f32[128,128]{1,0:T(8,128)}, u32[]{:S(2)}) copy-start(f32[128,128]{1,0:T(8,128)} %constant.34.clone.group_ref) | copy-start | bytes 196612
  15.2 49.1 %copy-start.6 = (bf16[64,96]{1,0:T(8,128)(2,1)S(1)}, bf16[64,96]{1,0:T(8,128)(2,1)}, u32[]{:S(2)}) copy-start(bf16[64,96]{1,0:T(8,128)(2,1)} %constant.33.clone.back_ref) | copy-start | bytes 36868
  17.2 14.3 %collective-permute-start.2 = (bf16[4,2,32,640]{3,2,1,0:T(8,128)(2,1)}, bf16[4,2,32,640]{3,2,1,0:T(8,128)(2,1)S(1)}, u32[]{:S(2)}, u32[]{:S(2)}) collective-permute-start(bf16[4,2,32,640]{3,2,1,0:T(8,128)(2,1)} %get-tuple-element.34), channel_id=1, source_target_pairs={{0,64},{64,0},{128,192},{192,128},{1,65},{65,1},{129,193},{193,129... | collective-permute-start | bytes 983048 | tf_op jit(solution)/shard_map/ppermute | solution.py:254
  17.2 16.4 %collective-permute-start.3 = (bf16[4,2,32,640]{3,2,1,0:T(8,128)(2,1)S(1)}, bf16[4,2,32,640]{3,2,1,0:T(8,128)(2,1)S(1)}, u32[]{:S(2)}, u32[]{:S(2)}) collective-permute-start(bf16[4,2,32,640]{3,2,1,0:T(8,128)(2,1)S(1)} %get-tuple-element.33.own), channel_id=1, source_target_pairs={{0,192},{64,128},{128,64},{192,0},{1,193},{65,129},{129,65},{193,1... | collective-permute-start | bytes 983048 | tf_op jit(solution)/shard_map/ppermute | solution.py:254
  19.4 1.0 %copy-start.3 = (bf16[4,2,32,640]{3,2,1,0:T(8,128)(2,1)S(1)}, bf16[4,2,32,640]{3,2,1,0:T(8,128)(2,1)}, u32[]{:S(2)}) copy-start(bf16[4,2,32,640]{3,2,1,0:T(8,128)(2,1)} %copy-done.2) | copy-start | bytes 983044
  36.1 28.1 %all-to-all-start = ((f32[256,1,128]{2,1,0:T(1,128)}), f32[256,1,128]{2,1,0:T(1,128)S(1)}, u32[]{:S(2)}, u32[]{:S(2)}) async-start(f32[256,1,128]{2,1,0:T(1,128)} %bitcast.2), calls=%async_computation | async-start | bytes 262144 | tf_op jit(solution)/shard_map/all_to_all | solution.py:325
  51.5 9.4 %collective-permute-start.8 = (f32[264,128]{1,0:T(8,128)S(1)}, f32[264,128]{1,0:T(8,128)S(1)}, u32[]{:S(2)}, u32[]{:S(2)}) collective-permute-start(f32[264,128]{1,0:T(8,128)S(1)} %get-tuple-element.41.held0), channel_id=1, source_target_pairs={{0,192},{64,128},{128,64},{192,0},{1,193},{65,129},{129,65},{193,1... | collective-permute-start | bytes 405512 | tf_op jit(solution)/shard_map/ppermute | solution.py:254
  54.2 6.9 %collective-permute-start.7 = (f32[264,128]{1,0:T(8,128)S(1)}, f32[264,128]{1,0:T(8,128)S(1)}, u32[]{:S(2)}, u32[]{:S(2)}) collective-permute-start(f32[264,128]{1,0:T(8,128)S(1)} %get-tuple-element.41.held0), channel_id=1, source_target_pairs={{0,128},{64,192},{128,0},{192,64},{1,129},{65,193},{129,1},{193,65... | collective-permute-start | bytes 405512 | tf_op jit(solution)/shard_map/ppermute | solution.py:254
  54.8 6.4 %collective-permute-start.6 = (f32[264,128]{1,0:T(8,128)S(1)}, f32[264,128]{1,0:T(8,128)S(1)}, u32[]{:S(2)}, u32[]{:S(2)}) collective-permute-start(f32[264,128]{1,0:T(8,128)S(1)} %get-tuple-element.41.held0), channel_id=1, source_target_pairs={{0,64},{64,0},{128,192},{192,128},{1,65},{65,1},{129,193},{193,129... | collective-permute-start | bytes 405512 | tf_op jit(solution)/shard_map/ppermute | solution.py:254

commit v5 on v4

--- a/solution.py
+++ b/solution.py
@@ -44,7 +44,7 @@
     back = np.concatenate([cosine[order], sine[order]], 0) / PATCH
     head, rest = halves(back)
     back3 = np.concatenate([head, head, rest], 1)
-    group = np.kron(eye, np.ones((PATCH, PATCH))).astype(np.float32)
+    group = np.kron(eye, np.ones((PATCH, PATCH))).astype(jnp.bfloat16)
     row, place = np.arange(128)[:, None], np.arange(128)[None, :] % 32
     pick = [
         row == place // 8 * 32 + turn * 16 + place % 8 * 2 + side for turn in range(ROUNDS) for side in range(2)
@@ -179,7 +179,9 @@
         other = jnp.where(lane & 8 == 0, pltpu.roll(other, 120, 1), pltpu.roll(other, 8, 1))
         spread.append(jnp.where(place // 8 == row, shares[k] + other, 0.0))
     spread = jnp.concatenate(spread, axis=0)
-    spread = jnp.dot(spread, group_ref[...], precision=lax.Precision.HIGHEST, preferred_element_type=jnp.float32)
+    head, rest = split(spread)
+    spread = dot(jnp.concatenate([head, rest], axis=0), group_ref[...])
+    spread = spread[: 8 * n] + spread[8 * n :]
     scale = spread * (1.0 / grid_count) + energy_eps
     inverse = 1.0 / scale
     root = lax.rsqrt(scale)

time: 66.8 us -> 66.7 us (level)
  waiting for transfers between devices: 21.6 us -> 22.8 us
    ppermute x9, waiting for transfers between devices: 18.5 us -> 19.7 us  [swapped(): lax.ppermute(x, 'acq', [(i, i ^ bits) for i in range(lax.axis_size('acq'))])]
  transfers between devices with their start and end apart: 10 -> 10, of which waited for: 9 -> 9; matrix products, arithmetic and copies ran while one was open for 10% -> 9% of each run, Pallas kernels for 6% -> 6%
where the time goes in v5:
time: 66.7 us; the launch traced here: 66.5 us
  starting transfers between devices  25.9 us (39%)
  waiting for transfers between devices  22.8 us (34%)
  Pallas kernels  8.97 us (13%)
  other arithmetic  6.07 us (9%)
  local copies, waits for them, and re-layouts  2.51 us (4%)
    ppermute x9, waiting for transfers between devices, swapped(): lax.ppermute(x, 'acq', [(i, i ^ bits) for i in range(lax.axis_size('acq'))])  19.7 us
    all_to_all x1, starting transfers between devices, shards(): lax.all_to_all(energy, ('tile', 'acq'), split_axis=0, concat_axis=0, tile...  15.4 us
    ppermute x9, starting transfers between devices, swapped(): lax.ppermute(x, 'acq', [(i, i ^ bits) for i in range(lax.axis_size('acq'))])  10.5 us
    select_n x3, other arithmetic, shards(): other = jnp.where(column == 0, right, left)  5.39 us
    pallas_call x2, Pallas kernels, shards(): pl.pallas_call(looks_kernel, out_shape=jax.ShapeDtypeStruct((2 * SETS, (f...  4.24 us
    all_to_all x1, waiting for transfers between devices, shards(): lax.all_to_all(energy, ('tile', 'acq'), split_axis=0, concat_axis=0, tile...  3.09 us
    pallas_call x1, Pallas kernels, shards(): pl.pallas_call(spectrum_kernel, out_shape=(jax.ShapeDtypeStruct((2 * SETS...  2.52 us
    pallas_call x1, Pallas kernels, shards(): pl.pallas_call(functools.partial(finish_kernel, float(grid_count)), out_s...  2.21 us
  transfers between devices with their start and end apart: 10, of which 9 were waited for; matrix products, arithmetic and copies ran while one was open for 9% of the time, Pallas kernels for 6%

profile of v5, /device:TPU:1, one launch (start us, length us, event | category | flops | bytes accessed | tf_op | source)
XLA Modules:
  0.0 66.5 jit_solution(5977916480986544592)
XLA Ops:
  0.0 0.0 copy-start.9
  0.0 0.0 copy-start.10
  0.0 0.0 copy-start
  0.0 0.0 copy-start.8
  0.0 1.2 %broadcast_select_fusion.4 = (bf16[4,2,32,640]{3,2,1,0:T(8,128)(2,1)S(1)}, bf16[4,2,32,640]{3,2,1,0:T(8,128)(2,1)S(1)}) fusion(pred[]{:T(512)S(6)} %eq.10, bf16[4,2,128,1280]{3,2,1,0:T(8,128)(2,1)} %param.10), kind=kLoop, calls=%fused_computation.6 | loop fusion | flops 327680 | bytes 1310721 | tf_op jit(solution)/shard_map/jit(_where)/select_n | solution.py:291
  1.2 2.1 %collective-permute-start = (bf16[4,2,32,640]{3,2,1,0:T(8,128)(2,1)S(1)}, bf16[4,2,32,640]{3,2,1,0:T(8,128)(2,1)S(1)}, u32[]{:S(2)}, u32[]{:S(2)}) collective-permute-start(bf16[4,2,32,640]{3,2,1,0:T(8,128)(2,1)S(1)} %get-tuple-element.28), channel_id=1, source_target_pairs={{0,64},{64,0},{128,192},{192,128},{1,65},{65,1},{129,193},{193,129... | collective-permute-start | bytes 983048 | tf_op jit(solution)/shard_map/ppermute | solution.py:256
  3.4 1.8 %collective-permute-start.1 = (bf16[4,2,32,640]{3,2,1,0:T(8,128)(2,1)S(1)}, bf16[4,2,32,640]{3,2,1,0:T(8,128)(2,1)S(1)}, u32[]{:S(2)}, u32[]{:S(2)}) collective-permute-start(bf16[4,2,32,640]{3,2,1,0:T(8,128)(2,1)S(1)} %get-tuple-element.29.own), channel_id=1, source_target_pairs={{0,192},{64,128},{128,64},{192,0},{1,193},{65,129},{129,65},{193,1... | collective-permute-start | bytes 983048 | tf_op jit(solution)/shard_map/ppermute | solution.py:256
  5.2 2.3 %broadcast_select_fusion = (bf16[4,2,64,640]{3,2,1,0:T(8,128)(2,1)}, bf16[4,2,64,640]{3,2,1,0:T(8,128)(2,1)S(1)}) fusion(pred[]{:T(512)S(6)} %eq.10, bf16[4,2,128,1280]{3,2,1,0:T(8,128)(2,1)} %param.10), kind=kLoop, calls=%fused_computation.2 | loop fusion | flops 655360 | bytes 2621441 | tf_op jit(solution)/shard_map/jit(_where)/select_n | solution.py:291
  7.4 0.0 copy-start.1
  7.4 0.0 copy-start.7
  7.4 0.3 collective-permute-start.4
  7.8 0.6 collective-permute-start.5
  8.4 1.1 %collective-permute-done.near = bf16[4,2,32,640]{3,2,1,0:T(8,128)(2,1)S(1)} collective-permute-done((bf16[4,2,32,640]{3,2,1,0:T(8,128)(2,1)S(1)}, bf16[4,2,32,640]{3,2,1,0:T(8,128)(2,1)S(1)}, u32[]{:S(2)}, u32[]{:S(2)}) %collective-permute-start) | collective-permute-done | bytes 327712 | tf_op jit(solution)/shard_map/ppermute | solution.py:256
  9.5 3.0 %collective-permute-done.1.far = bf16[4,2,32,640]{3,2,1,0:T(8,128)(2,1)S(1)} collective-permute-done((bf16[4,2,32,640]{3,2,1,0:T(8,128)(2,1)S(1)}, bf16[4,2,32,640]{3,2,1,0:T(8,128)(2,1)S(1)}, u32[]{:S(2)}, u32[]{:S(2)}) %collective-permute-start.1) | collective-permute-done | bytes 327712 | tf_op jit(solution)/shard_map/ppermute | solution.py:256
  12.5 0.0 copy-start.2
  12.5 0.7 %copy-done.2 = bf16[4,2,32,640]{3,2,1,0:T(8,128)(2,1)} copy-done((bf16[4,2,32,640]{3,2,1,0:T(8,128)(2,1)}, bf16[4,2,32,640]{3,2,1,0:T(8,128)(2,1)S(1)}, u32[]{:S(2)}) %copy-start.2) | copy-done | bytes 327704
  13.2 0.0 copy-start.4
  13.3 0.0 copy-start.5
  13.3 1.9 %broadcast_select_fusion.2 = (bf16[4,2,32,640]{3,2,1,0:T(8,128)(2,1)}, bf16[4,2,32,640]{3,2,1,0:T(8,128)(2,1)S(1)}) fusion(pred[]{:T(512)S(6)} %eq.10, bf16[4,2,128,1280]{3,2,1,0:T(8,128)(2,1)} %param.10), kind=kLoop, calls=%fused_computation.4 | loop fusion | flops 327680 | bytes 1310721 | tf_op jit(solution)/shard_map/jit(_where)/select_n | solution.py:291
  15.2 0.0 copy-start.6
  15.2 0.0 copy-done.9
  15.2 0.1 gt.18
  15.3 0.5 broadcast.36
  15.8 0.0 copy-done.10
  15.8 0.7 %fusion.4 = (s32[4,32]{1,0:T(4,128)S(1)}, s32[4,32]{1,0:T(4,128)S(1)}) fusion(s32[1,4,32,1]{2,3,1,0:T(1,128)S(1)} %copy-done.10, s32[]{:T(128)} %broadcast.36), kind=kLoop, calls=%fused_computation.17 | loop fusion | flops 128 | bytes 1540 | tf_op jit(solution)/shard_map/optimization_barrier | solution.py:292
  16.5 0.1 eq.11
  16.5 0.1 mul.21
  16.6 0.0 collective-permute-start.2
  16.6 2.2 %collective-permute-start.3 = (bf16[4,2,32,640]{3,2,1,0:T(8,128)(2,1)S(1)}, bf16[4,2,32,640]{3,2,1,0:T(8,128)(2,1)S(1)}, u32[]{:S(2)}, u32[]{:S(2)}) collective-permute-start(bf16[4,2,32,640]{3,2,1,0:T(8,128)(2,1)S(1)} %get-tuple-element.33.own), channel_id=1, source_target_pairs={{0,192},{64,128},{128,64},{192,0},{1,193},{65,129},{129,65},{193,1... | collective-permute-start | bytes 983048 | tf_op jit(solution)/shard_map/ppermute | solution.py:256
  18.9 0.0 copy-done
  18.9 0.0 copy-done.8
  18.9 0.0 copy-start.3
  18.9 1.0 %copy-done.3 = bf16[4,2,32,640]{3,2,1,0:T(8,128)(2,1)S(1)} copy-done((bf16[4,2,32,640]{3,2,1,0:T(8,128)(2,1)S(1)}, bf16[4,2,32,640]{3,2,1,0:T(8,128)(2,1)}, u32[]{:S(2)}) %copy-start.3) | copy-done | bytes 327704
  19.9 1.6 %looks.2.rest_0_ = f32[8,8,128]{2,1,0:T(8,128)S(1)} custom-call(s32[2,16]{1,0:T(2,128)S(1)} %copy-done.8, bf16[4,2,32,640]{3,2,1,0:T(8,128)(2,1)S(1)} %get-tuple-element.29.own, bf16[4,2,32,640]{3,2,1,0:T(8,128)(2,1)S(1)} %collective-permute-done.near, bf16[4,2,32,640]{3,2,1,0:T(8,128)(2,1)S(1)} %copy-done.3, bf16[640,128]{1,0:T(8,128)(2,1)S(1)} %copy-done), custom_call_target="tpu_custom_call" | custom-call | tf_op jit(solution)/shard_map/looks/pallas_call | solution.py:304
  21.5 0.1 fusion
  21.7 2.8 %collective-permute-done.4.near = bf16[4,2,64,640]{3,2,1,0:T(8,128)(2,1)S(1)} collective-permute-done((bf16[4,2,64,640]{3,2,1,0:T(8,128)(2,1)}, bf16[4,2,64,640]{3,2,1,0:T(8,128)(2,1)S(1)}, u32[]{:S(2)}, u32[]{:S(2)}) %collective-permute-start.4) | collective-permute-done | bytes 655392 | tf_op jit(solution)/shard_map/ppermute | solution.py:256
  24.5 2.1 %collective-permute-done.5.far = bf16[4,2,64,640]{3,2,1,0:T(8,128)(2,1)S(1)} collective-permute-done((bf16[4,2,64,640]{3,2,1,0:T(8,128)(2,1)S(1)}, bf16[4,2,64,640]{3,2,1,0:T(8,128)(2,1)S(1)}, u32[]{:S(2)}, u32[]{:S(2)}) %collective-permute-start.5) | collective-permute-done | bytes 655392 | tf_op jit(solution)/shard_map/ppermute | solution.py:256
  26.6 2.6 %looks.3.before = f32[8,24,128]{2,1,0:T(8,128)S(1)} custom-call(s32[2,16]{1,0:T(2,128)S(1)} %copy-done.8, bf16[4,2,64,640]{3,2,1,0:T(8,128)(2,1)S(1)} %get-tuple-element.35.own, bf16[4,2,64,640]{3,2,1,0:T(8,128)(2,1)S(1)} %collective-permute-done.4.near, bf16[4,2,64,640]{3,2,1,0:T(8,128)(2,1)S(1)} %collective-permute-done.5.far, ...), custom_call_target="tpu_custom_call" | custom-call | tf_op jit(solution)/shard_map/looks/pallas_call | solution.py:304
  29.2 2.3 %collective-permute-done.2.near = bf16[4,2,32,640]{3,2,1,0:T(8,128)(2,1)S(1)} collective-permute-done((bf16[4,2,32,640]{3,2,1,0:T(8,128)(2,1)}, bf16[4,2,32,640]{3,2,1,0:T(8,128)(2,1)S(1)}, u32[]{:S(2)}, u32[]{:S(2)}) %collective-permute-start.2) | collective-permute-done | bytes 327712 | tf_op jit(solution)/shard_map/ppermute | solution.py:256
  31.5 2.1 %collective-permute-done.3.far = bf16[4,2,32,640]{3,2,1,0:T(8,128)(2,1)S(1)} collective-permute-done((bf16[4,2,32,640]{3,2,1,0:T(8,128)(2,1)S(1)}, bf16[4,2,32,640]{3,2,1,0:T(8,128)(2,1)S(1)}, u32[]{:S(2)}, u32[]{:S(2)}) %collective-permute-start.3) | collective-permute-done | bytes 327712 | tf_op jit(solution)/shard_map/ppermute | solution.py:256
  33.6 0.0 copy-done.1
  33.6 0.0 copy-done.7
  33.6 2.5 %spectrum.1 = (f32[264,128]{1,0:T(8,128)S(1)}, f32[256,128]{1,0:T(8,128)}) custom-call(s32[2,16]{1,0:T(2,128)S(1)} %copy-done.8, bf16[4,2,32,640]{3,2,1,0:T(8,128)(2,1)S(1)} %get-tuple-element.33.own, bf16[4,2,32,640]{3,2,1,0:T(8,128)(2,1)S(1)} %collective-permute-done.2.near, bf16[4,2,32,640]{3,2,1,0:T(8,128)(2,1)S(1)} %collective-permute-done.3.far, ...), custom_call_target="tpu_custom_call" | custom-call | tf_op jit(solution)/shard_map/spectrum/pallas_call | solution.py:314
  36.1 15.4 %all-to-all-start = ((f32[256,1,128]{2,1,0:T(1,128)}), f32[256,1,128]{2,1,0:T(1,128)S(1)}, u32[]{:S(2)}, u32[]{:S(2)}) async-start(f32[256,1,128]{2,1,0:T(1,128)} %bitcast.2), calls=%async_computation | async-start | bytes 262144 | tf_op jit(solution)/shard_map/all_to_all | solution.py:327
  51.5 2.7 %collective-permute-start.8 = (f32[264,128]{1,0:T(8,128)S(1)}, f32[264,128]{1,0:T(8,128)S(1)}, u32[]{:S(2)}, u32[]{:S(2)}) collective-permute-start(f32[264,128]{1,0:T(8,128)S(1)} %get-tuple-element.41.held0), channel_id=1, source_target_pairs={{0,192},{64,128},{128,64},{192,0},{1,193},{65,129},{129,65},{193,1... | collective-permute-start | bytes 405512 | tf_op jit(solution)/shard_map/ppermute | solution.py:256
  54.2 0.6 collective-permute-start.7
  54.8 0.1 collective-permute-start.6
  54.9 6.1 %collective-permute-done.8.held3 = f32[264,128]{1,0:T(8,128)S(1)} collective-permute-done((f32[264,128]{1,0:T(8,128)S(1)}, f32[264,128]{1,0:T(8,128)S(1)}, u32[]{:S(2)}, u32[]{:S(2)}) %collective-permute-start.8) | collective-permute-done | bytes 135200 | tf_op jit(solution)/shard_map/ppermute | solution.py:256
  60.9 0.2 collective-permute-done.7.held2
  61.1 0.0 collective-permute-done.6.held1
  61.2 3.1 %all-to-all-done = f32[256,1,128]{2,1,0:T(1,128)S(1)} async-done(((f32[256,1,128]{2,1,0:T(1,128)}), f32[256,1,128]{2,1,0:T(1,128)S(1)}, u32[]{:S(2)}, u32[]{:S(2)}) %all-to-all-start) | async-done | bytes 131104 | tf_op jit(solution)/shard_map/all_to_all | solution.py:327
  64.2 0.0 copy-done.4
  64.2 0.0 copy-done.5
  64.2 0.0 copy-done.6
  64.2 2.2 %goldstein.1 = bf16[512,128]{1,0:T(8,128)(2,1)} custom-call(f32[264,128]{1,0:T(8,128)S(1)} %get-tuple-element.41.held0, f32[264,128]{1,0:T(8,128)S(1)} %collective-permute-done.6.held1, f32[264,128]{1,0:T(8,128)S(1)} %collective-permute-done.7.held2, f32[264,128]{1,0:T(8,128)S(1)} %collective-permute-done.8.held3, f32[256,128]{1,0:T(8,128)S(1)} %bitcast.12, ...), custom_call_target="tpu_custom_call" | custom-call | tf_op jit(solution)/shard_map/goldstein/pallas_call | solution.py:329
  (2 shorter events, 0.0 us)
Async XLA Ops:
  0.0 15.2 %copy-start.9 = (s32[1,4,32]{2,1,0:T(4,128)S(1)}, s32[1,4,32]{2,1,0:T(4,128)}, u32[]{:S(2)}) copy-start(s32[1,4,32]{2,1,0:T(4,128)} %param.13) | copy-start | bytes 1540
  0.0 15.8 %copy-start.10 = (s32[1,4,32,1]{2,3,1,0:T(1,128)S(1)}, s32[1,4,32,1]{2,3,1,0:T(1,128)}, u32[]{:S(2)}) copy-start(s32[1,4,32,1]{2,3,1,0:T(1,128)} %param.12) | copy-start | bytes 1540
  0.0 18.9 %copy-start = (bf16[640,128]{1,0:T(8,128)(2,1)S(1)}, bf16[640,128]{1,0:T(8,128)(2,1)}, u32[]{:S(2)}) copy-start(bf16[640,128]{1,0:T(8,128)(2,1)} %constant.30.clone.looks_ref) | copy-start | bytes 491524
  0.0 18.9 %copy-start.8 = (s32[2,16]{1,0:T(2,128)S(1)}, s32[2,16]{1,0:T(2,128)}, u32[]{:S(2)}) copy-start(s32[2,16]{1,0:T(2,128)} %match_ref.5) | copy-start | bytes 388
  1.2 8.3 %collective-permute-start = (bf16[4,2,32,640]{3,2,1,0:T(8,128)(2,1)S(1)}, bf16[4,2,32,640]{3,2,1,0:T(8,128)(2,1)S(1)}, u32[]{:S(2)}, u32[]{:S(2)}) collective-permute-start(bf16[4,2,32,640]{3,2,1,0:T(8,128)(2,1)S(1)} %get-tuple-element.28), channel_id=1, source_target_pairs={{0,64},{64,0},{128,192},{192,128},{1,65},{65,1},{129,193},{193,129... | collective-permute-start | bytes 983048 | tf_op jit(solution)/shard_map/ppermute | solution.py:256
  3.4 9.1 %collective-permute-start.1 = (bf16[4,2,32,640]{3,2,1,0:T(8,128)(2,1)S(1)}, bf16[4,2,32,640]{3,2,1,0:T(8,128)(2,1)S(1)}, u32[]{:S(2)}, u32[]{:S(2)}) collective-permute-start(bf16[4,2,32,640]{3,2,1,0:T(8,128)(2,1)S(1)} %get-tuple-element.29.own), channel_id=1, source_target_pairs={{0,192},{64,128},{128,64},{192,0},{1,193},{65,129},{129,65},{193,1... | collective-permute-start | bytes 983048 | tf_op jit(solution)/shard_map/ppermute | solution.py:256
  7.4 26.1 %copy-start.1 = (bf16[384,256]{1,0:T(8,128)(2,1)S(1)}, bf16[384,256]{1,0:T(8,128)(2,1)}, u32[]{:S(2)}) copy-start(bf16[384,256]{1,0:T(8,128)(2,1)} %constant.32.clone.cols_ref) | copy-start | bytes 589828
  7.4 26.1 %copy-start.7 = (bf16[64,96]{1,0:T(8,128)(2,1)S(1)}, bf16[64,96]{1,0:T(8,128)(2,1)}, u32[]{:S(2)}) copy-start(bf16[64,96]{1,0:T(8,128)(2,1)} %constant.31.clone.fwd_ref) | copy-start | bytes 36868
  7.4 17.0 %collective-permute-start.4 = (bf16[4,2,64,640]{3,2,1,0:T(8,128)(2,1)}, bf16[4,2,64,640]{3,2,1,0:T(8,128)(2,1)S(1)}, u32[]{:S(2)}, u32[]{:S(2)}) collective-permute-start(bf16[4,2,64,640]{3,2,1,0:T(8,128)(2,1)} %get-tuple-element.36), channel_id=1, source_target_pairs={{0,64},{64,0},{128,192},{192,128},{1,65},{65,1},{129,193},{193,129... | collective-permute-start | bytes 1966088 | tf_op jit(solution)/shard_map/ppermute | solution.py:256
  7.8 18.8 %collective-permute-start.5 = (bf16[4,2,64,640]{3,2,1,0:T(8,128)(2,1)S(1)}, bf16[4,2,64,640]{3,2,1,0:T(8,128)(2,1)S(1)}, u32[]{:S(2)}, u32[]{:S(2)}) collective-permute-start(bf16[4,2,64,640]{3,2,1,0:T(8,128)(2,1)S(1)} %get-tuple-element.35.own), channel_id=1, source_target_pairs={{0,192},{64,128},{128,64},{192,0},{1,193},{65,129},{129,65},{193,1... | collective-permute-start | bytes 1966088 | tf_op jit(solution)/shard_map/ppermute | solution.py:256
  12.5 0.7 %copy-start.2 = (bf16[4,2,32,640]{3,2,1,0:T(8,128)(2,1)}, bf16[4,2,32,640]{3,2,1,0:T(8,128)(2,1)S(1)}, u32[]{:S(2)}) copy-start(bf16[4,2,32,640]{3,2,1,0:T(8,128)(2,1)S(1)} %collective-permute-done.1.far) | copy-start | bytes 983044
  13.2 51.0 %copy-start.4 = (bf16[128,512]{1,0:T(8,128)(2,1)S(1)}, bf16[128,512]{1,0:T(8,128)(2,1)}, u32[]{:S(2)}) copy-start(bf16[128,512]{1,0:T(8,128)(2,1)} %constant.35.clone.pick_ref) | copy-start | bytes 393220
  13.3 51.0 %copy-start.5 = (bf16[128,128]{1,0:T(8,128)(2,1)S(1)}, bf16[128,128]{1,0:T(8,128)(2,1)}, u32[]{:S(2)}) copy-start(bf16[128,128]{1,0:T(8,128)(2,1)} %constant.34.clone.group_ref) | copy-start | bytes 98308
  15.2 49.1 %copy-start.6 = (bf16[64,96]{1,0:T(8,128)(2,1)S(1)}, bf16[64,96]{1,0:T(8,128)(2,1)}, u32[]{:S(2)}) copy-start(bf16[64,96]{1,0:T(8,128)(2,1)} %constant.33.clone.back_ref) | copy-start | bytes 36868
  16.6 14.9 %collective-permute-start.2 = (bf16[4,2,32,640]{3,2,1,0:T(8,128)(2,1)}, bf16[4,2,32,640]{3,2,1,0:T(8,128)(2,1)S(1)}, u32[]{:S(2)}, u32[]{:S(2)}) collective-permute-start(bf16[4,2,32,640]{3,2,1,0:T(8,128)(2,1)} %get-tuple-element.34), channel_id=1, source_target_pairs={{0,64},{64,0},{128,192},{192,128},{1,65},{65,1},{129,193},{193,129... | collective-permute-start | bytes 983048 | tf_op jit(solution)/shard_map/ppermute | solution.py:256
  16.6 16.9 %collective-permute-start.3 = (bf16[4,2,32,640]{3,2,1,0:T(8,128)(2,1)S(1)}, bf16[4,2,32,640]{3,2,1,0:T(8,128)(2,1)S(1)}, u32[]{:S(2)}, u32[]{:S(2)}) collective-permute-start(bf16[4,2,32,640]{3,2,1,0:T(8,128)(2,1)S(1)} %get-tuple-element.33.own), channel_id=1, source_target_pairs={{0,192},{64,128},{128,64},{192,0},{1,193},{65,129},{129,65},{193,1... | collective-permute-start | bytes 983048 | tf_op jit(solution)/shard_map/ppermute | solution.py:256
  18.9 1.0 %copy-start.3 = (bf16[4,2,32,640]{3,2,1,0:T(8,128)(2,1)S(1)}, bf16[4,2,32,640]{3,2,1,0:T(8,128)(2,1)}, u32[]{:S(2)}) copy-start(bf16[4,2,32,640]{3,2,1,0:T(8,128)(2,1)} %copy-done.2) | copy-start | bytes 983044
  36.1 28.1 %all-to-all-start = ((f32[256,1,128]{2,1,0:T(1,128)}), f32[256,1,128]{2,1,0:T(1,128)S(1)}, u32[]{:S(2)}, u32[]{:S(2)}) async-start(f32[256,1,128]{2,1,0:T(1,128)} %bitcast.2), calls=%async_computation | async-start | bytes 262144 | tf_op jit(solution)/shard_map/all_to_all | solution.py:327
  51.5 9.4 %collective-permute-start.8 = (f32[264,128]{1,0:T(8,128)S(1)}, f32[264,128]{1,0:T(8,128)S(1)}, u32[]{:S(2)}, u32[]{:S(2)}) collective-permute-start(f32[264,128]{1,0:T(8,128)S(1)} %get-tuple-element.41.held0), channel_id=1, source_target_pairs={{0,192},{64,128},{128,64},{192,0},{1,193},{65,129},{129,65},{193,1... | collective-permute-start | bytes 405512 | tf_op jit(solution)/shard_map/ppermute | solution.py:256
  54.2 6.9 %collective-permute-start.7 = (f32[264,128]{1,0:T(8,128)S(1)}, f32[264,128]{1,0:T(8,128)S(1)}, u32[]{:S(2)}, u32[]{:S(2)}) collective-permute-start(f32[264,128]{1,0:T(8,128)S(1)} %get-tuple-element.41.held0), channel_id=1, source_target_pairs={{0,128},{64,192},{128,0},{192,64},{1,129},{65,193},{129,1},{193,65... | collective-permute-start | bytes 405512 | tf_op jit(solution)/shard_map/ppermute | solution.py:256
  54.8 6.4 %collective-permute-start.6 = (f32[264,128]{1,0:T(8,128)S(1)}, f32[264,128]{1,0:T(8,128)S(1)}, u32[]{:S(2)}, u32[]{:S(2)}) collective-permute-start(f32[264,128]{1,0:T(8,128)S(1)} %get-tuple-element.41.held0), channel_id=1, source_target_pairs={{0,64},{64,0},{128,192},{192,128},{1,65},{65,1},{129,193},{193,129... | collective-permute-start | bytes 405512 | tf_op jit(solution)/shard_map/ppermute | solution.py:256
